TPU v7x, 32 devices: a whole 2x2x4 slice. The times are simulated.
32 devices in a mesh: ent: 8 (over z, y), rep: 4 (over x, core).
Axes of the slice: x: 2, y: 2, z: 4, core: 2. Of those that a mesh axis runs over, the one named last changes fastest.
Arguments:
- entity_emb: bfloat16 [73728, 256], P(('ent', 'rep')), may hold values from -5 to 5
- relation_emb: bfloat16 [474, 256], replicated, may hold values from -60 to 60
- in_weight: bfloat16 [256, 256], replicated, may hold values from -0.375 to 0.375
- out_weight: bfloat16 [256, 256], replicated, may hold values from -0.375 to 0.375
- loop_weight: bfloat16 [256, 256], replicated, may hold values from -0.375 to 0.375
- rel_weight: bfloat16 [256, 256], replicated, may hold values from -0.375 to 0.375
- loop_rel: float32 [256], replicated, may hold values from -4 to 4
- edge_src: int32 [576, 768], P(('ent', 'rep')), may hold values from 0 to 3327, as said below
- edge_dst: int32 [576, 768], P(('ent', 'rep')), may hold values from 0 to 127
- edge_rel: int32 [576, 768], P(('ent', 'rep')), may hold values from 0 to 473
- export_rows: int32 [8, 128], P('ent'), may hold values from 0 to 9215, as said below
- query_head: int32 [256], replicated, may hold values from 0 to 73727
- query_rel: int32 [256], replicated, may hold values from 0 to 473
Outputs:
- log_probs: float32 [256, 73728], P(None, ('ent', 'rep'))
- expected_tail: float32 [256, 256], P('rep')
Inputs may be any that keep to these rules, and one draw needn't show every extreme that they name: Each row of export_rows begins with a list of entries; the slots past the list's length hold filler values that no edge names. Some list fills the whole row. `edge_src`: A value j + 2304 with j >= 0 always names a list entry of export_rows, never filler.
All inputs are finite; a program needn't handle non-finite values.
Results may differ from a plain program's by a relative error of at most 0.0094.
Values may be sent and summed in bfloat16 or wider, within the bound.
No kernel may reach another device: no remote copies, remote signals or barrier semaphores. Data moves between devices by JAX's collectives and lax.ppermute only.
A program may use at most 64 MiB of HBM per device.

v0:
```python
import jax
import jax.numpy as jnp
from jax import lax
from jax.sharding import PartitionSpec as P

BLK = 128


def body(
    entity_emb,
    relation_emb,
    in_weight,
    out_weight,
    loop_weight,
    rel_weight,
    loop_rel,
    edge_src,
    edge_dst,
    edge_rel,
    export_rows,
    query_head,
    query_rel,
):
    groups = lax.axis_size("ent")
    copies = lax.axis_size("rep")
    member = lax.axis_index("rep")
    device = lax.axis_index("ent") * copies + member
    rows_dev = entity_emb.shape[0]
    columns = entity_emb.shape[1]
    listed = export_rows[0]
    slot_count = listed.shape[0]
    is_owned = listed // rows_dev == member
    picked = jnp.take(entity_emb, listed % rows_dev, axis=0).astype(jnp.float32)
    offered = jnp.where(is_owned[:, None], picked, 0.0)
    whole_rows = lax.psum(offered.astype(jnp.bfloat16), "rep")
    border_table = lax.all_gather(whole_rows[None], "ent", axis=0, tiled=True).reshape(
        groups * slot_count, columns
    )
    half_rel = relation_emb.shape[0] // 2
    block_rows = edge_dst.shape[1] * 0 + BLK
    positions = lax.broadcasted_iota(jnp.int32, (block_rows, 1), 0)

    def one_block(block_items):
        sources, targets, relation_ids = block_items
        is_near = sources < rows_dev
        near_rows = jnp.take(entity_emb, jnp.clip(sources, 0, rows_dev - 1), axis=0)
        far_index = jnp.clip(sources - rows_dev, 0, groups * slot_count - 1)
        far_rows = jnp.take(border_table, far_index, axis=0)
        source_rows = jnp.where(is_near[:, None], near_rows, far_rows)
        relation_rows = jnp.take(relation_emb, relation_ids, axis=0)
        composed = (source_rows.astype(jnp.float32) * relation_rows.astype(jnp.float32)).astype(
            jnp.bfloat16
        )
        is_hit = targets[None, :] == positions
        inward = relation_ids[None, :] < half_rel
        selector = jnp.concatenate([is_hit & inward, is_hit & jnp.logical_not(inward)], axis=0)
        block_sums = jnp.dot(
            selector.astype(jnp.bfloat16), composed, preferred_element_type=jnp.float32
        )
        counts = jnp.sum(selector.astype(jnp.float32), axis=1, keepdims=True)
        return (block_sums / jnp.maximum(counts, 1.0)).astype(jnp.bfloat16)

    blocks = lax.map(one_block, (edge_src, edge_dst, edge_rel))
    agg_in = blocks[:, :block_rows].reshape(rows_dev, columns)
    agg_out = blocks[:, block_rows:].reshape(rows_dev, columns)
    own_loop = (entity_emb.astype(jnp.float32) * loop_rel).astype(jnp.bfloat16)
    preact = jnp.dot(agg_in, in_weight, preferred_element_type=jnp.float32)
    preact = preact + jnp.dot(agg_out, out_weight, preferred_element_type=jnp.float32)
    preact = preact + jnp.dot(own_loop, loop_weight, preferred_element_type=jnp.float32)
    hidden = jnp.tanh(preact).astype(jnp.bfloat16)
    rel_full = jnp.dot(relation_emb, rel_weight, preferred_element_type=jnp.float32)
    first_row = device * rows_dev
    selected = query_head[:, None] - first_row == lax.broadcasted_iota(jnp.int32, (1, rows_dev), 1)
    head_rows = lax.psum(
        jnp.dot(selected.astype(jnp.bfloat16), hidden, preferred_element_type=jnp.float32),
        ("ent", "rep"),
    )
    query_vec = (head_rows * jnp.take(rel_full, query_rel, axis=0)).astype(jnp.bfloat16)
    scores = lax.dot_general(
        query_vec, hidden, (((1,), (1,)), ((), ())), preferred_element_type=jnp.float32
    )
    hidden_wide = hidden.astype(jnp.float32)
    batch_rows = query_vec.shape[0] // copies
    row_top = lax.pmax(jnp.max(scores, axis=1), ("ent", "rep"))
    weights = jnp.exp(scores - row_top[:, None])
    row_total, weighted = lax.psum(
        (jnp.sum(weights, axis=1), jnp.dot(weights, hidden_wide, precision=lax.Precision.HIGHEST)),
        ("ent", "rep"),
    )
    expected_all = weighted / row_total[:, None]
    expected_tail = lax.dynamic_slice_in_dim(expected_all, member * batch_rows, batch_rows, 0)
    log_probs = scores - row_top[:, None] - jnp.log(row_total)[:, None]
    return (log_probs, expected_tail)


def solution(mesh):
    placed = (
        P(("ent", "rep"), None),
        P(),
        P(),
        P(),
        P(),
        P(),
        P(),
        P(("ent", "rep"), None),
        P(("ent", "rep"), None),
        P(("ent", "rep"), None),
        P("ent", None),
        P(),
        P(),
    )
    return jax.shard_map(
        body,
        mesh=mesh,
        in_specs=placed,
        out_specs=(P(None, ("ent", "rep")), P("rep", None)),
        check_vma=False,
    )
```

profile of v0, /device:TPU:0, one launch (start us, length us, event | category | flops | bytes accessed | tf_op | source)
XLA Modules:
  0.0 620.0 jit_solution(11385256396522062451)
XLA Ops:
  16.0 29.5 %all-reduce.4.cloned.1.call-done = bf16[1,128,256]{2,1,0:T(8,128)(2,1)} async-done(((bf16[1,128,256]{2,1,0:T(8,128)(2,1)}), bf16[1,128,256]{2,1,0:T(8,128)(2,1)}) %all-reduce.4.cloned.1.call-update) | async-done | bytes 65552 | tf_op jit(solution)/shard_map/psum | solution.py:35
  45.5 31.6 %all_gather.3 = bf16[8,128,256]{2,1,0:T(8,128)(2,1)S(1)} all-gather(bf16[1,128,256]{2,1,0:T(8,128)(2,1)} %all-reduce.4.cloned.1.call-done), channel_id=1, replica_groups=mesh['ent'=8,'rep'=4] {'ent'}, dimensions={0}, use_global_device_ids=true | all-gather | bytes 589824 | tf_op jit(solution)/shard_map/all_gather | solution.py:36
  77.1 231.6 %while.13 = (s32[]{:T(128)}, bf16[18,256,256]{2,1,0:T(8,128)(2,1)}, s32[18,768]{1,0:T(8,128)}, s32[18,768]{1,0:T(8,128)}, s32[18,768]{1,0:T(8,128)}, /*index=5*/...) while((s32[]{:T(128)}, bf16[18,256,256]{2,1,0:T(8,128)(2,1)}, ...), condition=%wide.region_3.4_spmd.clone, body=%wide.region_1.3_spmd.clone.sunk | while | flops 103479296 | bytes 4359789 | solution.py:63
  79.8 2.7 gather_fusion
  82.5 2.7 gather_fusion.1
  85.2 2.7 gather_fusion.2
  92.7 2.7 gather_fusion
  95.4 2.7 gather_fusion.1
  98.1 2.7 gather_fusion.2
  105.6 2.7 gather_fusion
  108.3 2.7 gather_fusion.1
  110.9 2.7 gather_fusion.2
  118.4 2.7 gather_fusion
  121.1 2.7 gather_fusion.1
  123.8 2.7 gather_fusion.2
  131.3 2.7 gather_fusion
  134.0 2.7 gather_fusion.1
  136.7 2.7 gather_fusion.2
  144.2 2.7 gather_fusion
  146.8 2.7 gather_fusion.1
  149.5 2.7 gather_fusion.2
  157.0 2.7 gather_fusion
  159.7 2.7 gather_fusion.1
  162.4 2.7 gather_fusion.2
  169.9 2.7 gather_fusion
  172.6 2.7 gather_fusion.1
  175.3 2.7 gather_fusion.2
  182.8 2.7 gather_fusion
  185.4 2.7 gather_fusion.1
  188.1 2.7 gather_fusion.2
  195.6 2.7 gather_fusion
  198.3 2.7 gather_fusion.1
  201.0 2.7 gather_fusion.2
  208.5 2.7 gather_fusion
  211.2 2.7 gather_fusion.1
  213.8 2.7 gather_fusion.2
  221.4 2.7 gather_fusion
  224.0 2.7 gather_fusion.1
  226.7 2.7 gather_fusion.2
  239.6 2.7 gather_fusion.2
  272.8 2.7 gather_fusion
  288.4 2.7 gather_fusion.1
  291.0 2.7 gather_fusion.2
  316.5 125.2 %all-reduce.6.cloned.1.call-done = f32[256,256]{1,0:T(8,128)} async-done(((f32[256,256]{1,0:T(8,128)}), f32[256,256]{1,0:T(8,128)}) %all-reduce.6.cloned.1.call-update) | async-done | bytes 262160 | tf_op jit(solution)/shard_map/psum | solution.py:74
  443.7 39.2 %pmax.7 = f32[256]{0:T(256)S(1)} all-reduce(f32[256]{0:T(256)S(1)} %get-tuple-element.165), channel_id=1, replica_groups=mesh['ent'=8,'rep'=4] {'ent','rep'}, use_global_device_ids=true, to_apply=%region_6.7 | all-reduce | flops 256 | bytes 2048 | tf_op jit(solution)/shard_map/pmax | solution.py:84
  482.9 3.4 fusion.26
  486.8 40.1 %psum.30 = f32[256]{0:T(256)S(1)} all-reduce(f32[256]{0:T(256)S(1)} %exponential_reduce_fusion), channel_id=1, replica_groups=mesh['ent'=8,'rep'=4] {'ent','rep'}, use_global_device_ids=true, to_apply=%region_8.9 | all-reduce | flops 256 | bytes 2048 | tf_op jit(solution)/shard_map/psum | solution.py:86
  528.7 83.3 %all-reduce.8.cloned.1.call-done = f32[256,256]{1,0:T(8,128)} async-done(((f32[256,256]{1,0:T(8,128)}), f32[256,256]{1,0:T(8,128)}) %all-reduce.8.cloned.1.call-update) | async-done | bytes 262160 | tf_op jit(solution)/shard_map/psum | solution.py:86
  (311 shorter events, 146.1 us)
Async XLA Ops:
  7.2 303.3 %copy-start = (bf16[256,256]{1,0:T(8,128)(2,1)S(1)}, bf16[256,256]{1,0:T(8,128)(2,1)}, u32[]{:S(2)}) copy-start(bf16[256,256]{1,0:T(8,128)(2,1)} %param.17) | copy-start | bytes 393220
  7.2 69.9 %copy-start.2 = (bf16[2304,256]{1,0:T(8,128)(2,1)S(1)}, bf16[2304,256]{1,0:T(8,128)(2,1)}, u32[]{:S(2)}) copy-start(bf16[2304,256]{1,0:T(8,128)(2,1)} %param.15) | copy-start | bytes 3538948
  7.2 69.9 %copy-start.1 = (bf16[474,256]{1,0:T(8,128)(2,1)S(1)}, bf16[474,256]{1,0:T(8,128)(2,1)}, u32[]{:S(2)}) copy-start(bf16[474,256]{1,0:T(8,128)(2,1)} %param.16) | copy-start | bytes 728068
  7.2 38.3 %all-reduce.4.cloned.1.call-start = ((), (), s32[]{:S(2)}) async-start(), calls=%async_computation | async-start | bytes 131072 | tf_op jit(solution)/shard_map/psum | solution.py:35
  11.7 430.0 %all-reduce.6.cloned.1.call-start = ((), (), s32[]{:S(2)}) async-start(), calls=%async_computation.1 | async-start | bytes 524288 | tf_op jit(solution)/shard_map/psum | solution.py:74
  310.5 0.9 copy-start.4
  311.4 0.9 copy-start.5
  311.4 0.9 copy-start.7
  313.9 2.6 copy-start.6
  313.9 127.8 %copy-start.3 = (f32[256,256]{1,0:T(8,128)S(1)}, f32[256,256]{1,0:T(8,128)}, u32[]{:S(2)}) copy-start(f32[256,256]{1,0:T(8,128)} %gather_fusion.4) | copy-start | bytes 786436
  316.4 295.5 %all-reduce.8.cloned.1.call-start = ((), (), s32[]{:S(2)}) async-start(), calls=%async_computation.2 | async-start | bytes 524288 | tf_op jit(solution)/shard_map/psum | solution.py:86
Sparse Core Ops, SparseCore 0:
  11.8 33.7 all-reduce.3
  316.5 125.1 all-reduce.5
  486.9 124.9 all-reduce.7
where the time goes:
time: 625 us; the launch traced here: 620 us
  waiting for transfers between devices  238 us (38%)
  local copies, waits for them, and re-layouts  164 us (26%)
  blocking collectives  111 us (18%)
  other arithmetic  56.3 us (9%)
  matrix products  35.6 us (6%)
  between operations  13.9 us (2%)
    psum x1, waiting for transfers between devices, body(): lax.psum(jnp.dot(selected.astype(jnp.bfloat16), hidden, preferred_element...  125 us
    psum x1, waiting for transfers between devices, body(): lax.psum((jnp.sum(weights, axis=1), jnp.dot(weights, hidden_wide, precisi...  83.3 us
    gather x18, local copies, waits for them, and re-layouts, one_block(): near_rows = jnp.take(entity_emb, jnp.clip(sources, 0, rows_dev - 1), axis=0)  47.8 us
    gather x18, local copies, waits for them, and re-layouts, one_block(): relation_rows = jnp.take(relation_emb, relation_ids, axis=0)  47.8 us
    gather x18, local copies, waits for them, and re-layouts, one_block(): far_rows = jnp.take(border_table, far_index, axis=0)  47.8 us
    psum x1, blocking collectives, body(): lax.psum((jnp.sum(weights, axis=1), jnp.dot(weights, hidden_wide, precisi...  40.1 us
    pmax x1, blocking collectives, body(): row_top = lax.pmax(jnp.max(scores, axis=1), ('ent', 'rep'))  39.2 us
    all_gather x1, blocking collectives, body(): lax.all_gather(whole_rows[None], 'ent', axis=0, tiled=True)  31.6 us
  transfers between devices with their start and end apart: 3, of which 3 were waited for; matrix products, arithmetic and copies ran while one was open for 1% of the time, Pallas kernels for 0%

commit v1 on v0

v1 whole, which is shorter than its diff:
```python
import functools

import jax
import jax.numpy as jnp
from jax import lax
from jax.experimental import pallas as pl
from jax.experimental.pallas import tpu as pltpu
from jax.sharding import PartitionSpec as P

BLK = 128
CHUNK = 1024
BF16 = jnp.bfloat16
F32 = jnp.float32
BOTH = ("ent", "rep")
NT = (((1,), (1,)), ((), ()))
VMEM_LIMIT = 56 * 2**20


def one_hot(index, rows):
    where = lax.broadcasted_iota(jnp.int16, (rows, index.shape[1]), 0) == index.astype(jnp.int16)
    return jnp.where(where, jnp.asarray(1, BF16), jnp.asarray(0, BF16))


def layer_kernel(
    half_rel,
    src_ref,
    dst_ref,
    rel_ref,
    emb_ref,
    near_ref,
    far_ref,
    relation_ref,
    in_ref,
    out_ref,
    loop_ref,
    loop_rel_ref,
    head_ref,
    hidden_ref,
    heads_ref,
    gathered_ref,
):
    rows_dev = emb_ref.shape[0]
    far_chunks = far_ref.shape[0]

    def one_block(i, carry):
        src = src_ref[pl.ds(i, 1), :]
        rel = rel_ref[pl.ds(i, 1), :]
        gathered = jnp.dot(
            near_ref[...], one_hot(src, rows_dev), preferred_element_type=F32
        )
        if far_chunks == 1:
            gathered += jnp.dot(
                far_ref[0], one_hot(src - rows_dev, CHUNK), preferred_element_type=F32
            )
        else:
            gathered_ref[...] = gathered

            def one_chunk(j, carry):
                gathered_ref[...] += jnp.dot(
                    far_ref[j],
                    one_hot(src - rows_dev - j * CHUNK, CHUNK),
                    preferred_element_type=F32,
                )
                return carry

            lax.fori_loop(0, far_chunks, one_chunk, 0)
            gathered = gathered_ref[...]
        relation = jnp.dot(
            relation_ref[...], one_hot(rel, relation_ref.shape[1]), preferred_element_type=F32
        )
        composed = (gathered * relation).astype(BF16)
        key = dst_ref[pl.ds(i, 1), :] + jnp.where(rel >= half_rel, BLK, 0)
        selector = (
            lax.broadcasted_iota(jnp.int32, (2 * BLK, key.shape[1]), 0) == key
        ).astype(F32)
        counts = jnp.sum(selector, axis=1, keepdims=True)
        sums = lax.dot_general(selector.astype(BF16), composed, NT, preferred_element_type=F32)
        agg = (sums / jnp.maximum(counts, 1.0)).astype(BF16)
        here = pl.ds(pl.multiple_of(i * BLK, BLK), BLK)
        own = (emb_ref[here, :].astype(F32) * loop_rel_ref[...]).astype(BF16)
        preact = jnp.dot(agg[:BLK], in_ref[...], preferred_element_type=F32)
        preact += jnp.dot(agg[BLK:], out_ref[...], preferred_element_type=F32)
        preact += jnp.dot(own, loop_ref[...], preferred_element_type=F32)
        hidden_ref[here, :] = jnp.tanh(preact).astype(BF16)
        return carry

    lax.fori_loop(0, src_ref.shape[0], one_block, 0)
    picks = lax.broadcasted_iota(jnp.int32, (head_ref.shape[0], rows_dev), 1) == head_ref[...]
    heads_ref[...] = jnp.dot(
        picks.astype(F32).astype(BF16), hidden_ref[...], preferred_element_type=F32
    ).astype(BF16)


def score_kernel(heads_ref, rel_ref, hidden_ref, scores_ref, weighted_ref, stats_ref):
    query = (heads_ref[...].astype(F32) * rel_ref[...]).astype(BF16)
    scores = lax.dot_general(query, hidden_ref[...], NT, preferred_element_type=F32)
    scores_ref[...] = scores
    top = jnp.max(scores, axis=1, keepdims=True)
    high = top.astype(BF16)
    low = (top - high.astype(F32)).astype(BF16)
    top = high.astype(F32) + low.astype(F32)
    weights = jnp.exp(scores - top)
    total = jnp.sum(weights, axis=1, keepdims=True)
    weighted_ref[...] = jnp.dot(
        weights.astype(BF16), hidden_ref[...], preferred_element_type=F32
    ).astype(BF16)
    total_high = total.astype(BF16)
    total_low = (total - total_high.astype(F32)).astype(BF16)
    lanes = lax.broadcasted_iota(jnp.int32, (query.shape[0], 128), 1)
    wide = jnp.where(lanes == 0, high.astype(F32), 0.0)
    wide = jnp.where(lanes == 1, low.astype(F32), wide)
    wide = jnp.where(lanes == 2, total_high.astype(F32), wide)
    wide = jnp.where(lanes == 3, total_low.astype(F32), wide)
    stats_ref[...] = jnp.transpose(wide)[: stats_ref.shape[0]].astype(BF16)


def body(
    entity_emb,
    relation_emb,
    in_weight,
    out_weight,
    loop_weight,
    rel_weight,
    loop_rel,
    edge_src,
    edge_dst,
    edge_rel,
    export_rows,
    query_head,
    query_rel,
):
    groups = lax.axis_size("ent")
    copies = lax.axis_size("rep")
    devices = groups * copies
    group = lax.axis_index("ent")
    member = lax.axis_index("rep")
    device = group * copies + member
    rows_dev, columns = entity_emb.shape
    queries = query_head.shape[0]
    batch_rows = queries // copies
    share = -(-batch_rows // groups)
    padded = share * devices

    listed = export_rows[0]
    slots = listed.shape[0]
    is_owned = listed // rows_dev == member
    picked = jnp.take(entity_emb, listed % rows_dev, axis=0)
    offered = jnp.where(is_owned[:, None], picked, jnp.zeros_like(picked))
    pieces = lax.all_to_all(offered, "rep", 0, 0, tiled=True)
    mine = jnp.sum(
        pieces.reshape(copies, slots // copies, columns).astype(F32), axis=0
    ).astype(BF16)
    spread = jnp.broadcast_to(mine[None], (devices,) + mine.shape)
    table = lax.all_to_all(spread, BOTH, 0, 0).reshape(groups * slots, columns)
    far_count = -(-(groups * slots) // CHUNK) * CHUNK
    far = jnp.pad(table, ((0, far_count - groups * slots), (0, 0)))
    far = far.reshape(far_count // CHUNK, CHUNK, columns).transpose(0, 2, 1)

    relations = relation_emb.shape[0]
    rel_count = -(-relations // 256) * 256
    relation_t = jnp.pad(relation_emb, ((0, rel_count - relations), (0, 0))).T
    local_head = jnp.pad(
        query_head - device * rows_dev, (0, padded - queries), constant_values=-1
    )[:, None]

    hidden, heads = pl.pallas_call(
        functools.partial(layer_kernel, relations // 2),
        out_shape=(
            jax.ShapeDtypeStruct((rows_dev, columns), BF16),
            jax.ShapeDtypeStruct((padded, columns), BF16),
        ),
        scratch_shapes=[pltpu.VMEM((columns, edge_src.shape[1]), F32)],
        compiler_params=pltpu.CompilerParams(vmem_limit_bytes=VMEM_LIMIT),
    )(
        edge_src,
        edge_dst,
        edge_rel,
        entity_emb,
        entity_emb.T,
        far,
        relation_t,
        in_weight,
        out_weight,
        loop_weight,
        loop_rel[None],
        local_head,
    )

    parts = lax.all_to_all(heads, BOTH, 0, 0, tiled=True).reshape(devices, share, columns)
    own_heads = jnp.sum(parts.astype(F32), axis=0).astype(BF16)
    head_rows = lax.all_to_all(
        jnp.broadcast_to(own_heads[None], (devices, share, columns)), BOTH, 0, 0
    ).reshape(padded, columns)[:queries]
    query_factor = jnp.dot(
        jnp.take(relation_emb, query_rel, axis=0), rel_weight, preferred_element_type=F32
    )

    scores, weighted, stats = pl.pallas_call(
        score_kernel,
        out_shape=(
            jax.ShapeDtypeStruct((queries, rows_dev), F32),
            jax.ShapeDtypeStruct((queries, columns), BF16),
            jax.ShapeDtypeStruct((16, queries), BF16),
        ),
        compiler_params=pltpu.CompilerParams(vmem_limit_bytes=VMEM_LIMIT),
    )(head_rows, query_factor, hidden)

    split = weighted.reshape(copies, batch_rows, columns)
    split = jnp.pad(split, ((0, 0), (0, share * groups - batch_rows), (0, 0)))
    split = split.reshape(copies, groups, share, columns).transpose(1, 0, 2, 3)
    split = split.reshape(devices, share * columns)
    figures = jnp.broadcast_to(stats[:4].reshape(1, 4 * queries), (devices, 4 * queries))
    payload = jnp.concatenate([split, figures], axis=1).reshape(devices, -1, 128)
    received = lax.all_to_all(payload, BOTH, 0, 0).reshape(devices, -1)
    sums = received[:, : share * columns].reshape(devices, share, columns).astype(F32)
    figures = received[:, share * columns :].reshape(devices, 4, queries).astype(F32)
    tops = figures[:, 0] + figures[:, 1]
    totals = figures[:, 2] + figures[:, 3]
    row_top = jnp.max(tops, axis=0)
    scale = jnp.exp(tops - row_top)
    row_total = jnp.sum(totals * scale, axis=0)
    factor = jnp.pad(
        (scale / row_total).reshape(devices, copies, batch_rows),
        ((0, 0), (0, 0), (0, share * groups - batch_rows)),
    ).reshape(devices, -1)
    own_factor = lax.dynamic_slice_in_dim(
        factor, (member * groups + group) * share, share, 1
    )
    own_expected = jnp.sum(sums * own_factor[:, :, None], axis=0)
    expected_tail = lax.all_to_all(
        jnp.broadcast_to(own_expected[None], (groups, share, columns)), "ent", 0, 0
    ).reshape(groups * share, columns)[:batch_rows]
    log_probs = scores - (row_top + jnp.log(row_total))[:, None]
    return (log_probs, expected_tail)


def solution(mesh):
    placed = (
        P(("ent", "rep"), None),
        P(),
        P(),
        P(),
        P(),
        P(),
        P(),
        P(("ent", "rep"), None),
        P(("ent", "rep"), None),
        P(("ent", "rep"), None),
        P("ent", None),
        P(),
        P(),
    )
    return jax.shard_map(
        body,
        mesh=mesh,
        in_specs=placed,
        out_specs=(P(None, ("ent", "rep")), P("rep", None)),
        check_vma=False,
    )
```

time: 625 us -> 135 us (0.22)
  waiting for transfers between devices: 238 us -> 40.9 us
  local copies, waits for them, and re-layouts: 164 us -> 14.1 us
  blocking collectives: 111 us -> 8.13 us
  other arithmetic: 56.3 us -> 4.28 us
  Pallas kernels: 0 us -> 48.2 us
  matrix products: 35.6 us -> 0.94 us
  starting transfers between devices: 0.12 us -> 16.5 us
  between operations: 13.9 us -> 0.89 us
    psum x3 -> x0, waiting for transfers between devices: 238 us -> none  [the longest x1 125 us: body(): lax.psum(jnp.dot(selected.astype(jnp.bfloat16), hidden, preferred_element...]
    gather x56 -> x2, local copies, waits for them, and re-layouts: 147 us -> 3.34 us  [the longest x1 2.18 us: body(): picked = jnp.take(entity_emb, listed % rows_dev, axis=0)]
    pallas_call x0 -> x2, Pallas kernels: none -> 48.2 us  [the longest x1 44.3 us: body(): pl.pallas_call(functools.partial(layer_kernel, relations // 2), out_shape...]
    all_to_all x0 -> x5, waiting for transfers between devices: none -> 40.9 us  [the longest x1 12.3 us: body(): table = lax.all_to_all(spread, BOTH, 0, 0).reshape(groups * slots, columns)]
    psum x1 -> x0, blocking collectives: 40.1 us -> none  [body(): lax.psum((jnp.sum(weights, axis=1), jnp.dot(weights, hidden_wide, precisi...]
    pmax x1 -> x0, blocking collectives: 39.2 us -> none  [body(): row_top = lax.pmax(jnp.max(scores, axis=1), ('ent', 'rep'))]
    dot_general x25 -> x1, matrix products: 35.6 us -> 0.94 us  [body(): jnp.dot(jnp.take(relation_emb, query_rel, axis=0), rel_weight, preferred_...]
    all_gather x1 -> x0, blocking collectives: 31.6 us -> none  [body(): lax.all_gather(whole_rows[None], 'ent', axis=0, tiled=True)]
  transfers between devices with their start and end apart: 3 -> 5, of which waited for: 3 -> 5; matrix products, arithmetic and copies ran while one was open for 1% -> 5% of each run, Pallas kernels for 0% -> 0%
where the time goes in v1:
time: 135 us; the launch traced here: 134 us
  Pallas kernels  48.2 us (36%)
  waiting for transfers between devices  40.9 us (30%)
  starting transfers between devices  16.5 us (12%)
  local copies, waits for them, and re-layouts  14.1 us (10%)
  blocking collectives  8.13 us (6%)
  other arithmetic  4.28 us (3%)
    pallas_call x1, Pallas kernels, body(): pl.pallas_call(functools.partial(layer_kernel, relations // 2), out_shape...  44.3 us
    all_to_all x1, waiting for transfers between devices, body(): table = lax.all_to_all(spread, BOTH, 0, 0).reshape(groups * slots, columns)  12.3 us
    all_to_all x1, waiting for transfers between devices, body(): received = lax.all_to_all(payload, BOTH, 0, 0).reshape(devices, -1)  8.88 us
    all_to_all x1, waiting for transfers between devices, body(): lax.all_to_all(heads, BOTH, 0, 0, tiled=True)  8.19 us
    all_to_all x1, blocking collectives, body(): pieces = lax.all_to_all(offered, 'rep', 0, 0, tiled=True)  8.13 us
    all_to_all x1, waiting for transfers between devices, body(): lax.all_to_all(jnp.broadcast_to(own_heads[None], (devices, share, columns...  6.12 us
    all_to_all x1, waiting for transfers between devices, body(): lax.all_to_all(jnp.broadcast_to(own_expected[None], (groups, share, colum...  5.35 us
    all_to_all x1, starting transfers between devices, body(): table = lax.all_to_all(spread, BOTH, 0, 0).reshape(groups * slots, columns)  4.92 us
  transfers between devices with their start and end apart: 5, of which 5 were waited for; matrix products, arithmetic and copies ran while one was open for 5% of the time, Pallas kernels for 0%

profile of v1, /device:TPU:0, one launch (start us, length us, event | category | flops | bytes accessed | tf_op | source)
XLA Modules:
  0.0 133.9 jit_solution(14025893571894077807)
XLA Ops:
  0.6 0.0 copy-start
  0.6 0.0 copy-start.1
  0.7 0.8 divide_reduce_fusion
  1.4 0.7 compare_reduce_fusion
  2.1 0.7 fusion.8
  2.8 0.1 div.22
  2.9 0.1 rem.37
  2.9 0.1 ne.58
  3.0 0.0 copy-start.5
  3.1 2.2 %gather_fusion = bf16[128,256]{1,0:T(8,128)(2,1)S(1)} fusion(bf16[2304,256]{1,0:T(8,128)(2,1)} %emb_ref.1, s32[1024]{0:T(1024)S(1)} %pad_clamp_fusion.1), kind=kCustom, calls=%fused_computation | custom fusion | bytes 131584 | tf_op jit(solution)/shard_map/jit(_take)/gather | solution.py:147
  5.2 0.0 copy-start.2
  5.3 0.1 select_select_fusion
  5.4 8.1 %all_to_all.35 = bf16[4,32,256]{2,1,0:T(8,128)(2,1)S(1)} all-to-all(bf16[4,32,256]{2,1,0:T(8,128)(2,1)S(1)} %select_select_fusion), channel_id=1, replica_groups=mesh['ent'=8,'rep'=4] {'rep'}, dimensions={0} | all-to-all | bytes 131072 | tf_op jit(solution)/shard_map/all_to_all | solution.py:149
  13.5 0.8 broadcast_in_dim.75
  14.4 4.9 %all-to-all-start.1 = ((bf16[32,32,256]{2,1,0:T(8,128)(2,1)}), bf16[32,32,256]{2,1,0:T(8,128)(2,1)S(1)}, u32[]{:S(2)}, u32[]{:S(2)}) async-start(bf16[32,32,256]{2,1,0:T(8,128)(2,1)} %broadcast_in_dim.75), calls=%async_computation.1 | async-start | bytes 1048576 | tf_op jit(solution)/shard_map/all_to_all | solution.py:154
  19.3 1.5 %copy.19 = bf16[2304,256]{0,1:T(8,128)(2,1)} copy(bf16[2304,256]{1,0:T(8,128)(2,1)S(1)} %copy-done.1) | data formatting | bytes 2359296 | tf_op args[0]
  20.9 0.8 copy.22.head_ref
  21.7 0.1 copy.21
  21.8 0.7 pad_bitcast_fusion.relation_ref
  22.5 12.3 %all-to-all-done.1 = bf16[32,32,256]{2,1,0:T(8,128)(2,1)S(1)} async-done(((bf16[32,32,256]{2,1,0:T(8,128)(2,1)}), bf16[32,32,256]{2,1,0:T(8,128)(2,1)S(1)}, u32[]{:S(2)}, u32[]{:S(2)}) %all-to-all-start.1) | async-done | bytes 524320 | tf_op jit(solution)/shard_map/all_to_all | solution.py:154
  34.9 1.0 copy.20
  35.9 44.3 %shard_map.140 = (bf16[2304,256]{1,0:T(8,128)(2,1)}, bf16[256,256]{1,0:T(8,128)(2,1)}) custom-call(s32[18,768]{1,0:T(8,128)} %src_ref.1, s32[18,768]{1,0:T(8,128)} %dst_ref.1, s32[18,768]{1,0:T(8,128)} %rel_ref.1, bf16[2304,256]{1,0:T(8,128)(2,1)} %emb_ref.1, bf16[256,2304]{1,0:T(8,128)(2,1)} %bitcast.42, bf16[1,256,1024]{2,1,0:T(8,128)(2,1)} %bitcast.43, ...), custom_call_target="tpu_custom_call" | custom-call | tf_op jit(solution)/shard_map/pallas_call | solution.py:166
  80.2 3.1 %all-to-all-start.2 = ((bf16[32,8,256]{2,1,0:T(8,128)(2,1)}), bf16[32,8,256]{2,1,0:T(8,128)(2,1)S(1)}, u32[]{:S(2)}, u32[]{:S(2)}) async-start(bf16[32,8,256]{2,1,0:T(8,128)(2,1)} %bitcast.55), calls=%async_computation.2 | async-start | bytes 262144 | tf_op jit(solution)/shard_map/all_to_all | solution.py:189
  83.3 8.2 %all-to-all-done.2 = bf16[32,8,256]{2,1,0:T(8,128)(2,1)S(1)} async-done(((bf16[32,8,256]{2,1,0:T(8,128)(2,1)}), bf16[32,8,256]{2,1,0:T(8,128)(2,1)S(1)}, u32[]{:S(2)}, u32[]{:S(2)}) %all-to-all-start.2) | async-done | bytes 131104 | tf_op jit(solution)/shard_map/all_to_all | solution.py:189
  91.6 0.7 broadcast_in_dim.78
  92.2 2.6 %all-to-all-start.3 = ((bf16[32,8,256]{2,1,0:T(8,128)(2,1)}), bf16[32,8,256]{2,1,0:T(8,128)(2,1)S(1)}, u32[]{:S(2)}, u32[]{:S(2)}) async-start(bf16[32,8,256]{2,1,0:T(8,128)(2,1)} %broadcast_in_dim.78), calls=%async_computation.3 | async-start | bytes 262144 | tf_op jit(solution)/shard_map/all_to_all | solution.py:191
  94.8 1.2 gather_fusion.1
  96.0 0.9 fusion.rel_ref
  96.9 6.1 %all-to-all-done.3 = bf16[32,8,256]{2,1,0:T(8,128)(2,1)S(1)} async-done(((bf16[32,8,256]{2,1,0:T(8,128)(2,1)}), bf16[32,8,256]{2,1,0:T(8,128)(2,1)S(1)}, u32[]{:S(2)}, u32[]{:S(2)}) %all-to-all-start.3) | async-done | bytes 131104 | tf_op jit(solution)/shard_map/all_to_all | solution.py:191
  103.1 0.7 copy-done.4
  103.7 3.8 %shard_map.141 = (f32[256,2304]{1,0:T(8,128)}, bf16[256,256]{1,0:T(8,128)(2,1)}, bf16[16,256]{1,0:T(8,128)(2,1)}) custom-call(bf16[256,256]{1,0:T(8,128)(2,1)} %bitcast.50, f32[256,256]{1,0:T(8,128)} %fusion.rel_ref, bf16[2304,256]{1,0:T(8,128)(2,1)} %get-tuple-element.8.hidden_ref), custom_call_target="tpu_custom_call" | custom-call | tf_op jit(solution)/shard_map/pallas_call | solution.py:198
  107.6 1.1 copy.23
  108.7 0.7 slice_bitcast_fusion
  109.4 0.7 copy.31
  110.1 2.6 %all-to-all-start.4 = ((bf16[32,24,128]{2,1,0:T(8,128)(2,1)}), bf16[32,24,128]{2,1,0:T(8,128)(2,1)S(1)}, u32[]{:S(2)}, u32[]{:S(2)}) async-start(bf16[32,24,128]{2,1,0:T(8,128)(2,1)} %bitcast.22), calls=%async_computation.4 | async-start | bytes 393216 | tf_op jit(solution)/shard_map/all_to_all | solution.py:214
  112.7 8.9 %all-to-all-done.4 = bf16[32,24,128]{2,1,0:T(8,128)(2,1)S(1)} async-done(((bf16[32,24,128]{2,1,0:T(8,128)(2,1)}), bf16[32,24,128]{2,1,0:T(8,128)(2,1)S(1)}, u32[]{:S(2)}, u32[]{:S(2)}) %all-to-all-start.4) | async-done | bytes 196640 | tf_op jit(solution)/shard_map/all_to_all | solution.py:214
  121.6 0.1 reshape.150
  121.7 0.1 slice_add_fusion
  121.9 0.1 dynamic-slice
  122.0 0.1 dynamic-slice_divide_fusion
  122.0 0.1 mul.31
  122.1 0.1 copy.33
  122.2 0.1 multiply_reduce_fusion
  122.3 0.6 broadcast_in_dim.85
  122.9 3.4 %all-to-all-start.5 = ((f32[8,8,256]{2,1,0:T(8,128)}), f32[8,8,256]{2,1,0:T(8,128)S(1)}, u32[]{:S(2)}, u32[]{:S(2)}) async-start(f32[8,8,256]{2,1,0:T(8,128)} %broadcast_in_dim.85), calls=%async_computation.5 | async-start | bytes 131072 | tf_op jit(solution)/shard_map/all_to_all | solution.py:230
  126.3 1.6 %broadcast_subtract_fusion = f32[256,2304]{1,0:T(8,128)} fusion(f32[256,2304]{1,0:T(8,128)S(1)} %copy-done.3, f32[256]{0:T(256)S(1)} %log_add_fusion), kind=kLoop, calls=%fused_computation.2 | loop fusion | flops 589824 | bytes 4719616 | tf_op jit(solution)/shard_map/sub | solution.py:233
  127.9 5.4 %all-to-all-done.5 = f32[8,8,256]{2,1,0:T(8,128)S(1)} async-done(((f32[8,8,256]{2,1,0:T(8,128)}), f32[8,8,256]{2,1,0:T(8,128)S(1)}, u32[]{:S(2)}, u32[]{:S(2)}) %all-to-all-start.5) | async-done | bytes 65568 | tf_op jit(solution)/shard_map/all_to_all | solution.py:230
  133.3 0.6 copy.50
  (27 shorter events, 0.3 us)
Async XLA Ops:
  0.6 95.4 %copy-start = (bf16[256,256]{1,0:T(8,128)(2,1)S(1)}, bf16[256,256]{1,0:T(8,128)(2,1)}, u32[]{:S(2)}) copy-start(bf16[256,256]{1,0:T(8,128)(2,1)} %param.18) | copy-start | bytes 393220
  0.6 18.7 %copy-start.1 = (bf16[2304,256]{1,0:T(8,128)(2,1)S(1)}, bf16[2304,256]{1,0:T(8,128)(2,1)}, u32[]{:S(2)}) copy-start(bf16[2304,256]{1,0:T(8,128)(2,1)} %emb_ref.1) | copy-start | bytes 3538948
  3.0 17.8 %copy-start.5 = (s32[256]{0:T(256)S(1)}, s32[256]{0:T(256)}, u32[]{:S(2)}) copy-start(s32[256]{0:T(256)} %param.24) | copy-start | bytes 3076
  5.2 16.4 %copy-start.2 = (bf16[474,256]{1,0:T(8,128)(2,1)S(1)}, bf16[474,256]{1,0:T(8,128)(2,1)}, u32[]{:S(2)}) copy-start(bf16[474,256]{1,0:T(8,128)(2,1)} %param.14) | copy-start | bytes 728068
  14.4 20.5 %all-to-all-start.1 = ((bf16[32,32,256]{2,1,0:T(8,128)(2,1)}), bf16[32,32,256]{2,1,0:T(8,128)(2,1)S(1)}, u32[]{:S(2)}, u32[]{:S(2)}) async-start(bf16[32,32,256]{2,1,0:T(8,128)(2,1)} %broadcast_in_dim.75), calls=%async_computation.1 | async-start | bytes 1048576 | tf_op jit(solution)/shard_map/all_to_all | solution.py:154
  34.9 48.5 %copy-start.6 = (s32[256]{0:T(256)S(1)}, s32[256]{0:T(256)}, u32[]{:S(2)}) copy-start(s32[256]{0:T(256)} %param.25) | copy-start | bytes 3076
  80.2 11.3 %all-to-all-start.2 = ((bf16[32,8,256]{2,1,0:T(8,128)(2,1)}), bf16[32,8,256]{2,1,0:T(8,128)(2,1)S(1)}, u32[]{:S(2)}, u32[]{:S(2)}) async-start(bf16[32,8,256]{2,1,0:T(8,128)(2,1)} %bitcast.55), calls=%async_computation.2 | async-start | bytes 262144 | tf_op jit(solution)/shard_map/all_to_all | solution.py:189
  92.2 10.8 %all-to-all-start.3 = ((bf16[32,8,256]{2,1,0:T(8,128)(2,1)}), bf16[32,8,256]{2,1,0:T(8,128)(2,1)S(1)}, u32[]{:S(2)}, u32[]{:S(2)}) async-start(bf16[32,8,256]{2,1,0:T(8,128)(2,1)} %broadcast_in_dim.78), calls=%async_computation.3 | async-start | bytes 262144 | tf_op jit(solution)/shard_map/all_to_all | solution.py:191
  103.1 0.7 copy-start.4
  107.6 18.7 %copy-start.3 = (f32[256,2304]{1,0:T(8,128)S(1)}, f32[256,2304]{1,0:T(8,128)}, u32[]{:S(2)}) copy-start(f32[256,2304]{1,0:T(8,128)} %get-tuple-element.9) | copy-start | bytes 7077892
  110.1 11.5 %all-to-all-start.4 = ((bf16[32,24,128]{2,1,0:T(8,128)(2,1)}), bf16[32,24,128]{2,1,0:T(8,128)(2,1)S(1)}, u32[]{:S(2)}, u32[]{:S(2)}) async-start(bf16[32,24,128]{2,1,0:T(8,128)(2,1)} %bitcast.22), calls=%async_computation.4 | async-start | bytes 393216 | tf_op jit(solution)/shard_map/all_to_all | solution.py:214
  122.9 10.4 %all-to-all-start.5 = ((f32[8,8,256]{2,1,0:T(8,128)}), f32[8,8,256]{2,1,0:T(8,128)S(1)}, u32[]{:S(2)}, u32[]{:S(2)}) async-start(f32[8,8,256]{2,1,0:T(8,128)} %broadcast_in_dim.85), calls=%async_computation.5 | async-start | bytes 131072 | tf_op jit(solution)/shard_map/all_to_all | solution.py:230

commit v2 on v1

--- a/solution.py
+++ b/solution.py
@@ -13,7 +13,9 @@
 F32 = jnp.float32
 BOTH = ("ent", "rep")
 NT = (((1,), (1,)), ((), ()))
+TN = (((0,), (0,)), ((), ()))
 VMEM_LIMIT = 56 * 2**20
+NEAR_LIMIT = 56 * 2**20
 
 
 def one_hot(index, rows):
@@ -21,43 +23,98 @@
     return jnp.where(where, jnp.asarray(1, BF16), jnp.asarray(0, BF16))
 
 
-def layer_kernel(
+def one_hot_wide(index, rows):
+    where = lax.broadcasted_iota(jnp.int32, (rows, index.shape[1]), 0) == index
+    return where.astype(F32).astype(BF16)
+
+
+def near_kernel(
+    first, count, src_ref, rel_ref, near_ref, relation_ref, *rest
+):
+    mixed_ref, held_ref, sems = rest[-3:]
+    rows_dev = near_ref.shape[1]
+
+    def save(i, slot):
+        return pltpu.make_async_copy(held_ref.at[slot], mixed_ref.at[i], sems.at[slot])
+
+    def one_block(i, carry):
+        slot = lax.rem(i, 2)
+        src = src_ref[pl.ds(first + i, 1), :]
+        rel = rel_ref[pl.ds(first + i, 1), :]
+        gathered = jnp.dot(near_ref[...], one_hot(src, rows_dev), preferred_element_type=F32)
+        relation = jnp.dot(
+            relation_ref[...], one_hot(rel, relation_ref.shape[1]), preferred_element_type=F32
+        )
+        mixed = jnp.where(src < rows_dev, gathered, 1.0) * relation
+
+        @pl.when(i >= 2)
+        def _():
+            save(first + i - 2, slot).wait()
+
+        held_ref[slot] = mixed.astype(BF16)
+        save(first + i, slot).start()
+        return carry
+
+    lax.fori_loop(0, count, one_block, 0)
+    for i in range(max(count - 2, 0), count):
+        save(first + i, i % 2).wait()
+
+
+def far_kernel(
     half_rel,
     src_ref,
     dst_ref,
     rel_ref,
     emb_ref,
-    near_ref,
     far_ref,
-    relation_ref,
     in_ref,
     out_ref,
     loop_ref,
     loop_rel_ref,
     head_ref,
+    mixed_ref,
     hidden_ref,
     heads_ref,
+    far_t_ref,
     gathered_ref,
+    held_ref,
+    sems,
 ):
     rows_dev = emb_ref.shape[0]
+    blocks = src_ref.shape[0]
     far_chunks = far_ref.shape[0]
 
+    def load(i, slot):
+        return pltpu.make_async_copy(mixed_ref.at[i], held_ref.at[slot], sems.at[slot])
+
+    load(0, 0).start()
+
+    def turn(j, carry):
+        far_t_ref[j] = jnp.transpose(far_ref[j])
+        return carry
+
+    lax.fori_loop(0, far_chunks, turn, 0)
+
     def one_block(i, carry):
+        slot = lax.rem(i, 2)
+
+        @pl.when(i + 1 < blocks)
+        def _():
+            load(i + 1, 1 - slot).start()
+
+        load(i, slot).wait()
         src = src_ref[pl.ds(i, 1), :]
         rel = rel_ref[pl.ds(i, 1), :]
-        gathered = jnp.dot(
-            near_ref[...], one_hot(src, rows_dev), preferred_element_type=F32
-        )
         if far_chunks == 1:
-            gathered += jnp.dot(
-                far_ref[0], one_hot(src - rows_dev, CHUNK), preferred_element_type=F32
+            gathered = jnp.dot(
+                far_t_ref[0], one_hot(src - rows_dev, CHUNK), preferred_element_type=F32
             )
         else:
-            gathered_ref[...] = gathered
+            gathered_ref[...] = jnp.zeros_like(gathered_ref)
 
             def one_chunk(j, carry):
                 gathered_ref[...] += jnp.dot(
-                    far_ref[j],
+                    far_t_ref[j],
                     one_hot(src - rows_dev - j * CHUNK, CHUNK),
                     preferred_element_type=F32,
                 )
@@ -65,10 +122,8 @@
 
             lax.fori_loop(0, far_chunks, one_chunk, 0)
             gathered = gathered_ref[...]
-        relation = jnp.dot(
-            relation_ref[...], one_hot(rel, relation_ref.shape[1]), preferred_element_type=F32
-        )
-        composed = (gathered * relation).astype(BF16)
+        mixed = held_ref[slot].astype(F32)
+        composed = (jnp.where(src < rows_dev, 1.0, gathered) * mixed).astype(BF16)
         key = dst_ref[pl.ds(i, 1), :] + jnp.where(rel >= half_rel, BLK, 0)
         selector = (
             lax.broadcasted_iota(jnp.int32, (2 * BLK, key.shape[1]), 0) == key
@@ -84,11 +139,41 @@
         hidden_ref[here, :] = jnp.tanh(preact).astype(BF16)
         return carry
 
-    lax.fori_loop(0, src_ref.shape[0], one_block, 0)
-    picks = lax.broadcasted_iota(jnp.int32, (head_ref.shape[0], rows_dev), 1) == head_ref[...]
-    heads_ref[...] = jnp.dot(
-        picks.astype(F32).astype(BF16), hidden_ref[...], preferred_element_type=F32
+    lax.fori_loop(0, blocks, one_block, 0)
+    picks = one_hot_wide(head_ref[...], rows_dev)
+    heads_ref[...] = lax.dot_general(
+        picks, hidden_ref[...], TN, preferred_element_type=F32
     ).astype(BF16)
+
+
+def pick_kernel(index_ref, emb_ref, offered_ref):
+    picks = one_hot_wide(index_ref[...], emb_ref.shape[0])
+    offered_ref[...] = lax.dot_general(
+        picks, emb_ref[...], TN, preferred_element_type=F32
+    ).astype(BF16)
+
+
+def near_call(first, count, blocks, src, rel, near, relation, mixed=None):
+    columns, edges = near.shape[0], src.shape[1]
+    flops = 2 * count * edges * columns * (near.shape[1] + relation.shape[1])
+    anywhere = pl.BlockSpec(memory_space=pltpu.HBM)
+    whole = pl.BlockSpec(memory_space=pltpu.VMEM)
+    more = () if mixed is None else (mixed,)
+    return pl.pallas_call(
+        functools.partial(near_kernel, first, count),
+        out_shape=jax.ShapeDtypeStruct((blocks, columns, edges), BF16),
+        in_specs=[whole] * 4 + [anywhere] * len(more),
+        out_specs=anywhere,
+        input_output_aliases={4: 0} if more else {},
+        scratch_shapes=[
+            pltpu.VMEM((2, columns, edges), BF16),
+            pltpu.SemaphoreType.DMA((2,)),
+        ],
+        compiler_params=pltpu.CompilerParams(vmem_limit_bytes=NEAR_LIMIT),
+        cost_estimate=pl.CostEstimate(
+            flops=flops, bytes_accessed=2 * count * edges * columns, transcendentals=0
+        ),
+    )(src, rel, near, relation, *more)
 
 
 def score_kernel(heads_ref, rel_ref, hidden_ref, scores_ref, weighted_ref, stats_ref):
@@ -141,49 +226,65 @@
     share = -(-batch_rows // groups)
     padded = share * devices
 
-    listed = export_rows[0]
-    slots = listed.shape[0]
-    is_owned = listed // rows_dev == member
-    picked = jnp.take(entity_emb, listed % rows_dev, axis=0)
-    offered = jnp.where(is_owned[:, None], picked, jnp.zeros_like(picked))
+    blocks = edge_src.shape[0]
+    relations = relation_emb.shape[0]
+    rel_count = -(-relations // 256) * 256
+    relation_t = jnp.pad(relation_emb, ((0, rel_count - relations), (0, 0))).T
+    near_t = entity_emb.T
+    early = max(blocks * 5 // 18, 1)
+
+    slots = export_rows.shape[1]
+    offered = pl.pallas_call(
+        pick_kernel,
+        out_shape=jax.ShapeDtypeStruct((slots, columns), BF16),
+        compiler_params=pltpu.CompilerParams(vmem_limit_bytes=NEAR_LIMIT),
+    )(export_rows - member * rows_dev, entity_emb)
     pieces = lax.all_to_all(offered, "rep", 0, 0, tiled=True)
+    mixed = near_call(0, early, blocks, edge_src, edge_rel, near_t, relation_t)
     mine = jnp.sum(
         pieces.reshape(copies, slots // copies, columns).astype(F32), axis=0
     ).astype(BF16)
+    mine, mixed = lax.optimization_barrier((mine, mixed))
     spread = jnp.broadcast_to(mine[None], (devices,) + mine.shape)
     table = lax.all_to_all(spread, BOTH, 0, 0).reshape(groups * slots, columns)
+    mixed = near_call(
+        early, blocks - early, blocks, edge_src, edge_rel, near_t, relation_t, mixed
+    )
     far_count = -(-(groups * slots) // CHUNK) * CHUNK
     far = jnp.pad(table, ((0, far_count - groups * slots), (0, 0)))
-    far = far.reshape(far_count // CHUNK, CHUNK, columns).transpose(0, 2, 1)
-
-    relations = relation_emb.shape[0]
-    rel_count = -(-relations // 256) * 256
-    relation_t = jnp.pad(relation_emb, ((0, rel_count - relations), (0, 0))).T
+    far = far.reshape(far_count // CHUNK, CHUNK, columns)
+
     local_head = jnp.pad(
         query_head - device * rows_dev, (0, padded - queries), constant_values=-1
-    )[:, None]
-
+    )[None]
+    whole = pl.BlockSpec(memory_space=pltpu.VMEM)
     hidden, heads = pl.pallas_call(
-        functools.partial(layer_kernel, relations // 2),
+        functools.partial(far_kernel, relations // 2),
         out_shape=(
             jax.ShapeDtypeStruct((rows_dev, columns), BF16),
             jax.ShapeDtypeStruct((padded, columns), BF16),
         ),
-        scratch_shapes=[pltpu.VMEM((columns, edge_src.shape[1]), F32)],
+        in_specs=[whole] * 10 + [pl.BlockSpec(memory_space=pltpu.HBM)],
+        out_specs=(whole, whole),
+        scratch_shapes=[
+            pltpu.VMEM((far.shape[0], columns, CHUNK), BF16),
+            pltpu.VMEM((columns, edge_src.shape[1]), F32),
+            pltpu.VMEM((2, columns, edge_src.shape[1]), BF16),
+            pltpu.SemaphoreType.DMA((2,)),
+        ],
         compiler_params=pltpu.CompilerParams(vmem_limit_bytes=VMEM_LIMIT),
     )(
         edge_src,
         edge_dst,
         edge_rel,
         entity_emb,
-        entity_emb.T,
         far,
-        relation_t,
         in_weight,
         out_weight,
         loop_weight,
         loop_rel[None],
         local_head,
+        mixed,
     )
 
     parts = lax.all_to_all(heads, BOTH, 0, 0, tiled=True).reshape(devices, share, columns)

time: 135 us -> 131 us (0.970)
  waiting for transfers between devices: 40.9 us -> 28.6 us
  Pallas kernels: 48.2 us -> 58.8 us
  starting transfers between devices: 16.5 us -> 25.4 us
  blocking collectives: 8.13 us -> 0 us
  local copies, waits for them, and re-layouts: 14.1 us -> 11.5 us
    all_to_all x1, waiting for transfers between devices: 12.3 us -> 0.01 us  [body(): table = lax.all_to_all(spread, BOTH, 0, 0).reshape(groups * slots, columns)]
    pallas_call x1 -> x4, Pallas kernels: 44.3 us -> 55 us  [the longest x2 28.5 us: near_call(): pl.pallas_call(functools.partial(near_kernel, first, count), out_shape=ja...]
    all_to_all x1 -> x0, blocking collectives: 8.13 us -> none  [body(): pieces = lax.all_to_all(offered, 'rep', 0, 0, tiled=True)]
    all_to_all x0 -> x1, starting transfers between devices: none -> 4.21 us  [body(): pieces = lax.all_to_all(offered, 'rep', 0, 0, tiled=True)]
    all_to_all x1, starting transfers between devices: 3.07 us -> 5.84 us  [body(): lax.all_to_all(heads, BOTH, 0, 0, tiled=True)]
    gather x1 -> x0, local copies, waits for them, and re-layouts: 2.18 us -> none  [body(): picked = jnp.take(entity_emb, listed % rows_dev, axis=0)]
    all_to_all x1, starting transfers between devices: 4.92 us -> 6.87 us  [body(): table = lax.all_to_all(spread, BOTH, 0, 0).reshape(groups * slots, columns)]
    unnamed x23, local copies, waits for them, and re-layouts: 4.53 us -> 6.13 us
  transfers between devices with their start and end apart: 5 -> 6, of which waited for: 5 -> 4; matrix products, arithmetic and copies ran while one was open for 5% -> 6% of each run, Pallas kernels for 0% -> 22%
where the time goes in v2:
time: 131 us; the launch traced here: 130 us
  Pallas kernels  58.8 us (45%)
  waiting for transfers between devices  28.6 us (22%)
  starting transfers between devices  25.4 us (19%)
  local copies, waits for them, and re-layouts  11.5 us (9%)
  other arithmetic  3.85 us (3%)
    pallas_call x2, Pallas kernels, near_call(): pl.pallas_call(functools.partial(near_kernel, first, count), out_shape=ja...  28.5 us
    pallas_call x1, Pallas kernels, body(): pl.pallas_call(functools.partial(far_kernel, relations // 2), out_shape=(...  24.2 us
    all_to_all x1, waiting for transfers between devices, body(): received = lax.all_to_all(payload, BOTH, 0, 0).reshape(devices, -1)  8.88 us
    all_to_all x1, waiting for transfers between devices, body(): lax.all_to_all(heads, BOTH, 0, 0, tiled=True)  8.19 us
    all_to_all x1, starting transfers between devices, body(): table = lax.all_to_all(spread, BOTH, 0, 0).reshape(groups * slots, columns)  6.87 us
    unnamed x23, local copies, waits for them, and re-layouts  6.13 us
    all_to_all x1, waiting for transfers between devices, body(): lax.all_to_all(jnp.broadcast_to(own_heads[None], (devices, share, columns...  6.12 us
    all_to_all x1, starting transfers between devices, body(): lax.all_to_all(heads, BOTH, 0, 0, tiled=True)  5.84 us
  transfers between devices with their start and end apart: 6, of which 4 were waited for; matrix products, arithmetic and copies ran while one was open for 6% of the time, Pallas kernels for 22%

profile of v2, /device:TPU:0, one launch (start us, length us, event | category | flops | bytes accessed | tf_op | source)
XLA Modules:
  0.0 129.9 jit_solution(15711977736176277268)
XLA Ops:
  0.6 0.0 copy-start
  0.6 0.0 copy-start.1
  0.7 1.2 broadcast_subtract_fusion.2.index_ref
  1.9 2.3 %shard_map.140 = bf16[128,256]{1,0:T(8,128)(2,1)} custom-call(s32[1,128]{1,0:T(1,128)} %broadcast_subtract_fusion.2.index_ref, bf16[2304,256]{1,0:T(8,128)(2,1)} %emb_ref.3), custom_call_target="tpu_custom_call" | custom-call | tf_op jit(solution)/shard_map/pallas_call | solution.py:237
  4.2 4.2 %all-to-all-start = ((bf16[4,32,256]{2,1,0:T(8,128)(2,1)}), bf16[4,32,256]{2,1,0:T(8,128)(2,1)S(1)}, u32[]{:S(2)}, u32[]{:S(2)}) async-start(bf16[4,32,256]{2,1,0:T(8,128)(2,1)} %bitcast.48), calls=%async_computation | async-start | bytes 131072 | tf_op jit(solution)/shard_map/all_to_all | solution.py:242
  8.4 2.4 %copy.20 = bf16[2304,256]{0,1:T(8,128)(2,1)} copy(bf16[2304,256]{1,0:T(8,128)(2,1)} %emb_ref.3) | data formatting | bytes 2359296 | tf_op args[0]
  10.8 0.0 copy-done.1
  10.8 0.1 copy.21
  10.9 0.7 pad_bitcast_fusion.relation_ref
  11.6 8.9 %shard_map.141.rest_0_ = bf16[18,256,768]{2,1,0:T(8,128)(2,1)} custom-call(s32[18,768]{1,0:T(8,128)} %src_ref.5, s32[18,768]{1,0:T(8,128)} %rel_ref.5, bf16[256,2304]{1,0:T(8,128)(2,1)} %bitcast.38, bf16[256,512]{1,0:T(8,128)(2,1)} %pad_bitcast_fusion.relation_ref), custom_call_target="tpu_custom_call" | custom-call | flops 5536481280 | bytes 1966080 | tf_op jit(solution)/shard_map/pallas_call | solution.py:162
  20.5 0.0 copy-done.5
  20.5 0.6 broadcast_subtract_fusion.1
  21.1 0.0 all-to-all-done
  21.1 0.8 broadcast_in_dim.49
  22.0 6.9 %all-to-all-start.1 = ((bf16[32,32,256]{2,1,0:T(8,128)(2,1)}), bf16[32,32,256]{2,1,0:T(8,128)(2,1)S(1)}, u32[]{:S(2)}, u32[]{:S(2)}) async-start(bf16[32,32,256]{2,1,0:T(8,128)(2,1)} %broadcast_in_dim.49), calls=%async_computation.1 | async-start | bytes 1048576 | tf_op jit(solution)/shard_map/all_to_all | solution.py:249
  28.9 19.6 %shard_map.142.mixed_ref = bf16[18,256,768]{2,1,0:T(8,128)(2,1)} custom-call(s32[18,768]{1,0:T(8,128)} %src_ref.5, s32[18,768]{1,0:T(8,128)} %rel_ref.5, bf16[256,2304]{1,0:T(8,128)(2,1)} %bitcast.39, bf16[256,512]{1,0:T(8,128)(2,1)} %pad_bitcast_fusion.relation_ref, bf16[18,256,768]{2,1,0:T(8,128)(2,1)} %shard_map.141.rest_0_), custom_call_target="tpu_custom_call", output_to_operand_aliasing={{}: (4, {})} | custom-call | flops 14394851328 | bytes 5111808 | tf_op jit(solution)/shard_map/pallas_call | solution.py:162
  48.5 0.0 all-to-all-done.1
  48.5 0.0 copy-start.3
  48.5 0.8 copy-done.3
  49.3 24.2 %shard_map.143 = (bf16[2304,256]{1,0:T(8,128)(2,1)}, bf16[256,256]{1,0:T(8,128)(2,1)}) custom-call(s32[18,768]{1,0:T(8,128)} %src_ref.5, s32[18,768]{1,0:T(8,128)} %dst_ref.1, s32[18,768]{1,0:T(8,128)} %rel_ref.5, bf16[2304,256]{1,0:T(8,128)(2,1)} %emb_ref.3, bf16[1,1024,256]{2,1,0:T(8,128)(2,1)} %bitcast.37, bf16[256,256]{1,0:T(8,128)(2,1)} %in_ref.1, ...), custom_call_target="tpu_custom_call" | custom-call | tf_op jit(solution)/shard_map/pallas_call | solution.py:261
  73.5 5.8 %all-to-all-start.2 = ((bf16[32,8,256]{2,1,0:T(8,128)(2,1)}), bf16[32,8,256]{2,1,0:T(8,128)(2,1)S(1)}, u32[]{:S(2)}, u32[]{:S(2)}) async-start(bf16[32,8,256]{2,1,0:T(8,128)(2,1)} %bitcast.50), calls=%async_computation.2 | async-start | bytes 262144 | tf_op jit(solution)/shard_map/all_to_all | solution.py:290
  79.3 0.0 copy-done.6
  79.4 8.2 %all-to-all-done.2 = bf16[32,8,256]{2,1,0:T(8,128)(2,1)S(1)} async-done(((bf16[32,8,256]{2,1,0:T(8,128)(2,1)}), bf16[32,8,256]{2,1,0:T(8,128)(2,1)S(1)}, u32[]{:S(2)}, u32[]{:S(2)}) %all-to-all-start.2) | async-done | bytes 131104 | tf_op jit(solution)/shard_map/all_to_all | solution.py:290
  87.6 0.7 broadcast_in_dim.52
  88.3 2.6 %all-to-all-start.3 = ((bf16[32,8,256]{2,1,0:T(8,128)(2,1)}), bf16[32,8,256]{2,1,0:T(8,128)(2,1)S(1)}, u32[]{:S(2)}, u32[]{:S(2)}) async-start(bf16[32,8,256]{2,1,0:T(8,128)(2,1)} %broadcast_in_dim.52), calls=%async_computation.3 | async-start | bytes 262144 | tf_op jit(solution)/shard_map/all_to_all | solution.py:292
  90.9 1.2 gather_fusion
  92.0 0.0 copy-done
  92.0 0.9 fusion.rel_ref
  92.9 6.1 %all-to-all-done.3 = bf16[32,8,256]{2,1,0:T(8,128)(2,1)S(1)} async-done(((bf16[32,8,256]{2,1,0:T(8,128)(2,1)}), bf16[32,8,256]{2,1,0:T(8,128)(2,1)S(1)}, u32[]{:S(2)}, u32[]{:S(2)}) %all-to-all-start.3) | async-done | bytes 131104 | tf_op jit(solution)/shard_map/all_to_all | solution.py:292
  99.1 0.6 copy-done.4
  99.7 3.9 %shard_map.144 = (f32[256,2304]{1,0:T(8,128)}, bf16[256,256]{1,0:T(8,128)(2,1)}, bf16[16,256]{1,0:T(8,128)(2,1)}) custom-call(bf16[256,256]{1,0:T(8,128)(2,1)} %bitcast.45, f32[256,256]{1,0:T(8,128)} %fusion.rel_ref, bf16[2304,256]{1,0:T(8,128)(2,1)} %get-tuple-element.12.hidden_ref), custom_call_target="tpu_custom_call" | custom-call | tf_op jit(solution)/shard_map/pallas_call | solution.py:299
  103.6 1.1 copy.22
  104.7 0.7 slice_bitcast_fusion
  105.4 0.7 copy.30
  106.1 2.6 %all-to-all-start.4 = ((bf16[32,24,128]{2,1,0:T(8,128)(2,1)}), bf16[32,24,128]{2,1,0:T(8,128)(2,1)S(1)}, u32[]{:S(2)}, u32[]{:S(2)}) async-start(bf16[32,24,128]{2,1,0:T(8,128)(2,1)} %bitcast.19), calls=%async_computation.4 | async-start | bytes 393216 | tf_op jit(solution)/shard_map/all_to_all | solution.py:315
  108.7 8.9 %all-to-all-done.4 = bf16[32,24,128]{2,1,0:T(8,128)(2,1)S(1)} async-done(((bf16[32,24,128]{2,1,0:T(8,128)(2,1)}), bf16[32,24,128]{2,1,0:T(8,128)(2,1)S(1)}, u32[]{:S(2)}, u32[]{:S(2)}) %all-to-all-start.4) | async-done | bytes 196640 | tf_op jit(solution)/shard_map/all_to_all | solution.py:315
  117.6 0.1 reshape.74
  117.7 0.1 slice_add_fusion
  117.9 0.1 dynamic-slice
  118.0 0.1 dynamic-slice_divide_fusion
  118.0 0.1 mul.35
  118.2 0.1 copy.32
  118.2 0.1 multiply_reduce_fusion
  118.3 0.6 broadcast_in_dim.59
  118.9 3.4 %all-to-all-start.5 = ((f32[8,8,256]{2,1,0:T(8,128)}), f32[8,8,256]{2,1,0:T(8,128)S(1)}, u32[]{:S(2)}, u32[]{:S(2)}) async-start(f32[8,8,256]{2,1,0:T(8,128)} %broadcast_in_dim.59), calls=%async_computation.5 | async-start | bytes 131072 | tf_op jit(solution)/shard_map/all_to_all | solution.py:331
  122.3 1.6 %broadcast_subtract_fusion = f32[256,2304]{1,0:T(8,128)} fusion(f32[256,2304]{1,0:T(8,128)S(1)} %copy-done.2, f32[256]{0:T(256)S(1)} %log_add_fusion), kind=kLoop, calls=%fused_computation.1 | loop fusion | flops 589824 | bytes 4719616 | tf_op jit(solution)/shard_map/sub | solution.py:334
  123.9 5.4 %all-to-all-done.5 = f32[8,8,256]{2,1,0:T(8,128)S(1)} async-done(((f32[8,8,256]{2,1,0:T(8,128)}), f32[8,8,256]{2,1,0:T(8,128)S(1)}, u32[]{:S(2)}, u32[]{:S(2)}) %all-to-all-start.5) | async-done | bytes 65568 | tf_op jit(solution)/shard_map/all_to_all | solution.py:331
  129.3 0.6 copy.50
  (20 shorter events, 0.3 us)
Async XLA Ops:
  0.6 91.4 %copy-start = (bf16[256,256]{1,0:T(8,128)(2,1)S(1)}, bf16[256,256]{1,0:T(8,128)(2,1)}, u32[]{:S(2)}) copy-start(bf16[256,256]{1,0:T(8,128)(2,1)} %param.18) | copy-start | bytes 393220
  0.6 10.1 %copy-start.1 = (bf16[474,256]{1,0:T(8,128)(2,1)S(1)}, bf16[474,256]{1,0:T(8,128)(2,1)}, u32[]{:S(2)}) copy-start(bf16[474,256]{1,0:T(8,128)(2,1)} %param.14) | copy-start | bytes 728068
  4.2 16.9 %all-to-all-start = ((bf16[4,32,256]{2,1,0:T(8,128)(2,1)}), bf16[4,32,256]{2,1,0:T(8,128)(2,1)S(1)}, u32[]{:S(2)}, u32[]{:S(2)}) async-start(bf16[4,32,256]{2,1,0:T(8,128)(2,1)} %bitcast.48), calls=%async_computation | async-start | bytes 131072 | tf_op jit(solution)/shard_map/all_to_all | solution.py:242
  11.6 8.9 %copy-start.5 = (s32[256]{0:T(256)S(1)}, s32[256]{0:T(256)}, u32[]{:S(2)}) copy-start(s32[256]{0:T(256)} %param.24) | copy-start | bytes 3076
  22.0 26.5 %all-to-all-start.1 = ((bf16[32,32,256]{2,1,0:T(8,128)(2,1)}), bf16[32,32,256]{2,1,0:T(8,128)(2,1)S(1)}, u32[]{:S(2)}, u32[]{:S(2)}) async-start(bf16[32,32,256]{2,1,0:T(8,128)(2,1)} %broadcast_in_dim.49), calls=%async_computation.1 | async-start | bytes 1048576 | tf_op jit(solution)/shard_map/all_to_all | solution.py:249
  48.5 0.8 copy-start.3
  49.3 30.1 %copy-start.6 = (s32[256]{0:T(256)S(1)}, s32[256]{0:T(256)}, u32[]{:S(2)}) copy-start(s32[256]{0:T(256)} %param.25) | copy-start | bytes 3076
  73.5 14.1 %all-to-all-start.2 = ((bf16[32,8,256]{2,1,0:T(8,128)(2,1)}), bf16[32,8,256]{2,1,0:T(8,128)(2,1)S(1)}, u32[]{:S(2)}, u32[]{:S(2)}) async-start(bf16[32,8,256]{2,1,0:T(8,128)(2,1)} %bitcast.50), calls=%async_computation.2 | async-start | bytes 262144 | tf_op jit(solution)/shard_map/all_to_all | solution.py:290
  88.3 10.8 %all-to-all-start.3 = ((bf16[32,8,256]{2,1,0:T(8,128)(2,1)}), bf16[32,8,256]{2,1,0:T(8,128)(2,1)S(1)}, u32[]{:S(2)}, u32[]{:S(2)}) async-start(bf16[32,8,256]{2,1,0:T(8,128)(2,1)} %broadcast_in_dim.52), calls=%async_computation.3 | async-start | bytes 262144 | tf_op jit(solution)/shard_map/all_to_all | solution.py:292
  99.1 0.6 copy-start.4
  103.6 18.7 %copy-start.2 = (f32[256,2304]{1,0:T(8,128)S(1)}, f32[256,2304]{1,0:T(8,128)}, u32[]{:S(2)}) copy-start(f32[256,2304]{1,0:T(8,128)} %get-tuple-element.13) | copy-start | bytes 7077892
  106.1 11.5 %all-to-all-start.4 = ((bf16[32,24,128]{2,1,0:T(8,128)(2,1)}), bf16[32,24,128]{2,1,0:T(8,128)(2,1)S(1)}, u32[]{:S(2)}, u32[]{:S(2)}) async-start(bf16[32,24,128]{2,1,0:T(8,128)(2,1)} %bitcast.19), calls=%async_computation.4 | async-start | bytes 393216 | tf_op jit(solution)/shard_map/all_to_all | solution.py:315
  118.9 10.4 %all-to-all-start.5 = ((f32[8,8,256]{2,1,0:T(8,128)}), f32[8,8,256]{2,1,0:T(8,128)S(1)}, u32[]{:S(2)}, u32[]{:S(2)}) async-start(f32[8,8,256]{2,1,0:T(8,128)} %broadcast_in_dim.59), calls=%async_computation.5 | async-start | bytes 131072 | tf_op jit(solution)/shard_map/all_to_all | solution.py:331

commit v3 on v2

v3 whole, which is shorter than its diff:
```python
import functools

import jax
import jax.numpy as jnp
from jax import lax
from jax.experimental import pallas as pl
from jax.experimental.pallas import tpu as pltpu
from jax.sharding import PartitionSpec as P

BLK = 128
CHUNK = 1024
BF16 = jnp.bfloat16
F32 = jnp.float32
BOTH = ("ent", "rep")
NT = (((1,), (1,)), ((), ()))
TN = (((0,), (0,)), ((), ()))
VMEM_LIMIT = 56 * 2**20
STEP = 2
AHEAD = 5


def one_hot(index, rows):
    where = lax.broadcasted_iota(jnp.int16, (rows, index.shape[1]), 0) == index.astype(jnp.int16)
    return jnp.where(where, jnp.asarray(1, BF16), jnp.asarray(0, BF16))


def one_hot_wide(index, rows):
    where = lax.broadcasted_iota(jnp.int32, (rows, index.shape[1]), 0) == index
    return where.astype(F32).astype(BF16)


def order_blocks(head_ref, first_block, blocks, flag_ref, order_ref):
    def clear(b, carry):
        flag_ref[b] = 0
        return carry

    def mark(q, carry):
        block = lax.shift_right_arithmetic(head_ref[q], BLK.bit_length() - 1) - first_block
        flag_ref[jnp.where((block >= 0) & (block < blocks), block, blocks)] = 1
        return carry

    def place(wanted, b, position):
        taken = flag_ref[b] == wanted
        order_ref[jnp.where(taken, position, blocks + 1)] = b
        return position + taken.astype(jnp.int32)

    lax.fori_loop(0, blocks, clear, 0)
    lax.fori_loop(0, head_ref.shape[0], mark, 0, unroll=8)
    found = lax.fori_loop(0, blocks, functools.partial(place, 1), 0)
    lax.fori_loop(0, blocks, functools.partial(place, 0), found)
    order_ref[blocks] = found


def head_steps(order_ref, blocks):
    return (order_ref[blocks] + STEP - 1) // STEP


def near_kernel(part, ahead, *refs):
    if part == 0:
        base_ref, head_ref, src_ref, rel_ref, near_ref, relation_ref = refs[:6]
        mixed_ref, order_ref, held_ref, sems, flag_ref = refs[6:]
    else:
        order_ref, src_ref, rel_ref, near_ref, relation_ref, _ = refs[:6]
        mixed_ref, held_ref, sems = refs[6:]
    blocks = src_ref.shape[0]
    rows_dev = near_ref.shape[1]
    steps = blocks // STEP
    if part == 0:
        order_blocks(head_ref, base_ref[0], blocks, flag_ref, order_ref)
        start, stop = 0, 1
    else:
        middle = jnp.maximum(head_steps(order_ref, blocks), ahead)
        start, stop = (1, middle) if part == 1 else (middle, steps)
    count = stop - start

    def save(step, slot):
        return pltpu.make_async_copy(held_ref.at[slot], mixed_ref.at[step], sems.at[slot])

    def one_step(i, carry):
        slot = lax.rem(i, 2)

        @pl.when(i >= 2)
        def _():
            save(start + i - 2, slot).wait()

        for u in range(STEP):
            block = order_ref[(start + i) * STEP + u]
            src = src_ref[pl.ds(block, 1), :]
            rel = rel_ref[pl.ds(block, 1), :]
            gathered = jnp.dot(near_ref[...], one_hot(src, rows_dev), preferred_element_type=F32)
            relation = jnp.dot(
                relation_ref[...],
                one_hot(rel, relation_ref.shape[1]),
                preferred_element_type=F32,
            )
            mixed = jnp.where(src < rows_dev, gathered, 1.0) * relation
            held_ref[slot, u] = mixed.astype(BF16)
        save(start + i, slot).start()
        return carry

    lax.fori_loop(0, count, one_step, 0)
    for back in (2, 1):

        @pl.when(jnp.int32(count) >= back)
        def _():
            save(start + count - back, lax.rem(jnp.int32(count) - back + 2, 2)).wait()


def far_kernel(
    half_rel,
    last,
    order_ref,
    src_ref,
    dst_ref,
    rel_ref,
    emb_ref,
    far_ref,
    in_ref,
    out_ref,
    loop_ref,
    loop_rel_ref,
    extra_ref,
    mixed_ref,
    hidden_ref,
    *rest,
):
    far_t_ref, gathered_ref, agg_ref, held_ref, sems = rest[-5:]
    rows_dev = emb_ref.shape[0]
    blocks = src_ref.shape[0]
    far_chunks = far_ref.shape[0]
    middle = head_steps(order_ref, blocks)
    start, stop = (middle, blocks // STEP) if last else (0, middle)

    def load(step, slot):
        return pltpu.make_async_copy(mixed_ref.at[step], held_ref.at[slot], sems.at[slot])

    @pl.when(start < stop)
    def _():
        load(start, 0).start()

    def turn(j, carry):
        far_t_ref[j] = jnp.transpose(far_ref[j])
        return carry

    lax.fori_loop(0, far_chunks, turn, 0)
    hidden_ref[...] = extra_ref[...] if last else jnp.zeros_like(hidden_ref)

    def look_up(src, u):
        if far_chunks == 1:
            return jnp.dot(
                far_t_ref[0], one_hot(src - rows_dev, CHUNK), preferred_element_type=F32
            )
        gathered_ref[u] = jnp.zeros(gathered_ref.shape[1:], F32)

        def one_chunk(j, carry):
            gathered_ref[u] += jnp.dot(
                far_t_ref[j],
                one_hot(src - rows_dev - j * CHUNK, CHUNK),
                preferred_element_type=F32,
            )
            return carry

        lax.fori_loop(0, far_chunks, one_chunk, 0)
        return gathered_ref[u]

    def one_step(i, carry):
        slot = lax.rem(i, 2)

        @pl.when(start + i + 1 < stop)
        def _():
            load(start + i + 1, 1 - slot).start()

        load(start + i, slot).wait()
        rows = [pl.ds(order_ref[(start + i) * STEP + u], 1) for u in range(STEP)]
        srcs = [src_ref[row, :] for row in rows]
        found = [look_up(src, u) for u, src in enumerate(srcs)]
        composed = [
            (jnp.where(srcs[u] < rows_dev, 1.0, found[u]) * held_ref[slot, u].astype(F32)).astype(
                BF16
            )
            for u in range(STEP)
        ]
        for u, row in enumerate(rows):
            key = dst_ref[row, :] + jnp.where(rel_ref[row, :] >= half_rel, BLK, 0)
            selector = (
                lax.broadcasted_iota(jnp.int32, (2 * BLK, key.shape[1]), 0) == key
            ).astype(F32)
            counts = jnp.sum(selector, axis=1, keepdims=True)
            sums = lax.dot_general(
                selector.astype(BF16), composed[u], NT, preferred_element_type=F32
            )
            agg = (sums / jnp.maximum(counts, 1.0)).astype(BF16)
            here = pl.ds(pl.multiple_of(((start + i) * STEP + u) * BLK, BLK), BLK)
            agg_ref[0, here, :] = agg[:BLK]
            agg_ref[1, here, :] = agg[BLK:]
        return carry

    lax.fori_loop(0, stop - start, one_step, 0)

    def finish(i, carry):
        here = pl.ds(pl.multiple_of(i * STEP * BLK, STEP * BLK), STEP * BLK)
        rows = [
            pl.ds(pl.multiple_of(order_ref[i * STEP + u] * BLK, BLK), BLK) for u in range(STEP)
        ]
        own = jnp.concatenate([emb_ref[row, :] for row in rows], axis=0)
        own = (own.astype(F32) * loop_rel_ref[...]).astype(BF16)
        preact = jnp.dot(agg_ref[0, here, :], in_ref[...], preferred_element_type=F32)
        preact += jnp.dot(agg_ref[1, here, :], out_ref[...], preferred_element_type=F32)
        preact += jnp.dot(own, loop_ref[...], preferred_element_type=F32)
        hidden = jnp.tanh(preact).astype(BF16)
        for u, row in enumerate(rows):
            hidden_ref[row, :] = hidden[u * BLK : (u + 1) * BLK]
        return carry

    lax.fori_loop(start, stop, finish, 0)
    if not last:
        picks = one_hot_wide(extra_ref[...], rows_dev)
        rest[0][...] = lax.dot_general(
            picks, hidden_ref[...], TN, preferred_element_type=F32
        ).astype(BF16)


def pick_kernel(index_ref, emb_ref, offered_ref):
    picks = one_hot_wide(index_ref[...], emb_ref.shape[0])
    offered_ref[...] = lax.dot_general(
        picks, emb_ref[...], TN, preferred_element_type=F32
    ).astype(BF16)


SMEM = pl.BlockSpec(memory_space=pltpu.SMEM)
WHOLE = pl.BlockSpec(memory_space=pltpu.VMEM)
HBM = pl.BlockSpec(memory_space=pltpu.HBM)


def near_call(part, ahead, src, rel, near, relation, more):
    columns, edges = near.shape[0], src.shape[1]
    blocks = src.shape[0]
    steps = blocks // STEP
    count = STEP * (1, ahead - 1, steps - ahead)[part]
    flops = 2 * count * edges * columns * (near.shape[1] + relation.shape[1])
    mixed_type = jax.ShapeDtypeStruct((steps, STEP, columns, edges), BF16)
    order_type = jax.ShapeDtypeStruct((blocks + 2,), jnp.int32)
    scratch = [
        pltpu.VMEM((2, STEP, columns, edges), BF16),
        pltpu.SemaphoreType.DMA((2,)),
    ]
    settings = dict(
        compiler_params=pltpu.CompilerParams(vmem_limit_bytes=VMEM_LIMIT),
        cost_estimate=pl.CostEstimate(
            flops=flops, bytes_accessed=2 * count * edges * columns, transcendentals=0
        ),
    )
    if part == 0:
        return pl.pallas_call(
            functools.partial(near_kernel, part, ahead),
            out_shape=(mixed_type, order_type),
            in_specs=[SMEM] * 2 + [WHOLE] * 4,
            out_specs=(HBM, SMEM),
            scratch_shapes=scratch + [pltpu.SMEM((blocks + 1,), jnp.int32)],
            **settings,
        )(*more, src, rel, near, relation)
    mixed, order = more
    return pl.pallas_call(
        functools.partial(near_kernel, part, ahead),
        out_shape=mixed_type,
        in_specs=[SMEM] + [WHOLE] * 4 + [HBM],
        out_specs=HBM,
        input_output_aliases={5: 0},
        scratch_shapes=scratch,
        **settings,
    )(order, src, rel, near, relation, mixed)


def far_call(half_rel, last, order, edges, emb, far, weights, extra, mixed, padded):
    rows_dev, columns = emb.shape
    blocks, width = edges[0].shape
    hidden_type = jax.ShapeDtypeStruct((rows_dev, columns), BF16)
    heads_type = jax.ShapeDtypeStruct((padded, columns), BF16)
    return pl.pallas_call(
        functools.partial(far_kernel, half_rel, last),
        out_shape=hidden_type if last else (hidden_type, heads_type),
        in_specs=[SMEM] + [WHOLE] * 10 + [HBM],
        out_specs=WHOLE if last else (WHOLE, WHOLE),
        scratch_shapes=[
            pltpu.VMEM((far.shape[0], columns, CHUNK), BF16),
            pltpu.VMEM((STEP, columns, width if far.shape[0] > 1 else 128), F32),
            pltpu.VMEM((2, rows_dev, columns), BF16),
            pltpu.VMEM((2, STEP, columns, width), BF16),
            pltpu.SemaphoreType.DMA((2,)),
        ],
        compiler_params=pltpu.CompilerParams(vmem_limit_bytes=VMEM_LIMIT),
        cost_estimate=pl.CostEstimate(
            flops=blocks * width * columns * far.shape[0] * CHUNK,
            bytes_accessed=blocks * width * columns,
            transcendentals=0,
        ),
    )(order, *edges, emb, far, *weights, extra, mixed)


def score_kernel(heads_ref, rel_ref, hidden_ref, scores_ref, weighted_ref, stats_ref):
    query = (heads_ref[...].astype(F32) * rel_ref[...]).astype(BF16)
    scores = lax.dot_general(query, hidden_ref[...], NT, preferred_element_type=F32)
    scores_ref[...] = scores
    top = jnp.max(scores, axis=1, keepdims=True)
    high = top.astype(BF16)
    low = (top - high.astype(F32)).astype(BF16)
    top = high.astype(F32) + low.astype(F32)
    weights = jnp.exp(scores - top)
    total = jnp.sum(weights, axis=1, keepdims=True)
    weighted_ref[...] = jnp.dot(
        weights.astype(BF16), hidden_ref[...], preferred_element_type=F32
    ).astype(BF16)
    total_high = total.astype(BF16)
    total_low = (total - total_high.astype(F32)).astype(BF16)
    lanes = lax.broadcasted_iota(jnp.int32, (query.shape[0], 128), 1)
    wide = jnp.where(lanes == 0, high.astype(F32), 0.0)
    wide = jnp.where(lanes == 1, low.astype(F32), wide)
    wide = jnp.where(lanes == 2, total_high.astype(F32), wide)
    wide = jnp.where(lanes == 3, total_low.astype(F32), wide)
    stats_ref[...] = jnp.transpose(wide)[: stats_ref.shape[0]].astype(BF16)


def body(
    entity_emb,
    relation_emb,
    in_weight,
    out_weight,
    loop_weight,
    rel_weight,
    loop_rel,
    edge_src,
    edge_dst,
    edge_rel,
    export_rows,
    query_head,
    query_rel,
):
    groups = lax.axis_size("ent")
    copies = lax.axis_size("rep")
    devices = groups * copies
    group = lax.axis_index("ent")
    member = lax.axis_index("rep")
    device = group * copies + member
    rows_dev, columns = entity_emb.shape
    queries = query_head.shape[0]
    batch_rows = queries // copies
    share = -(-batch_rows // groups)
    padded = share * devices

    blocks = edge_src.shape[0]
    relations = relation_emb.shape[0]
    rel_count = -(-relations // 256) * 256
    relation_t = jnp.pad(relation_emb, ((0, rel_count - relations), (0, 0))).T
    near_t = entity_emb.T
    ahead = min(AHEAD, blocks // STEP)

    slots = export_rows.shape[1]
    offered = pl.pallas_call(
        pick_kernel,
        out_shape=jax.ShapeDtypeStruct((slots, columns), BF16),
        compiler_params=pltpu.CompilerParams(vmem_limit_bytes=VMEM_LIMIT),
    )(export_rows - member * rows_dev, entity_emb)
    pieces = lax.all_to_all(offered, "rep", 0, 0, tiled=True)
    mixed, order = near_call(
        0, ahead, edge_src, edge_rel, near_t, relation_t, ((device * blocks)[None], query_head)
    )
    mine = jnp.sum(
        pieces.reshape(copies, slots // copies, columns).astype(F32), axis=0
    ).astype(BF16)
    mine, mixed = lax.optimization_barrier((mine, mixed))
    spread = jnp.broadcast_to(mine[None], (devices,) + mine.shape)
    table = lax.all_to_all(spread, BOTH, 0, 0).reshape(groups * slots, columns)
    mixed = near_call(1, ahead, edge_src, edge_rel, near_t, relation_t, (mixed, order))
    far_count = -(-(groups * slots) // CHUNK) * CHUNK
    far = jnp.pad(table, ((0, far_count - groups * slots), (0, 0)))
    far = far.reshape(far_count // CHUNK, CHUNK, columns)

    local_head = jnp.pad(
        query_head - device * rows_dev, (0, padded - queries), constant_values=-1
    )[None]
    weights = (in_weight, out_weight, loop_weight, loop_rel[None])
    edges = (edge_src, edge_dst, edge_rel)
    half_rel = relations // 2
    hidden, heads = far_call(
        half_rel, False, order, edges, entity_emb, far, weights, local_head, mixed, padded
    )
    heads, mixed = lax.optimization_barrier((heads, mixed))
    parts = lax.all_to_all(heads, BOTH, 0, 0, tiled=True).reshape(devices, share, columns)
    mixed = near_call(2, ahead, edge_src, edge_rel, near_t, relation_t, (mixed, order))
    own_heads = jnp.sum(parts.astype(F32), axis=0).astype(BF16)
    own_heads, mixed = lax.optimization_barrier((own_heads, mixed))
    head_rows = lax.all_to_all(
        jnp.broadcast_to(own_heads[None], (devices, share, columns)), BOTH, 0, 0
    ).reshape(padded, columns)[:queries]
    hidden = far_call(
        half_rel, True, order, edges, entity_emb, far, weights, hidden, mixed, padded
    )
    query_factor = jnp.dot(
        jnp.take(relation_emb, query_rel, axis=0), rel_weight, preferred_element_type=F32
    )

    scores, weighted, stats = pl.pallas_call(
        score_kernel,
        out_shape=(
            jax.ShapeDtypeStruct((queries, rows_dev), F32),
            jax.ShapeDtypeStruct((queries, columns), BF16),
            jax.ShapeDtypeStruct((16, queries), BF16),
        ),
        compiler_params=pltpu.CompilerParams(vmem_limit_bytes=VMEM_LIMIT),
    )(head_rows, query_factor, hidden)

    split = weighted.reshape(copies, batch_rows, columns)
    split = jnp.pad(split, ((0, 0), (0, share * groups - batch_rows), (0, 0)))
    split = split.reshape(copies, groups, share, columns).transpose(1, 0, 2, 3)
    split = split.reshape(devices, share * columns)
    figures = jnp.broadcast_to(stats[:4].reshape(1, 4 * queries), (devices, 4 * queries))
    payload = jnp.concatenate([split, figures], axis=1).reshape(devices, -1, 128)
    received = lax.all_to_all(payload, BOTH, 0, 0).reshape(devices, -1)
    sums = received[:, : share * columns].reshape(devices, share, columns).astype(F32)
    figures = received[:, share * columns :].reshape(devices, 4, queries).astype(F32)
    tops = figures[:, 0] + figures[:, 1]
    totals = figures[:, 2] + figures[:, 3]
    row_top = jnp.max(tops, axis=0)
    scale = jnp.exp(tops - row_top)
    row_total = jnp.sum(totals * scale, axis=0)
    factor = jnp.pad(
        (scale / row_total).reshape(devices, copies, batch_rows),
        ((0, 0), (0, 0), (0, share * groups - batch_rows)),
    ).reshape(devices, -1)
    own_factor = lax.dynamic_slice_in_dim(
        factor, (member * groups + group) * share, share, 1
    )
    own_expected = jnp.sum(sums * own_factor[:, :, None], axis=0)
    expected_tail = lax.all_to_all(
        jnp.broadcast_to(own_expected[None], (groups, share, columns)), "ent", 0, 0
    ).reshape(groups * share, columns)[:batch_rows]
    log_probs = scores - (row_top + jnp.log(row_total))[:, None]
    return (log_probs, expected_tail)


def solution(mesh):
    placed = (
        P(("ent", "rep"), None),
        P(),
        P(),
        P(),
        P(),
        P(),
        P(),
        P(("ent", "rep"), None),
        P(("ent", "rep"), None),
        P(("ent", "rep"), None),
        P("ent", None),
        P(),
        P(),
    )
    return jax.shard_map(
        body,
        mesh=mesh,
        in_specs=placed,
        out_specs=(P(None, ("ent", "rep")), P("rep", None)),
        check_vma=False,
    )
```

time: 131 us -> 131 us (level); the launches traced: 130 us -> 132 us
  starting transfers between devices: 25.4 us -> 37.9 us
  waiting for transfers between devices: 28.6 us -> 17.2 us
    all_to_all x1, waiting for transfers between devices: 8.19 us -> 0.01 us  [body(): lax.all_to_all(heads, BOTH, 0, 0, tiled=True)]
    all_to_all x1, starting transfers between devices: 5.84 us -> 12.1 us  [body(): lax.all_to_all(heads, BOTH, 0, 0, tiled=True)]
    all_to_all x1, waiting for transfers between devices: 6.12 us -> 0.01 us  [body(): lax.all_to_all(jnp.broadcast_to(own_heads[None], (devices, share, columns...]
    all_to_all x1, starting transfers between devices: 2.58 us -> 5.83 us  [body(): lax.all_to_all(jnp.broadcast_to(own_heads[None], (devices, share, columns...]
    all_to_all x1, starting transfers between devices: 2.58 us -> 5.59 us  [body(): received = lax.all_to_all(payload, BOTH, 0, 0).reshape(devices, -1)]
    all_to_all x1, waiting for transfers between devices: 0.01 us -> 2.96 us  [body(): table = lax.all_to_all(spread, BOTH, 0, 0).reshape(groups * slots, columns)]
    pallas_call x3 -> x5, Pallas kernels: 52.7 us -> 53.9 us  [the longest x2 24 us: near_call(): pl.pallas_call(functools.partial(near_kernel, part, ahead), out_shape=mix...]
  transfers between devices with their start and end apart: 6 -> 6, of which waited for: 4 -> 3; matrix products, arithmetic and copies ran while one was open for 6% -> 6% of each run, Pallas kernels for 22% -> 35%
where the time goes in v3:
time: 131 us; the launch traced here: 132 us
  Pallas kernels  60 us (46%)
  starting transfers between devices  37.9 us (29%)
  waiting for transfers between devices  17.2 us (13%)
  local copies, waits for them, and re-layouts  11.5 us (9%)
  other arithmetic  3.83 us (3%)
    pallas_call x2, Pallas kernels, near_call(): pl.pallas_call(functools.partial(near_kernel, part, ahead), out_shape=mix...  24 us
    pallas_call x2, Pallas kernels, far_call(): pl.pallas_call(functools.partial(far_kernel, half_rel, last), out_shape=h...  23.3 us
    all_to_all x1, starting transfers between devices, body(): lax.all_to_all(heads, BOTH, 0, 0, tiled=True)  12.1 us
    all_to_all x1, waiting for transfers between devices, body(): received = lax.all_to_all(payload, BOTH, 0, 0).reshape(devices, -1)  8.88 us
    all_to_all x1, starting transfers between devices, body(): table = lax.all_to_all(spread, BOTH, 0, 0).reshape(groups * slots, columns)  6.88 us
    pallas_call x1, Pallas kernels, near_call(): pl.pallas_call(functools.partial(near_kernel, part, ahead), out_shape=(mi...  6.6 us
    unnamed x23, local copies, waits for them, and re-layouts  6.15 us
    all_to_all x1, starting transfers between devices, body(): lax.all_to_all(jnp.broadcast_to(own_heads[None], (devices, share, columns...  5.83 us
  transfers between devices with their start and end apart: 6, of which 3 were waited for; matrix products, arithmetic and copies ran while one was open for 6% of the time, Pallas kernels for 35%

profile of v3, /device:TPU:0, one launch (start us, length us, event | category | flops | bytes accessed | tf_op | source)
XLA Modules:
  0.0 132.4 jit_solution(12784973428874886325)
XLA Ops:
  0.6 0.0 copy-start
  0.6 0.0 copy-start.5
  0.7 0.0 copy-start.1
  0.7 1.2 broadcast_subtract_fusion.2.index_ref
  1.9 2.3 %shard_map.141 = bf16[128,256]{1,0:T(8,128)(2,1)} custom-call(s32[1,128]{1,0:T(1,128)} %broadcast_subtract_fusion.2.index_ref, bf16[2304,256]{1,0:T(8,128)(2,1)} %emb_ref.5), custom_call_target="tpu_custom_call" | custom-call | tf_op jit(solution)/shard_map/pallas_call | solution.py:358
  4.2 4.2 %all-to-all-start = ((bf16[4,32,256]{2,1,0:T(8,128)(2,1)}), bf16[4,32,256]{2,1,0:T(8,128)(2,1)S(1)}, u32[]{:S(2)}, u32[]{:S(2)}) async-start(bf16[4,32,256]{2,1,0:T(8,128)(2,1)} %bitcast.51), calls=%async_computation | async-start | bytes 131072 | tf_op jit(solution)/shard_map/all_to_all | solution.py:363
  8.4 2.4 %copy.21 = bf16[2304,256]{0,1:T(8,128)(2,1)} copy(bf16[2304,256]{1,0:T(8,128)(2,1)} %emb_ref.5) | data formatting | bytes 2359296 | tf_op args[0]
  10.8 0.0 copy-done.5
  10.8 0.0 copy-done.1
  10.8 0.1 copy.22
  10.9 0.8 pad_bitcast_fusion.refs_5_.refs_4_
  11.7 1.1 gather_fusion
  12.9 0.9 fusion.rel_ref
  13.8 6.6 %shard_map.140 = (bf16[9,2,256,768]{3,2,1,0:T(8,128)(2,1)}, s32[20]{0:T(128)}) custom-call(s32[1]{0:T(128)} %bitcast.refs_0_, s32[256]{0:T(256)} %refs_1_.3, s32[18,768]{1,0:T(8,128)} %src_ref.3, s32[18,768]{1,0:T(8,128)} %rel_ref.3, bf16[256,2304]{1,0:T(8,128)(2,1)} %bitcast.38, bf16[256,512]{1,0:T(8,128)(2,1)} %pad_bitcast_fusion.refs_5_.refs_4_), custom_call_target="tpu_custom_call" | custom-call | flops 2214592512 | bytes 786432 | tf_op jit(solution)/shard_map/pallas_call | solution.py:254
  20.4 0.0 all-to-all-done
  20.4 0.9 broadcast_in_dim.53
  21.3 6.9 %all-to-all-start.1 = ((bf16[32,32,256]{2,1,0:T(8,128)(2,1)}), bf16[32,32,256]{2,1,0:T(8,128)(2,1)S(1)}, u32[]{:S(2)}, u32[]{:S(2)}) async-start(bf16[32,32,256]{2,1,0:T(8,128)(2,1)} %broadcast_in_dim.53), calls=%async_computation.1 | async-start | bytes 1048576 | tf_op jit(solution)/shard_map/all_to_all | solution.py:372
  28.2 0.6 broadcast_subtract_fusion.1
  28.8 12.0 %shard_map.142.mixed_ref.refs_5_ = bf16[9,2,256,768]{3,2,1,0:T(8,128)(2,1)} custom-call(s32[20]{0:T(128)} %get-tuple-element.15.refs_0_.order_ref, s32[18,768]{1,0:T(8,128)} %src_ref.3, s32[18,768]{1,0:T(8,128)} %rel_ref.3, bf16[256,2304]{1,0:T(8,128)(2,1)} %bitcast.39, ...), custom_call_target="tpu_custom_call", output_to_operand_aliasing={{}: (5, {})} | custom-call | flops 8858370048 | bytes 3145728 | tf_op jit(solution)/shard_map/pallas_call | solution.py:263
  40.8 3.0 %all-to-all-done.1 = bf16[32,32,256]{2,1,0:T(8,128)(2,1)S(1)} async-done(((bf16[32,32,256]{2,1,0:T(8,128)(2,1)}), bf16[32,32,256]{2,1,0:T(8,128)(2,1)S(1)}, u32[]{:S(2)}, u32[]{:S(2)}) %all-to-all-start.1) | async-done | bytes 524320 | tf_op jit(solution)/shard_map/all_to_all | solution.py:372
  43.7 0.8 copy-done.4
  44.5 7.3 %shard_map.143 = (bf16[2304,256]{1,0:T(8,128)(2,1)}, bf16[256,256]{1,0:T(8,128)(2,1)}) custom-call(s32[20]{0:T(128)} %get-tuple-element.15.refs_0_.order_ref, s32[18,768]{1,0:T(8,128)} %src_ref.3, s32[18,768]{1,0:T(8,128)} %dst_ref.3, s32[18,768]{1,0:T(8,128)} %rel_ref.3, bf16[2304,256]{1,0:T(8,128)(2,1)} %emb_ref.5, bf16[1,1024,256]{2,1,0:T(8,128)(2,1)} %bitcast.47, ...), custom_call_target="tpu_custom_call" | custom-call | flops 3623878656 | bytes 3538944 | tf_op jit(solution)/shard_map/pallas_call | solution.py:279
  51.8 12.1 %all-to-all-start.2 = ((bf16[32,8,256]{2,1,0:T(8,128)(2,1)}), bf16[32,8,256]{2,1,0:T(8,128)(2,1)S(1)}, u32[]{:S(2)}, u32[]{:S(2)}) async-start(bf16[32,8,256]{2,1,0:T(8,128)(2,1)} %bitcast.53), calls=%async_computation.2 | async-start | bytes 262144 | tf_op jit(solution)/shard_map/all_to_all | solution.py:388
  63.9 12.0 %shard_map.144.mixed_ref = bf16[9,2,256,768]{3,2,1,0:T(8,128)(2,1)} custom-call(s32[20]{0:T(128)} %get-tuple-element.15.refs_0_.order_ref, s32[18,768]{1,0:T(8,128)} %src_ref.3, s32[18,768]{1,0:T(8,128)} %rel_ref.3, bf16[256,2304]{1,0:T(8,128)(2,1)} %bitcast.40, bf16[256,512]{1,0:T(8,128)(2,1)} %pad_bitcast_fusion.refs_5_.refs_4_, ...), custom_call_target="tpu_custom_call", output_to_operand_aliasing={{}: (5, {})} | custom-call | flops 8858370048 | bytes 3145728 | tf_op jit(solution)/shard_map/pallas_call | solution.py:263
  75.9 0.0 all-to-all-done.2
  76.0 0.7 broadcast_in_dim.56
  76.6 5.8 %all-to-all-start.3 = ((bf16[32,8,256]{2,1,0:T(8,128)(2,1)}), bf16[32,8,256]{2,1,0:T(8,128)(2,1)S(1)}, u32[]{:S(2)}, u32[]{:S(2)}) async-start(bf16[32,8,256]{2,1,0:T(8,128)(2,1)} %broadcast_in_dim.56), calls=%async_computation.3 | async-start | bytes 262144 | tf_op jit(solution)/shard_map/all_to_all | solution.py:392
  82.5 16.0 %shard_map.145.hidden_ref = bf16[2304,256]{1,0:T(8,128)(2,1)} custom-call(s32[20]{0:T(128)} %get-tuple-element.15.refs_0_.order_ref, s32[18,768]{1,0:T(8,128)} %src_ref.3, s32[18,768]{1,0:T(8,128)} %dst_ref.3, s32[18,768]{1,0:T(8,128)} %rel_ref.3, bf16[2304,256]{1,0:T(8,128)(2,1)} %emb_ref.5, bf16[1,1024,256]{2,1,0:T(8,128)(2,1)} %bitcast.48, ...), custom_call_target="tpu_custom_call" | custom-call | flops 3623878656 | bytes 3538944 | tf_op jit(solution)/shard_map/pallas_call | solution.py:279
  98.5 0.0 all-to-all-done.3
  98.5 0.6 copy-done.3
  99.2 3.9 %shard_map.146 = (f32[256,2304]{1,0:T(8,128)}, bf16[256,256]{1,0:T(8,128)(2,1)}, bf16[16,256]{1,0:T(8,128)(2,1)}) custom-call(bf16[256,256]{1,0:T(8,128)(2,1)} %bitcast.46, f32[256,256]{1,0:T(8,128)} %fusion.rel_ref, bf16[2304,256]{1,0:T(8,128)(2,1)} %shard_map.145.hidden_ref), custom_call_target="tpu_custom_call" | custom-call | tf_op jit(solution)/shard_map/pallas_call | solution.py:402
  103.0 1.1 copy.23
  104.1 0.7 slice_bitcast_fusion
  104.9 0.7 copy.31
  105.6 5.6 %all-to-all-start.4 = ((bf16[32,24,128]{2,1,0:T(8,128)(2,1)}), bf16[32,24,128]{2,1,0:T(8,128)(2,1)S(1)}, u32[]{:S(2)}, u32[]{:S(2)}) async-start(bf16[32,24,128]{2,1,0:T(8,128)(2,1)} %bitcast.20), calls=%async_computation.4 | async-start | bytes 393216 | tf_op jit(solution)/shard_map/all_to_all | solution.py:418
  111.2 8.9 %all-to-all-done.4 = bf16[32,24,128]{2,1,0:T(8,128)(2,1)S(1)} async-done(((bf16[32,24,128]{2,1,0:T(8,128)(2,1)}), bf16[32,24,128]{2,1,0:T(8,128)(2,1)S(1)}, u32[]{:S(2)}, u32[]{:S(2)}) %all-to-all-start.4) | async-done | bytes 196640 | tf_op jit(solution)/shard_map/all_to_all | solution.py:418
  120.1 0.1 reshape.74
  120.2 0.1 slice_add_fusion
  120.4 0.1 dynamic-slice
  120.5 0.1 dynamic-slice_divide_fusion
  120.5 0.1 mul.39
  120.6 0.1 copy.33
  120.7 0.1 multiply_reduce_fusion
  120.8 0.6 broadcast_in_dim.63
  121.4 3.4 %all-to-all-start.5 = ((f32[8,8,256]{2,1,0:T(8,128)}), f32[8,8,256]{2,1,0:T(8,128)S(1)}, u32[]{:S(2)}, u32[]{:S(2)}) async-start(f32[8,8,256]{2,1,0:T(8,128)} %broadcast_in_dim.63), calls=%async_computation.5 | async-start | bytes 131072 | tf_op jit(solution)/shard_map/all_to_all | solution.py:434
  124.8 1.6 %broadcast_subtract_fusion = f32[256,2304]{1,0:T(8,128)} fusion(f32[256,2304]{1,0:T(8,128)S(1)} %copy-done.2, f32[256]{0:T(256)S(1)} %log_add_fusion), kind=kLoop, calls=%fused_computation.1 | loop fusion | flops 589824 | bytes 4719616 | tf_op jit(solution)/shard_map/sub | solution.py:437
  126.4 5.4 %all-to-all-done.5 = f32[8,8,256]{2,1,0:T(8,128)S(1)} async-done(((f32[8,8,256]{2,1,0:T(8,128)}), f32[8,8,256]{2,1,0:T(8,128)S(1)}, u32[]{:S(2)}, u32[]{:S(2)}) %all-to-all-start.5) | async-done | bytes 65568 | tf_op jit(solution)/shard_map/all_to_all | solution.py:434
  131.8 0.6 copy.52
  (22 shorter events, 0.3 us)
Async XLA Ops:
  0.6 12.2 %copy-start = (bf16[256,256]{1,0:T(8,128)(2,1)S(1)}, bf16[256,256]{1,0:T(8,128)(2,1)}, u32[]{:S(2)}) copy-start(bf16[256,256]{1,0:T(8,128)(2,1)} %param.18) | copy-start | bytes 393220
  0.6 10.1 %copy-start.5 = (s32[256]{0:T(256)S(1)}, s32[256]{0:T(256)}, u32[]{:S(2)}) copy-start(s32[256]{0:T(256)} %param.25) | copy-start | bytes 3076
  0.7 10.1 %copy-start.1 = (bf16[474,256]{1,0:T(8,128)(2,1)S(1)}, bf16[474,256]{1,0:T(8,128)(2,1)}, u32[]{:S(2)}) copy-start(bf16[474,256]{1,0:T(8,128)(2,1)} %param.14) | copy-start | bytes 728068
  4.2 16.2 %all-to-all-start = ((bf16[4,32,256]{2,1,0:T(8,128)(2,1)}), bf16[4,32,256]{2,1,0:T(8,128)(2,1)S(1)}, u32[]{:S(2)}, u32[]{:S(2)}) async-start(bf16[4,32,256]{2,1,0:T(8,128)(2,1)} %bitcast.51), calls=%async_computation | async-start | bytes 131072 | tf_op jit(solution)/shard_map/all_to_all | solution.py:363
  13.8 14.4 %copy-start.6 = (s32[256]{0:T(256)S(1)}, s32[256]{0:T(256)}, u32[]{:S(2)}) copy-start(s32[256]{0:T(256)} %refs_1_.3) | copy-start | bytes 3076
  21.3 22.4 %all-to-all-start.1 = ((bf16[32,32,256]{2,1,0:T(8,128)(2,1)}), bf16[32,32,256]{2,1,0:T(8,128)(2,1)S(1)}, u32[]{:S(2)}, u32[]{:S(2)}) async-start(bf16[32,32,256]{2,1,0:T(8,128)(2,1)} %broadcast_in_dim.53), calls=%async_computation.1 | async-start | bytes 1048576 | tf_op jit(solution)/shard_map/all_to_all | solution.py:372
  43.7 0.8 copy-start.4
  51.8 24.1 %all-to-all-start.2 = ((bf16[32,8,256]{2,1,0:T(8,128)(2,1)}), bf16[32,8,256]{2,1,0:T(8,128)(2,1)S(1)}, u32[]{:S(2)}, u32[]{:S(2)}) async-start(bf16[32,8,256]{2,1,0:T(8,128)(2,1)} %bitcast.53), calls=%async_computation.2 | async-start | bytes 262144 | tf_op jit(solution)/shard_map/all_to_all | solution.py:388
  76.6 21.9 %all-to-all-start.3 = ((bf16[32,8,256]{2,1,0:T(8,128)(2,1)}), bf16[32,8,256]{2,1,0:T(8,128)(2,1)S(1)}, u32[]{:S(2)}, u32[]{:S(2)}) async-start(bf16[32,8,256]{2,1,0:T(8,128)(2,1)} %broadcast_in_dim.56), calls=%async_computation.3 | async-start | bytes 262144 | tf_op jit(solution)/shard_map/all_to_all | solution.py:392
  98.5 0.7 copy-start.3
  103.0 21.8 %copy-start.2 = (f32[256,2304]{1,0:T(8,128)S(1)}, f32[256,2304]{1,0:T(8,128)}, u32[]{:S(2)}) copy-start(f32[256,2304]{1,0:T(8,128)} %get-tuple-element.25) | copy-start | bytes 7077892
  105.6 14.5 %all-to-all-start.4 = ((bf16[32,24,128]{2,1,0:T(8,128)(2,1)}), bf16[32,24,128]{2,1,0:T(8,128)(2,1)S(1)}, u32[]{:S(2)}, u32[]{:S(2)}) async-start(bf16[32,24,128]{2,1,0:T(8,128)(2,1)} %bitcast.20), calls=%async_computation.4 | async-start | bytes 393216 | tf_op jit(solution)/shard_map/all_to_all | solution.py:418
  121.4 10.4 %all-to-all-start.5 = ((f32[8,8,256]{2,1,0:T(8,128)}), f32[8,8,256]{2,1,0:T(8,128)S(1)}, u32[]{:S(2)}, u32[]{:S(2)}) async-start(f32[8,8,256]{2,1,0:T(8,128)} %broadcast_in_dim.63), calls=%async_computation.5 | async-start | bytes 131072 | tf_op jit(solution)/shard_map/all_to_all | solution.py:434

commit v4 on v3

--- a/solution.py
+++ b/solution.py
@@ -29,6 +29,10 @@
     return where.astype(F32).astype(BF16)
 
 
+def is_outside(src, rows_dev):
+    return jnp.where(src < rows_dev, 0.0, 1.0).astype(BF16)
+
+
 def order_blocks(head_ref, first_block, blocks, flag_ref, order_ref):
     def clear(b, carry):
         flag_ref[b] = 0
@@ -51,26 +55,24 @@
     order_ref[blocks] = found
 
 
-def head_steps(order_ref, blocks):
-    return (order_ref[blocks] + STEP - 1) // STEP
-
-
-def near_kernel(part, ahead, *refs):
-    if part == 0:
+def middle_step(order_ref, blocks, ahead):
+    return jnp.maximum((order_ref[blocks] + STEP - 1) // STEP, ahead)
+
+
+def near_kernel(rest, ahead, *refs):
+    if rest:
+        order_ref, src_ref, rel_ref, near_ref, relation_ref, _ = refs[:6]
+        mixed_ref, held_ref, sems = refs[6:]
+    else:
         base_ref, head_ref, src_ref, rel_ref, near_ref, relation_ref = refs[:6]
         mixed_ref, order_ref, held_ref, sems, flag_ref = refs[6:]
-    else:
-        order_ref, src_ref, rel_ref, near_ref, relation_ref, _ = refs[:6]
-        mixed_ref, held_ref, sems = refs[6:]
     blocks = src_ref.shape[0]
     rows_dev = near_ref.shape[1]
     steps = blocks // STEP
-    if part == 0:
+    if not rest:
         order_blocks(head_ref, base_ref[0], blocks, flag_ref, order_ref)
-        start, stop = 0, 1
-    else:
-        middle = jnp.maximum(head_steps(order_ref, blocks), ahead)
-        start, stop = (1, middle) if part == 1 else (middle, steps)
+    middle = middle_step(order_ref, blocks, ahead)
+    start, stop = (middle, steps) if rest else (0, middle)
     count = stop - start
 
     def save(step, slot):
@@ -93,22 +95,24 @@
                 one_hot(rel, relation_ref.shape[1]),
                 preferred_element_type=F32,
             )
-            mixed = jnp.where(src < rows_dev, gathered, 1.0) * relation
-            held_ref[slot, u] = mixed.astype(BF16)
+            is_far = is_outside(src, rows_dev)
+            held_ref[slot, u] = (gathered.astype(BF16) + is_far) * relation.astype(BF16)
         save(start + i, slot).start()
         return carry
 
     lax.fori_loop(0, count, one_step, 0)
     for back in (2, 1):
 
-        @pl.when(jnp.int32(count) >= back)
+        @pl.when(count >= back)
         def _():
-            save(start + count - back, lax.rem(jnp.int32(count) - back + 2, 2)).wait()
+            save(start + count - back, lax.rem(count - back, 2)).wait()
 
 
 def far_kernel(
     half_rel,
     last,
+    ahead,
+    base_ref,
     order_ref,
     src_ref,
     dst_ref,
@@ -119,16 +123,18 @@
     out_ref,
     loop_ref,
     loop_rel_ref,
-    extra_ref,
-    mixed_ref,
-    hidden_ref,
     *rest,
 ):
     far_t_ref, gathered_ref, agg_ref, held_ref, sems = rest[-5:]
+    if last:
+        before_ref, query_rel_ref, relation_ref, rel_weight_ref = rest[:4]
+        mixed_ref, hidden_ref, factor_ref = rest[4:7]
+    else:
+        head_ref, mixed_ref, hidden_ref, heads_ref = rest[:4]
     rows_dev = emb_ref.shape[0]
     blocks = src_ref.shape[0]
     far_chunks = far_ref.shape[0]
-    middle = head_steps(order_ref, blocks)
+    middle = middle_step(order_ref, blocks, ahead)
     start, stop = (middle, blocks // STEP) if last else (0, middle)
 
     def load(step, slot):
@@ -143,7 +149,7 @@
         return carry
 
     lax.fori_loop(0, far_chunks, turn, 0)
-    hidden_ref[...] = extra_ref[...] if last else jnp.zeros_like(hidden_ref)
+    hidden_ref[...] = before_ref[...] if last else jnp.zeros_like(hidden_ref)
 
     def look_up(src, u):
         if far_chunks == 1:
@@ -175,21 +181,18 @@
         srcs = [src_ref[row, :] for row in rows]
         found = [look_up(src, u) for u, src in enumerate(srcs)]
         composed = [
-            (jnp.where(srcs[u] < rows_dev, 1.0, found[u]) * held_ref[slot, u].astype(F32)).astype(
-                BF16
-            )
+            (found[u].astype(BF16) + (1 - is_outside(srcs[u], rows_dev))) * held_ref[slot, u]
             for u in range(STEP)
         ]
         for u, row in enumerate(rows):
             key = dst_ref[row, :] + jnp.where(rel_ref[row, :] >= half_rel, BLK, 0)
-            selector = (
-                lax.broadcasted_iota(jnp.int32, (2 * BLK, key.shape[1]), 0) == key
-            ).astype(F32)
-            counts = jnp.sum(selector, axis=1, keepdims=True)
-            sums = lax.dot_general(
-                selector.astype(BF16), composed[u], NT, preferred_element_type=F32
-            )
-            agg = (sums / jnp.maximum(counts, 1.0)).astype(BF16)
+            selector = one_hot(key, 2 * BLK)
+            counts = selector[:, :128]
+            for lane in range(128, selector.shape[1], 128):
+                counts = counts + selector[:, lane : lane + 128]
+            counts = jnp.sum(counts.astype(F32), axis=1, keepdims=True)
+            sums = lax.dot_general(selector, composed[u], NT, preferred_element_type=F32)
+            agg = (sums * (1.0 / jnp.maximum(counts, 1.0))).astype(BF16)
             here = pl.ds(pl.multiple_of(((start + i) * STEP + u) * BLK, BLK), BLK)
             agg_ref[0, here, :] = agg[:BLK]
             agg_ref[1, here, :] = agg[BLK:]
@@ -213,15 +216,23 @@
         return carry
 
     lax.fori_loop(start, stop, finish, 0)
-    if not last:
-        picks = one_hot_wide(extra_ref[...], rows_dev)
-        rest[0][...] = lax.dot_general(
+    if last:
+        picks = one_hot(query_rel_ref[...], relation_ref.shape[1])
+        rows = lax.dot_general(
+            picks, relation_ref[...], (((0,), (1,)), ((), ())), preferred_element_type=F32
+        )
+        factor_ref[...] = jnp.dot(
+            rows.astype(BF16), rel_weight_ref[...], preferred_element_type=F32
+        )
+    else:
+        picks = one_hot_wide(head_ref[...] - base_ref[0] * BLK, rows_dev)
+        heads_ref[...] = lax.dot_general(
             picks, hidden_ref[...], TN, preferred_element_type=F32
         ).astype(BF16)
 
 
-def pick_kernel(index_ref, emb_ref, offered_ref):
-    picks = one_hot_wide(index_ref[...], emb_ref.shape[0])
+def pick_kernel(base_ref, index_ref, emb_ref, offered_ref):
+    picks = one_hot(index_ref[...] - base_ref[0], emb_ref.shape[0])
     offered_ref[...] = lax.dot_general(
         picks, emb_ref[...], TN, preferred_element_type=F32
     ).astype(BF16)
@@ -232,11 +243,11 @@
 HBM = pl.BlockSpec(memory_space=pltpu.HBM)
 
 
-def near_call(part, ahead, src, rel, near, relation, more):
+def near_call(rest, ahead, src, rel, near, relation, more):
     columns, edges = near.shape[0], src.shape[1]
     blocks = src.shape[0]
     steps = blocks // STEP
-    count = STEP * (1, ahead - 1, steps - ahead)[part]
+    count = STEP * (steps - ahead if rest else ahead)
     flops = 2 * count * edges * columns * (near.shape[1] + relation.shape[1])
     mixed_type = jax.ShapeDtypeStruct((steps, STEP, columns, edges), BF16)
     order_type = jax.ShapeDtypeStruct((blocks + 2,), jnp.int32)
@@ -250,9 +261,9 @@
             flops=flops, bytes_accessed=2 * count * edges * columns, transcendentals=0
         ),
     )
-    if part == 0:
+    if not rest:
         return pl.pallas_call(
-            functools.partial(near_kernel, part, ahead),
+            functools.partial(near_kernel, rest, ahead),
             out_shape=(mixed_type, order_type),
             in_specs=[SMEM] * 2 + [WHOLE] * 4,
             out_specs=(HBM, SMEM),
@@ -261,7 +272,7 @@
         )(*more, src, rel, near, relation)
     mixed, order = more
     return pl.pallas_call(
-        functools.partial(near_kernel, part, ahead),
+        functools.partial(near_kernel, rest, ahead),
         out_shape=mixed_type,
         in_specs=[SMEM] + [WHOLE] * 4 + [HBM],
         out_specs=HBM,
@@ -271,16 +282,14 @@
     )(order, src, rel, near, relation, mixed)
 
 
-def far_call(half_rel, last, order, edges, emb, far, weights, extra, mixed, padded):
+def far_call(half_rel, last, ahead, scalars, edges, emb, far, weights, more, mixed, second):
     rows_dev, columns = emb.shape
     blocks, width = edges[0].shape
-    hidden_type = jax.ShapeDtypeStruct((rows_dev, columns), BF16)
-    heads_type = jax.ShapeDtypeStruct((padded, columns), BF16)
     return pl.pallas_call(
-        functools.partial(far_kernel, half_rel, last),
-        out_shape=hidden_type if last else (hidden_type, heads_type),
-        in_specs=[SMEM] + [WHOLE] * 10 + [HBM],
-        out_specs=WHOLE if last else (WHOLE, WHOLE),
+        functools.partial(far_kernel, half_rel, last, ahead),
+        out_shape=(jax.ShapeDtypeStruct((rows_dev, columns), BF16), second),
+        in_specs=[SMEM] * 2 + [WHOLE] * (9 + len(more)) + [HBM],
+        out_specs=(WHOLE, WHOLE),
         scratch_shapes=[
             pltpu.VMEM((far.shape[0], columns, CHUNK), BF16),
             pltpu.VMEM((STEP, columns, width if far.shape[0] > 1 else 128), F32),
@@ -294,7 +303,7 @@
             bytes_accessed=blocks * width * columns,
             transcendentals=0,
         ),
-    )(order, *edges, emb, far, *weights, extra, mixed)
+    )(*scalars, *edges, emb, far, *weights, *more, mixed)
 
 
 def score_kernel(heads_ref, rel_ref, hidden_ref, scores_ref, weighted_ref, stats_ref):
@@ -358,45 +367,62 @@
     offered = pl.pallas_call(
         pick_kernel,
         out_shape=jax.ShapeDtypeStruct((slots, columns), BF16),
+        in_specs=[SMEM, WHOLE, WHOLE],
+        out_specs=WHOLE,
         compiler_params=pltpu.CompilerParams(vmem_limit_bytes=VMEM_LIMIT),
-    )(export_rows - member * rows_dev, entity_emb)
+    )((member * rows_dev)[None], export_rows, entity_emb)
     pieces = lax.all_to_all(offered, "rep", 0, 0, tiled=True)
-    mixed, order = near_call(
-        0, ahead, edge_src, edge_rel, near_t, relation_t, ((device * blocks)[None], query_head)
-    )
     mine = jnp.sum(
         pieces.reshape(copies, slots // copies, columns).astype(F32), axis=0
     ).astype(BF16)
-    mine, mixed = lax.optimization_barrier((mine, mixed))
+    mine, near_t = lax.optimization_barrier((mine, near_t))
     spread = jnp.broadcast_to(mine[None], (devices,) + mine.shape)
     table = lax.all_to_all(spread, BOTH, 0, 0).reshape(groups * slots, columns)
-    mixed = near_call(1, ahead, edge_src, edge_rel, near_t, relation_t, (mixed, order))
+    base = (device * blocks)[None]
+    mixed, order = near_call(
+        False, ahead, edge_src, edge_rel, near_t, relation_t, (base, query_head)
+    )
     far_count = -(-(groups * slots) // CHUNK) * CHUNK
     far = jnp.pad(table, ((0, far_count - groups * slots), (0, 0)))
     far = far.reshape(far_count // CHUNK, CHUNK, columns)
 
-    local_head = jnp.pad(
-        query_head - device * rows_dev, (0, padded - queries), constant_values=-1
-    )[None]
+    heads_row = jnp.pad(query_head, (0, padded - queries), constant_values=-1)[None]
     weights = (in_weight, out_weight, loop_weight, loop_rel[None])
     edges = (edge_src, edge_dst, edge_rel)
     half_rel = relations // 2
     hidden, heads = far_call(
-        half_rel, False, order, edges, entity_emb, far, weights, local_head, mixed, padded
+        half_rel,
+        False,
+        ahead,
+        (base, order),
+        edges,
+        entity_emb,
+        far,
+        weights,
+        (heads_row,),
+        mixed,
+        jax.ShapeDtypeStruct((padded, columns), BF16),
     )
     heads, mixed = lax.optimization_barrier((heads, mixed))
     parts = lax.all_to_all(heads, BOTH, 0, 0, tiled=True).reshape(devices, share, columns)
-    mixed = near_call(2, ahead, edge_src, edge_rel, near_t, relation_t, (mixed, order))
+    mixed = near_call(True, ahead, edge_src, edge_rel, near_t, relation_t, (mixed, order))
     own_heads = jnp.sum(parts.astype(F32), axis=0).astype(BF16)
     own_heads, mixed = lax.optimization_barrier((own_heads, mixed))
     head_rows = lax.all_to_all(
         jnp.broadcast_to(own_heads[None], (devices, share, columns)), BOTH, 0, 0
     ).reshape(padded, columns)[:queries]
-    hidden = far_call(
-        half_rel, True, order, edges, entity_emb, far, weights, hidden, mixed, padded
-    )
-    query_factor = jnp.dot(
-        jnp.take(relation_emb, query_rel, axis=0), rel_weight, preferred_element_type=F32
+    hidden, query_factor = far_call(
+        half_rel,
+        True,
+        ahead,
+        (base, order),
+        edges,
+        entity_emb,
+        far,
+        weights,
+        (hidden, query_rel[None], relation_t, rel_weight),
+        mixed,
+        jax.ShapeDtypeStruct((queries, columns), F32),
     )
 
     scores, weighted, stats = pl.pallas_call(

time: 131 us -> 117 us (0.89); the launches traced: 132 us -> 116 us
  starting transfers between devices: 37.9 us -> 31.2 us
  Pallas kernels: 60 us -> 56.8 us
  waiting for transfers between devices: 17.2 us -> 15 us
  other arithmetic: 3.83 us -> 2.02 us
    all_to_all x1, starting transfers between devices: 12.1 us -> 5.84 us  [body(): lax.all_to_all(heads, BOTH, 0, 0, tiled=True)]
    pallas_call x5 -> x4, Pallas kernels: 53.9 us -> 50.6 us  [the longest x2 22.3 us: far_call(): pl.pallas_call(functools.partial(far_kernel, half_rel, last, ahead), out_...]
    all_to_all x1, waiting for transfers between devices: 2.96 us -> 0.01 us  [body(): table = lax.all_to_all(spread, BOTH, 0, 0).reshape(groups * slots, columns)]
    sub x2 -> x0, other arithmetic: 1.8 us -> none  [the longest x1 1.23 us: body(): export_rows - member * rows_dev]
    unnamed x23 -> x17, local copies, waits for them, and re-layouts: 6.15 us -> 6.2 us
  transfers between devices with their start and end apart: 6 -> 6, of which waited for: 3 -> 3; matrix products, arithmetic and copies ran while one was open for 6% -> 4% of each run, Pallas kernels for 35% -> 33%
where the time goes in v4:
time: 117 us; the launch traced here: 116 us
  Pallas kernels  56.8 us (49%)
  starting transfers between devices  31.2 us (27%)
  waiting for transfers between devices  15 us (13%)
  local copies, waits for them, and re-layouts  10.4 us (9%)
  other arithmetic  2.02 us (2%)
    pallas_call x2, Pallas kernels, far_call(): pl.pallas_call(functools.partial(far_kernel, half_rel, last, ahead), out_...  22.3 us
    pallas_call x1, Pallas kernels, near_call(): pl.pallas_call(functools.partial(near_kernel, rest, ahead), out_shape=(mi...  16.3 us
    pallas_call x1, Pallas kernels, near_call(): pl.pallas_call(functools.partial(near_kernel, rest, ahead), out_shape=mix...  12 us
    all_to_all x1, waiting for transfers between devices, body(): received = lax.all_to_all(payload, BOTH, 0, 0).reshape(devices, -1)  8.88 us
    unnamed x17, local copies, waits for them, and re-layouts  6.2 us
    all_to_all x1, starting transfers between devices, body(): table = lax.all_to_all(spread, BOTH, 0, 0).reshape(groups * slots, columns)  6.09 us
    all_to_all x1, starting transfers between devices, body(): lax.all_to_all(heads, BOTH, 0, 0, tiled=True)  5.84 us
    all_to_all x1, starting transfers between devices, body(): lax.all_to_all(jnp.broadcast_to(own_heads[None], (devices, share, columns...  5.83 us
  transfers between devices with their start and end apart: 6, of which 3 were waited for; matrix products, arithmetic and copies ran while one was open for 4% of the time, Pallas kernels for 33%

profile of v4, /device:TPU:0, one launch (start us, length us, event | category | flops | bytes accessed | tf_op | source)
XLA Modules:
  0.0 116.3 jit_solution(8303607186710962854)
XLA Ops:
  0.6 0.0 copy-start
  0.6 2.4 %shard_map.140 = bf16[128,256]{1,0:T(8,128)(2,1)} custom-call(s32[1]{0:T(128)} %bitcast.1.base_ref, s32[1,128]{1,0:T(1,128)} %index_ref.1, bf16[2304,256]{1,0:T(8,128)(2,1)} %emb_ref.5), custom_call_target="tpu_custom_call" | custom-call | tf_op jit(solution)/shard_map/pallas_call | solution.py:367
  3.0 4.2 %all-to-all-start = ((bf16[4,32,256]{2,1,0:T(8,128)(2,1)}), bf16[4,32,256]{2,1,0:T(8,128)(2,1)S(1)}, u32[]{:S(2)}, u32[]{:S(2)}) async-start(bf16[4,32,256]{2,1,0:T(8,128)(2,1)} %bitcast.51), calls=%async_computation | async-start | bytes 131072 | tf_op jit(solution)/shard_map/all_to_all | solution.py:374
  7.2 1.1 copy.21
  8.3 0.7 pad_bitcast_fusion.refs_5_.refs_4_.rest_2_
  9.1 0.0 copy-done
  9.1 1.5 %copy.20 = bf16[2304,256]{0,1:T(8,128)(2,1)} copy(bf16[2304,256]{1,0:T(8,128)(2,1)S(1)} %copy-done) | data formatting | bytes 2359296 | tf_op args[0]
  10.6 0.8 all-to-all-done
  11.4 0.8 broadcast_in_dim.48
  12.2 6.1 %all-to-all-start.1 = ((bf16[32,32,256]{2,1,0:T(8,128)(2,1)}), bf16[32,32,256]{2,1,0:T(8,128)(2,1)S(1)}, u32[]{:S(2)}, u32[]{:S(2)}) async-start(bf16[32,32,256]{2,1,0:T(8,128)(2,1)} %broadcast_in_dim.48), calls=%async_computation.1 | async-start | bytes 1048576 | tf_op jit(solution)/shard_map/all_to_all | solution.py:380
  18.3 16.3 %shard_map.141 = (bf16[9,2,256,768]{3,2,1,0:T(8,128)(2,1)}, s32[20]{0:T(128)}) custom-call(s32[1]{0:T(128)} %bitcast.refs_0_.base_ref, s32[256]{0:T(256)} %refs_1_.2, s32[18,768]{1,0:T(8,128)} %src_ref.3, s32[18,768]{1,0:T(8,128)} %rel_ref.3, bf16[256,2304]{1,0:T(8,128)(2,1)} %bitcast.39, bf16[256,512]{1,0:T(8,128)(2,1)} %pad_bitcast_fusion.refs_5_.refs_4_.rest_2_), custom_call_target="tpu_custom_call" | custom-call | flops 11072962560 | bytes 3932160 | tf_op jit(solution)/shard_map/pallas_call | solution.py:265
  34.6 0.0 all-to-all-done.1
  34.7 0.0 copy-start.3
  34.7 0.8 copy-done.3
  35.4 11.6 %shard_map.142 = (bf16[2304,256]{1,0:T(8,128)(2,1)}, bf16[256,256]{1,0:T(8,128)(2,1)}) custom-call(s32[1]{0:T(128)} %bitcast.refs_0_.base_ref, s32[20]{0:T(128)} %get-tuple-element.18.order_ref.refs_0_, s32[18,768]{1,0:T(8,128)} %src_ref.3, s32[18,768]{1,0:T(8,128)} %dst_ref.3, s32[18,768]{1,0:T(8,128)} %rel_ref.3, bf16[2304,256]{1,0:T(8,128)(2,1)} %emb_ref.5, ...), custom_call_target="tpu_custom_call" | custom-call | flops 3623878656 | bytes 3538944 | tf_op jit(solution)/shard_map/pallas_call | solution.py:288
  47.1 5.8 %all-to-all-start.2 = ((bf16[32,8,256]{2,1,0:T(8,128)(2,1)}), bf16[32,8,256]{2,1,0:T(8,128)(2,1)S(1)}, u32[]{:S(2)}, u32[]{:S(2)}) async-start(bf16[32,8,256]{2,1,0:T(8,128)(2,1)} %bitcast.53), calls=%async_computation.2 | async-start | bytes 262144 | tf_op jit(solution)/shard_map/all_to_all | solution.py:407
  52.9 12.0 %shard_map.143.rest_4_ = bf16[9,2,256,768]{3,2,1,0:T(8,128)(2,1)} custom-call(s32[20]{0:T(128)} %get-tuple-element.18.order_ref.refs_0_, s32[18,768]{1,0:T(8,128)} %src_ref.3, s32[18,768]{1,0:T(8,128)} %rel_ref.3, bf16[256,2304]{1,0:T(8,128)(2,1)} %bitcast.40, ...), custom_call_target="tpu_custom_call", output_to_operand_aliasing={{}: (5, {})} | custom-call | flops 8858370048 | bytes 3145728 | tf_op jit(solution)/shard_map/pallas_call | solution.py:274
  65.0 0.0 all-to-all-done.2
  65.0 0.7 broadcast_in_dim.51
  65.7 5.8 %all-to-all-start.3 = ((bf16[32,8,256]{2,1,0:T(8,128)(2,1)}), bf16[32,8,256]{2,1,0:T(8,128)(2,1)S(1)}, u32[]{:S(2)}, u32[]{:S(2)}) async-start(bf16[32,8,256]{2,1,0:T(8,128)(2,1)} %broadcast_in_dim.51), calls=%async_computation.3 | async-start | bytes 262144 | tf_op jit(solution)/shard_map/all_to_all | solution.py:411
  71.5 10.6 %shard_map.144 = (bf16[2304,256]{1,0:T(8,128)(2,1)}, f32[256,256]{1,0:T(8,128)}) custom-call(s32[1]{0:T(128)} %bitcast.refs_0_.base_ref, s32[20]{0:T(128)} %get-tuple-element.18.order_ref.refs_0_, s32[18,768]{1,0:T(8,128)} %src_ref.3, s32[18,768]{1,0:T(8,128)} %dst_ref.3, s32[18,768]{1,0:T(8,128)} %rel_ref.3, bf16[2304,256]{1,0:T(8,128)(2,1)} %emb_ref.5, ...), custom_call_target="tpu_custom_call" | custom-call | flops 3623878656 | bytes 3538944 | tf_op jit(solution)/shard_map/pallas_call | solution.py:288
  82.1 0.0 all-to-all-done.3
  82.2 0.0 copy-start.2
  82.2 0.6 copy-done.2
  82.8 3.8 %shard_map.145 = (f32[256,2304]{1,0:T(8,128)}, bf16[256,256]{1,0:T(8,128)(2,1)}, bf16[16,256]{1,0:T(8,128)(2,1)}) custom-call(bf16[256,256]{1,0:T(8,128)(2,1)} %bitcast.46, f32[256,256]{1,0:T(8,128)} %get-tuple-element.27.rel_ref, bf16[2304,256]{1,0:T(8,128)(2,1)} %get-tuple-element.28.hidden_ref), custom_call_target="tpu_custom_call" | custom-call | tf_op jit(solution)/shard_map/pallas_call | solution.py:428
  86.6 0.0 copy-start.1
  86.6 1.1 copy.22
  87.7 0.7 slice_bitcast_fusion
  88.5 0.7 copy.30
  89.2 5.8 %all-to-all-start.4 = ((bf16[32,24,128]{2,1,0:T(8,128)(2,1)}), bf16[32,24,128]{2,1,0:T(8,128)(2,1)S(1)}, u32[]{:S(2)}, u32[]{:S(2)}) async-start(bf16[32,24,128]{2,1,0:T(8,128)(2,1)} %bitcast.22), calls=%async_computation.4 | async-start | bytes 393216 | tf_op jit(solution)/shard_map/all_to_all | solution.py:444
  95.0 8.9 %all-to-all-done.4 = bf16[32,24,128]{2,1,0:T(8,128)(2,1)S(1)} async-done(((bf16[32,24,128]{2,1,0:T(8,128)(2,1)}), bf16[32,24,128]{2,1,0:T(8,128)(2,1)S(1)}, u32[]{:S(2)}, u32[]{:S(2)}) %all-to-all-start.4) | async-done | bytes 196640 | tf_op jit(solution)/shard_map/all_to_all | solution.py:444
  104.0 0.1 reshape.69
  104.0 0.1 slice_add_fusion
  104.2 0.1 dynamic-slice
  104.3 0.1 dynamic-slice_divide_fusion
  104.4 0.1 mul.35
  104.5 0.1 copy.32
  104.6 0.1 multiply_reduce_fusion
  104.6 0.6 broadcast_in_dim.56
  105.3 3.4 %all-to-all-start.5 = ((f32[8,8,256]{2,1,0:T(8,128)}), f32[8,8,256]{2,1,0:T(8,128)S(1)}, u32[]{:S(2)}, u32[]{:S(2)}) async-start(f32[8,8,256]{2,1,0:T(8,128)} %broadcast_in_dim.56), calls=%async_computation.5 | async-start | bytes 131072 | tf_op jit(solution)/shard_map/all_to_all | solution.py:460
  108.6 0.0 copy-done.1
  108.6 1.6 %broadcast_subtract_fusion = f32[256,2304]{1,0:T(8,128)} fusion(f32[256,2304]{1,0:T(8,128)S(1)} %copy-done.1, f32[256]{0:T(256)S(1)} %log_add_fusion), kind=kLoop, calls=%fused_computation | loop fusion | flops 589824 | bytes 4719616 | tf_op jit(solution)/shard_map/sub | solution.py:463
  110.3 5.4 %all-to-all-done.5 = f32[8,8,256]{2,1,0:T(8,128)S(1)} async-done(((f32[8,8,256]{2,1,0:T(8,128)}), f32[8,8,256]{2,1,0:T(8,128)S(1)}, u32[]{:S(2)}, u32[]{:S(2)}) %all-to-all-start.5) | async-done | bytes 65568 | tf_op jit(solution)/shard_map/all_to_all | solution.py:460
  115.6 0.6 copy.50
  (12 shorter events, 0.2 us)
Async XLA Ops:
  0.6 8.4 %copy-start = (bf16[2304,256]{1,0:T(8,128)(2,1)S(1)}, bf16[2304,256]{1,0:T(8,128)(2,1)}, u32[]{:S(2)}) copy-start(bf16[2304,256]{1,0:T(8,128)(2,1)} %emb_ref.5) | copy-start | bytes 3538948
  3.0 8.3 %all-to-all-start = ((bf16[4,32,256]{2,1,0:T(8,128)(2,1)}), bf16[4,32,256]{2,1,0:T(8,128)(2,1)S(1)}, u32[]{:S(2)}, u32[]{:S(2)}) async-start(bf16[4,32,256]{2,1,0:T(8,128)(2,1)} %bitcast.51), calls=%async_computation | async-start | bytes 131072 | tf_op jit(solution)/shard_map/all_to_all | solution.py:374
  12.2 22.4 %all-to-all-start.1 = ((bf16[32,32,256]{2,1,0:T(8,128)(2,1)}), bf16[32,32,256]{2,1,0:T(8,128)(2,1)S(1)}, u32[]{:S(2)}, u32[]{:S(2)}) async-start(bf16[32,32,256]{2,1,0:T(8,128)(2,1)} %broadcast_in_dim.48), calls=%async_computation.1 | async-start | bytes 1048576 | tf_op jit(solution)/shard_map/all_to_all | solution.py:380
  34.7 0.8 copy-start.3
  47.1 17.9 %all-to-all-start.2 = ((bf16[32,8,256]{2,1,0:T(8,128)(2,1)}), bf16[32,8,256]{2,1,0:T(8,128)(2,1)S(1)}, u32[]{:S(2)}, u32[]{:S(2)}) async-start(bf16[32,8,256]{2,1,0:T(8,128)(2,1)} %bitcast.53), calls=%async_computation.2 | async-start | bytes 262144 | tf_op jit(solution)/shard_map/all_to_all | solution.py:407
  65.7 16.5 %all-to-all-start.3 = ((bf16[32,8,256]{2,1,0:T(8,128)(2,1)}), bf16[32,8,256]{2,1,0:T(8,128)(2,1)S(1)}, u32[]{:S(2)}, u32[]{:S(2)}) async-start(bf16[32,8,256]{2,1,0:T(8,128)(2,1)} %broadcast_in_dim.51), calls=%async_computation.3 | async-start | bytes 262144 | tf_op jit(solution)/shard_map/all_to_all | solution.py:411
  82.2 0.6 copy-start.2
  86.6 22.0 %copy-start.1 = (f32[256,2304]{1,0:T(8,128)S(1)}, f32[256,2304]{1,0:T(8,128)}, u32[]{:S(2)}) copy-start(f32[256,2304]{1,0:T(8,128)} %get-tuple-element.29) | copy-start | bytes 7077892
  89.2 14.7 %all-to-all-start.4 = ((bf16[32,24,128]{2,1,0:T(8,128)(2,1)}), bf16[32,24,128]{2,1,0:T(8,128)(2,1)S(1)}, u32[]{:S(2)}, u32[]{:S(2)}) async-start(bf16[32,24,128]{2,1,0:T(8,128)(2,1)} %bitcast.22), calls=%async_computation.4 | async-start | bytes 393216 | tf_op jit(solution)/shard_map/all_to_all | solution.py:444
  105.3 10.4 %all-to-all-start.5 = ((f32[8,8,256]{2,1,0:T(8,128)}), f32[8,8,256]{2,1,0:T(8,128)S(1)}, u32[]{:S(2)}, u32[]{:S(2)}) async-start(f32[8,8,256]{2,1,0:T(8,128)} %broadcast_in_dim.56), calls=%async_computation.5 | async-start | bytes 131072 | tf_op jit(solution)/shard_map/all_to_all | solution.py:460

commit v5 on v4

--- a/solution.py
+++ b/solution.py
@@ -16,7 +16,8 @@
 TN = (((0,), (0,)), ((), ()))
 VMEM_LIMIT = 56 * 2**20
 STEP = 2
-AHEAD = 5
+AHEAD = 6
+SCORE_LIMIT = 24 * 2**20
 
 
 def one_hot(index, rows):
@@ -33,25 +34,21 @@
     return jnp.where(src < rows_dev, 0.0, 1.0).astype(BF16)
 
 
-def order_blocks(head_ref, first_block, blocks, flag_ref, order_ref):
-    def clear(b, carry):
-        flag_ref[b] = 0
-        return carry
-
-    def mark(q, carry):
+def order_blocks(head_ref, first_block, blocks, order_ref):
+    def mark(q, marks):
         block = lax.shift_right_arithmetic(head_ref[q], BLK.bit_length() - 1) - first_block
-        flag_ref[jnp.where((block >= 0) & (block < blocks), block, blocks)] = 1
-        return carry
-
-    def place(wanted, b, position):
-        taken = flag_ref[b] == wanted
-        order_ref[jnp.where(taken, position, blocks + 1)] = b
-        return position + taken.astype(jnp.int32)
-
-    lax.fori_loop(0, blocks, clear, 0)
-    lax.fori_loop(0, head_ref.shape[0], mark, 0, unroll=8)
-    found = lax.fori_loop(0, blocks, functools.partial(place, 1), 0)
-    lax.fori_loop(0, blocks, functools.partial(place, 0), found)
+        inside = (block >= 0) & (block < blocks)
+        return marks | jnp.where(inside, lax.shift_left(1, jnp.where(inside, block, 0)), 0)
+
+    marks = lax.fori_loop(0, head_ref.shape[0], mark, jnp.int32(0), unroll=16)
+    position = jnp.int32(0)
+    for wanted in (1, 0):
+        for b in range(blocks):
+            taken = (lax.shift_right_logical(marks, b) & 1) == wanted
+            order_ref[jnp.where(taken, position, blocks + 1)] = jnp.int32(b)
+            position = position + taken.astype(jnp.int32)
+        if wanted:
+            found = position
     order_ref[blocks] = found
 
 
@@ -65,12 +62,12 @@
         mixed_ref, held_ref, sems = refs[6:]
     else:
         base_ref, head_ref, src_ref, rel_ref, near_ref, relation_ref = refs[:6]
-        mixed_ref, order_ref, held_ref, sems, flag_ref = refs[6:]
+        mixed_ref, order_ref, held_ref, sems = refs[6:]
     blocks = src_ref.shape[0]
     rows_dev = near_ref.shape[1]
     steps = blocks // STEP
     if not rest:
-        order_blocks(head_ref, base_ref[0], blocks, flag_ref, order_ref)
+        order_blocks(head_ref, base_ref[0], blocks, order_ref)
     middle = middle_step(order_ref, blocks, ahead)
     start, stop = (middle, steps) if rest else (0, middle)
     count = stop - start
@@ -125,14 +122,14 @@
     loop_rel_ref,
     *rest,
 ):
-    far_t_ref, gathered_ref, agg_ref, held_ref, sems = rest[-5:]
+    far_t_ref, gathered_ref, agg_ref, held_ref, own_ref, made_ref, sems, own_sems, out_sems = rest[-9:]
     if last:
-        before_ref, query_rel_ref, relation_ref, rel_weight_ref = rest[:4]
-        mixed_ref, hidden_ref, factor_ref = rest[4:7]
+        query_rel_ref, relation_ref, rel_weight_ref, mixed_ref, _ = rest[:5]
+        hidden_ref, factor_ref = rest[5:7]
     else:
         head_ref, mixed_ref, hidden_ref, heads_ref = rest[:4]
-    rows_dev = emb_ref.shape[0]
     blocks = src_ref.shape[0]
+    rows_dev = blocks * BLK
     far_chunks = far_ref.shape[0]
     middle = middle_step(order_ref, blocks, ahead)
     start, stop = (middle, blocks // STEP) if last else (0, middle)
@@ -140,6 +137,21 @@
     def load(step, slot):
         return pltpu.make_async_copy(mixed_ref.at[step], held_ref.at[slot], sems.at[slot])
 
+    def block_rows(step, u):
+        return pl.ds(pl.multiple_of(order_ref[step * STEP + u] * BLK, BLK), BLK)
+
+    def load_own(step, u):
+        slot = lax.rem(step, 2)
+        return pltpu.make_async_copy(
+            emb_ref.at[block_rows(step, u)], own_ref.at[slot, u], own_sems.at[slot, u]
+        )
+
+    def give(step, u):
+        rows = block_rows(step, u)
+        return pltpu.make_async_copy(
+            made_ref.at[rows], hidden_ref.at[rows], out_sems.at[step * STEP + u]
+        )
+
     @pl.when(start < stop)
     def _():
         load(start, 0).start()
@@ -149,7 +161,8 @@
         return carry
 
     lax.fori_loop(0, far_chunks, turn, 0)
-    hidden_ref[...] = before_ref[...] if last else jnp.zeros_like(hidden_ref)
+    if not last:
+        made_ref[...] = jnp.zeros_like(made_ref)
 
     def look_up(src, u):
         if far_chunks == 1:
@@ -169,14 +182,35 @@
         lax.fori_loop(0, far_chunks, one_chunk, 0)
         return gathered_ref[u]
 
+    def finish(step, slot):
+        own = own_ref[slot].reshape(STEP * BLK, own_ref.shape[-1])
+        own = (own.astype(F32) * loop_rel_ref[...]).astype(BF16)
+        preact = jnp.dot(agg_ref[0, slot], in_ref[...], preferred_element_type=F32)
+        preact += jnp.dot(agg_ref[1, slot], out_ref[...], preferred_element_type=F32)
+        preact += jnp.dot(own, loop_ref[...], preferred_element_type=F32)
+        hidden = jnp.tanh(preact).astype(BF16)
+        for u in range(STEP):
+            made_ref[block_rows(step, u), :] = hidden[u * BLK : (u + 1) * BLK]
+
     def one_step(i, carry):
         slot = lax.rem(i, 2)
+        step = start + i
+        before = jnp.maximum(step - 1, start)
+
+        @pl.when(i > 0)
+        def _():
+            for u in range(STEP):
+                load_own(before, u).wait()
+
+        for u in range(STEP):
+            load_own(step, u).start()
 
         @pl.when(start + i + 1 < stop)
         def _():
             load(start + i + 1, 1 - slot).start()
 
         load(start + i, slot).wait()
+        finish(before, lax.rem(step + 1, 2))
         rows = [pl.ds(order_ref[(start + i) * STEP + u], 1) for u in range(STEP)]
         srcs = [src_ref[row, :] for row in rows]
         found = [look_up(src, u) for u, src in enumerate(srcs)]
@@ -193,29 +227,27 @@
             counts = jnp.sum(counts.astype(F32), axis=1, keepdims=True)
             sums = lax.dot_general(selector, composed[u], NT, preferred_element_type=F32)
             agg = (sums * (1.0 / jnp.maximum(counts, 1.0))).astype(BF16)
-            here = pl.ds(pl.multiple_of(((start + i) * STEP + u) * BLK, BLK), BLK)
-            agg_ref[0, here, :] = agg[:BLK]
-            agg_ref[1, here, :] = agg[BLK:]
+            here = pl.ds(u * BLK, BLK)
+            agg_ref[0, lax.rem(step, 2), here, :] = agg[:BLK]
+            agg_ref[1, lax.rem(step, 2), here, :] = agg[BLK:]
+
+        @pl.when(i > 0)
+        def _():
+            for u in range(STEP):
+                give(before, u).start()
+
         return carry
 
     lax.fori_loop(0, stop - start, one_step, 0)
 
-    def finish(i, carry):
-        here = pl.ds(pl.multiple_of(i * STEP * BLK, STEP * BLK), STEP * BLK)
-        rows = [
-            pl.ds(pl.multiple_of(order_ref[i * STEP + u] * BLK, BLK), BLK) for u in range(STEP)
-        ]
-        own = jnp.concatenate([emb_ref[row, :] for row in rows], axis=0)
-        own = (own.astype(F32) * loop_rel_ref[...]).astype(BF16)
-        preact = jnp.dot(agg_ref[0, here, :], in_ref[...], preferred_element_type=F32)
-        preact += jnp.dot(agg_ref[1, here, :], out_ref[...], preferred_element_type=F32)
-        preact += jnp.dot(own, loop_ref[...], preferred_element_type=F32)
-        hidden = jnp.tanh(preact).astype(BF16)
-        for u, row in enumerate(rows):
-            hidden_ref[row, :] = hidden[u * BLK : (u + 1) * BLK]
-        return carry
-
-    lax.fori_loop(start, stop, finish, 0)
+    @pl.when(start < stop)
+    def _():
+        for u in range(STEP):
+            load_own(stop - 1, u).wait()
+        finish(stop - 1, lax.rem(stop - 1, 2))
+        for u in range(STEP):
+            give(stop - 1, u).start()
+
     if last:
         picks = one_hot(query_rel_ref[...], relation_ref.shape[1])
         rows = lax.dot_general(
@@ -227,8 +259,15 @@
     else:
         picks = one_hot_wide(head_ref[...] - base_ref[0] * BLK, rows_dev)
         heads_ref[...] = lax.dot_general(
-            picks, hidden_ref[...], TN, preferred_element_type=F32
+            picks, made_ref[...], TN, preferred_element_type=F32
         ).astype(BF16)
+
+    def gave(step, carry):
+        for u in range(STEP):
+            give(step, u).wait()
+        return carry
+
+    lax.fori_loop(start, stop, gave, 0)
 
 
 def pick_kernel(base_ref, index_ref, emb_ref, offered_ref):
@@ -267,7 +306,7 @@
             out_shape=(mixed_type, order_type),
             in_specs=[SMEM] * 2 + [WHOLE] * 4,
             out_specs=(HBM, SMEM),
-            scratch_shapes=scratch + [pltpu.SMEM((blocks + 1,), jnp.int32)],
+            scratch_shapes=scratch,
             **settings,
         )(*more, src, rel, near, relation)
     mixed, order = more
@@ -282,20 +321,25 @@
     )(order, src, rel, near, relation, mixed)
 
 
-def far_call(half_rel, last, ahead, scalars, edges, emb, far, weights, more, mixed, second):
+def far_call(half_rel, last, ahead, scalars, edges, emb, far, weights, more, kept, second):
     rows_dev, columns = emb.shape
     blocks, width = edges[0].shape
     return pl.pallas_call(
         functools.partial(far_kernel, half_rel, last, ahead),
         out_shape=(jax.ShapeDtypeStruct((rows_dev, columns), BF16), second),
-        in_specs=[SMEM] * 2 + [WHOLE] * (9 + len(more)) + [HBM],
-        out_specs=(WHOLE, WHOLE),
+        in_specs=[SMEM] * 2 + [WHOLE] * 3 + [HBM] + [WHOLE] * (5 + len(more)) + [HBM] * (2 if last else 1),
+        out_specs=(HBM, WHOLE),
+        input_output_aliases={12 + len(more): 0} if last else {},
         scratch_shapes=[
             pltpu.VMEM((far.shape[0], columns, CHUNK), BF16),
             pltpu.VMEM((STEP, columns, width if far.shape[0] > 1 else 128), F32),
-            pltpu.VMEM((2, rows_dev, columns), BF16),
+            pltpu.VMEM((2, 2, STEP * BLK, columns), BF16),
             pltpu.VMEM((2, STEP, columns, width), BF16),
+            pltpu.VMEM((2, STEP, BLK, columns), BF16),
+            pltpu.VMEM((rows_dev, columns), BF16),
             pltpu.SemaphoreType.DMA((2,)),
+            pltpu.SemaphoreType.DMA((2, STEP)),
+            pltpu.SemaphoreType.DMA((blocks,)),
         ],
         compiler_params=pltpu.CompilerParams(vmem_limit_bytes=VMEM_LIMIT),
         cost_estimate=pl.CostEstimate(
@@ -303,30 +347,43 @@
             bytes_accessed=blocks * width * columns,
             transcendentals=0,
         ),
-    )(*scalars, *edges, emb, far, *weights, *more, mixed)
-
-
-def score_kernel(heads_ref, rel_ref, hidden_ref, scores_ref, weighted_ref, stats_ref):
+    )(*scalars, *edges, emb, far, *weights, *more, *kept)
+
+
+def score_kernel(packed, groups, heads_ref, rel_ref, hidden_ref, scores_ref, *outs):
     query = (heads_ref[...].astype(F32) * rel_ref[...]).astype(BF16)
     scores = lax.dot_general(query, hidden_ref[...], NT, preferred_element_type=F32)
     scores_ref[...] = scores
     top = jnp.max(scores, axis=1, keepdims=True)
-    high = top.astype(BF16)
-    low = (top - high.astype(F32)).astype(BF16)
-    top = high.astype(F32) + low.astype(F32)
+    high = top.astype(BF16).astype(F32)
+    low = (top - high).astype(BF16).astype(F32)
+    top = high + low
     weights = jnp.exp(scores - top)
     total = jnp.sum(weights, axis=1, keepdims=True)
-    weighted_ref[...] = jnp.dot(
-        weights.astype(BF16), hidden_ref[...], preferred_element_type=F32
-    ).astype(BF16)
-    total_high = total.astype(BF16)
-    total_low = (total - total_high.astype(F32)).astype(BF16)
-    lanes = lax.broadcasted_iota(jnp.int32, (query.shape[0], 128), 1)
-    wide = jnp.where(lanes == 0, high.astype(F32), 0.0)
-    wide = jnp.where(lanes == 1, low.astype(F32), wide)
-    wide = jnp.where(lanes == 2, total_high.astype(F32), wide)
-    wide = jnp.where(lanes == 3, total_low.astype(F32), wide)
-    stats_ref[...] = jnp.transpose(wide)[: stats_ref.shape[0]].astype(BF16)
+    weighted = jnp.dot(weights.astype(BF16), hidden_ref[...], preferred_element_type=F32)
+    total_high = total.astype(BF16).astype(F32)
+    lanes = lax.broadcasted_iota(jnp.int32, (query.shape[0], 128), 1) % 4
+    wide = jnp.where(lanes == 0, high, total - total_high)
+    wide = jnp.where(lanes == 1, low, wide)
+    wide = jnp.where(lanes == 2, total_high, wide)
+    stats = jnp.transpose(wide)
+    if not packed:
+        weighted_ref, stats_ref = outs
+        weighted_ref[...] = weighted.astype(BF16)
+        stats_ref[...] = stats[: stats_ref.shape[0]].astype(BF16)
+        return
+    (payload_ref,) = outs
+    upper = lax.broadcasted_iota(jnp.int32, (8, 128), 0) < 4
+    figures = jnp.where(upper, stats[:8, :128], stats[:8, 128:])
+    devices = payload_ref.shape[0]
+    copies = devices // groups
+    share = query.shape[0] // devices
+    for device in range(devices):
+        first = (device % copies * groups + device // copies) * share
+        rows = weighted[first : first + share]
+        payload_ref[device] = jnp.concatenate(
+            [rows[:, :128], rows[:, 128:], figures], axis=0
+        ).astype(BF16)
 
 
 def body(
@@ -400,7 +457,7 @@
         far,
         weights,
         (heads_row,),
-        mixed,
+        (mixed,),
         jax.ShapeDtypeStruct((padded, columns), BF16),
     )
     heads, mixed = lax.optimization_barrier((heads, mixed))
@@ -420,30 +477,40 @@
         entity_emb,
         far,
         weights,
-        (hidden, query_rel[None], relation_t, rel_weight),
-        mixed,
+        (query_rel[None], relation_t, rel_weight),
+        (mixed, hidden),
         jax.ShapeDtypeStruct((queries, columns), F32),
     )
 
-    scores, weighted, stats = pl.pallas_call(
-        score_kernel,
-        out_shape=(
-            jax.ShapeDtypeStruct((queries, rows_dev), F32),
+    packed = share == 8 and share * devices == queries and (queries, columns) == (256, 256)
+    score_type = jax.ShapeDtypeStruct((queries, rows_dev), F32)
+    if packed:
+        more = (jax.ShapeDtypeStruct((devices, 24, 128), BF16),)
+    else:
+        more = (
             jax.ShapeDtypeStruct((queries, columns), BF16),
             jax.ShapeDtypeStruct((16, queries), BF16),
-        ),
-        compiler_params=pltpu.CompilerParams(vmem_limit_bytes=VMEM_LIMIT),
+        )
+    scores, *parts = pl.pallas_call(
+        functools.partial(score_kernel, packed, groups),
+        out_shape=(score_type,) + more,
+        compiler_params=pltpu.CompilerParams(vmem_limit_bytes=SCORE_LIMIT),
     )(head_rows, query_factor, hidden)
-
-    split = weighted.reshape(copies, batch_rows, columns)
-    split = jnp.pad(split, ((0, 0), (0, share * groups - batch_rows), (0, 0)))
-    split = split.reshape(copies, groups, share, columns).transpose(1, 0, 2, 3)
-    split = split.reshape(devices, share * columns)
-    figures = jnp.broadcast_to(stats[:4].reshape(1, 4 * queries), (devices, 4 * queries))
-    payload = jnp.concatenate([split, figures], axis=1).reshape(devices, -1, 128)
-    received = lax.all_to_all(payload, BOTH, 0, 0).reshape(devices, -1)
-    sums = received[:, : share * columns].reshape(devices, share, columns).astype(F32)
-    figures = received[:, share * columns :].reshape(devices, 4, queries).astype(F32)
+    if packed:
+        received = lax.all_to_all(parts[0], BOTH, 0, 0).astype(F32)
+        sums = jnp.concatenate([received[:, :8], received[:, 8:16]], axis=2)
+        figures = jnp.concatenate([received[:, 16:20], received[:, 20:24]], axis=2)
+    else:
+        split = parts[0].reshape(copies, batch_rows, columns)
+        split = jnp.pad(split, ((0, 0), (0, share * groups - batch_rows), (0, 0)))
+        split = split.reshape(copies, groups, share, columns).transpose(1, 0, 2, 3)
+        split = split.reshape(devices, share * columns)
+        figures = parts[1][:4].reshape(1, 4 * queries)
+        figures = jnp.broadcast_to(figures, (devices, 4 * queries))
+        payload = jnp.concatenate([split, figures], axis=1).reshape(devices, -1, 128)
+        received = lax.all_to_all(payload, BOTH, 0, 0).reshape(devices, -1).astype(F32)
+        sums = received[:, : share * columns].reshape(devices, share, columns)
+        figures = received[:, share * columns :].reshape(devices, 4, queries)
     tops = figures[:, 0] + figures[:, 1]
     totals = figures[:, 2] + figures[:, 3]
     row_top = jnp.max(tops, axis=0)

time: 117 us -> 113 us (0.966)
  Pallas kernels: 56.8 us -> 53.7 us
    pallas_call x1, Pallas kernels: 12 us -> 9.59 us  [near_call(): pl.pallas_call(functools.partial(near_kernel, rest, ahead), out_shape=mix...]
    pallas_call x1, Pallas kernels: 16.3 us -> 18.3 us  [near_call(): pl.pallas_call(functools.partial(near_kernel, rest, ahead), out_shape=(mi...]
    pallas_call x1, Pallas kernels: 3.85 us -> 2.45 us  [body(): pl.pallas_call(functools.partial(score_kernel, packed, groups), out_shape...]
    pallas_call x2, Pallas kernels: 22.3 us -> 20.9 us  [far_call(): pl.pallas_call(functools.partial(far_kernel, half_rel, last, ahead), out_...]
    unnamed x17 -> x11, local copies, waits for them, and re-layouts: 6.2 us -> 6.3 us
  transfers between devices with their start and end apart: 6 -> 6, of which waited for: 3 -> 3; matrix products, arithmetic and copies ran while one was open for 4% -> 4% of each run, Pallas kernels for 33% -> 32%
where the time goes in v5:
time: 113 us; the launch traced here: 112 us
  Pallas kernels  53.7 us (48%)
  starting transfers between devices  31.2 us (28%)
  waiting for transfers between devices  15 us (13%)
  local copies, waits for them, and re-layouts  9.32 us (8%)
  other arithmetic  2.01 us (2%)
    pallas_call x2, Pallas kernels, far_call(): pl.pallas_call(functools.partial(far_kernel, half_rel, last, ahead), out_...  20.9 us
    pallas_call x1, Pallas kernels, near_call(): pl.pallas_call(functools.partial(near_kernel, rest, ahead), out_shape=(mi...  18.3 us
    pallas_call x1, Pallas kernels, near_call(): pl.pallas_call(functools.partial(near_kernel, rest, ahead), out_shape=mix...  9.59 us
    all_to_all x1, waiting for transfers between devices, body(): received = lax.all_to_all(parts[0], BOTH, 0, 0).astype(F32)  8.88 us
    unnamed x11, local copies, waits for them, and re-layouts  6.3 us
    all_to_all x1, starting transfers between devices, body(): table = lax.all_to_all(spread, BOTH, 0, 0).reshape(groups * slots, columns)  6.12 us
    all_to_all x1, starting transfers between devices, body(): lax.all_to_all(heads, BOTH, 0, 0, tiled=True)  5.84 us
    all_to_all x1, starting transfers between devices, body(): received = lax.all_to_all(parts[0], BOTH, 0, 0).astype(F32)  5.84 us
  transfers between devices with their start and end apart: 6, of which 3 were waited for; matrix products, arithmetic and copies ran while one was open for 4% of the time, Pallas kernels for 32%

profile of v5, /device:TPU:0, one launch (start us, length us, event | category | flops | bytes accessed | tf_op | source)
XLA Modules:
  0.0 112.0 jit_solution(10624486356453921089)
XLA Ops:
  0.6 0.0 copy-start.2
  0.6 2.4 %shard_map.140 = bf16[128,256]{1,0:T(8,128)(2,1)} custom-call(s32[1]{0:T(128)} %bitcast.1.base_ref, s32[1,128]{1,0:T(1,128)} %index_ref.1, bf16[2304,256]{1,0:T(8,128)(2,1)} %emb_ref.5), custom_call_target="tpu_custom_call" | custom-call | tf_op jit(solution)/shard_map/pallas_call | solution.py:424
  3.0 4.2 %all-to-all-start = ((bf16[4,32,256]{2,1,0:T(8,128)(2,1)}), bf16[4,32,256]{2,1,0:T(8,128)(2,1)S(1)}, u32[]{:S(2)}, u32[]{:S(2)}) async-start(bf16[4,32,256]{2,1,0:T(8,128)(2,1)} %bitcast.27), calls=%async_computation | async-start | bytes 131072 | tf_op jit(solution)/shard_map/all_to_all | solution.py:431
  7.2 1.1 copy.18
  8.3 0.7 pad_bitcast_fusion.refs_5_.refs_4_.rest_1_
  9.1 0.0 copy-done.2
  9.1 1.5 %copy.17 = bf16[2304,256]{0,1:T(8,128)(2,1)} copy(bf16[2304,256]{1,0:T(8,128)(2,1)S(1)} %copy-done.2) | data formatting | bytes 2359296 | tf_op args[0]
  10.6 0.8 all-to-all-done
  11.4 0.9 broadcast_in_dim.18
  12.2 6.1 %all-to-all-start.1 = ((bf16[32,32,256]{2,1,0:T(8,128)(2,1)}), bf16[32,32,256]{2,1,0:T(8,128)(2,1)S(1)}, u32[]{:S(2)}, u32[]{:S(2)}) async-start(bf16[32,32,256]{2,1,0:T(8,128)(2,1)} %broadcast_in_dim.18), calls=%async_computation.1 | async-start | bytes 1048576 | tf_op jit(solution)/shard_map/all_to_all | solution.py:437
  18.4 18.3 %shard_map.141 = (bf16[9,2,256,768]{3,2,1,0:T(8,128)(2,1)}, s32[20]{0:T(128)}) custom-call(s32[1]{0:T(128)} %bitcast.refs_0_.base_ref, s32[256]{0:T(256)} %refs_1_.2, s32[18,768]{1,0:T(8,128)} %src_ref.3, s32[18,768]{1,0:T(8,128)} %rel_ref.3, bf16[256,2304]{1,0:T(8,128)(2,1)} %bitcast.23, bf16[256,512]{1,0:T(8,128)(2,1)} %pad_bitcast_fusion.refs_5_.refs_4_.rest_1_), custom_call_target="tpu_custom_call" | custom-call | flops 13287555072 | bytes 4718592 | tf_op jit(solution)/shard_map/pallas_call | solution.py:304
  36.7 0.0 all-to-all-done.1
  36.7 0.0 copy-start.3
  36.7 0.8 copy-done.3
  37.6 12.4 %shard_map.142 = (bf16[2304,256]{1,0:T(8,128)(2,1)}, bf16[256,256]{1,0:T(8,128)(2,1)}) custom-call(s32[1]{0:T(128)} %bitcast.refs_0_.base_ref, s32[20]{0:T(128)} %get-tuple-element.17.order_ref.refs_0_, s32[18,768]{1,0:T(8,128)} %src_ref.3, s32[18,768]{1,0:T(8,128)} %dst_ref.3, s32[18,768]{1,0:T(8,128)} %rel_ref.3, bf16[2304,256]{1,0:T(8,128)(2,1)} %emb_ref.5, ...), custom_call_target="tpu_custom_call" | custom-call | flops 3623878656 | bytes 3538944 | tf_op jit(solution)/shard_map/pallas_call | solution.py:327
  50.0 5.8 %all-to-all-start.2 = ((bf16[32,8,256]{2,1,0:T(8,128)(2,1)}), bf16[32,8,256]{2,1,0:T(8,128)(2,1)S(1)}, u32[]{:S(2)}, u32[]{:S(2)}) async-start(bf16[32,8,256]{2,1,0:T(8,128)(2,1)} %bitcast.29), calls=%async_computation.2 | async-start | bytes 262144 | tf_op jit(solution)/shard_map/all_to_all | solution.py:464
  55.9 9.6 %shard_map.143.rest_3_ = bf16[9,2,256,768]{3,2,1,0:T(8,128)(2,1)} custom-call(s32[20]{0:T(128)} %get-tuple-element.17.order_ref.refs_0_, s32[18,768]{1,0:T(8,128)} %src_ref.3, s32[18,768]{1,0:T(8,128)} %rel_ref.3, bf16[256,2304]{1,0:T(8,128)(2,1)} %bitcast.24, ...), custom_call_target="tpu_custom_call", output_to_operand_aliasing={{}: (5, {})} | custom-call | flops 6643777536 | bytes 2359296 | tf_op jit(solution)/shard_map/pallas_call | solution.py:313
  65.5 0.0 all-to-all-done.2
  65.5 0.7 broadcast_in_dim.42
  66.2 5.8 %all-to-all-start.3 = ((bf16[32,8,256]{2,1,0:T(8,128)(2,1)}), bf16[32,8,256]{2,1,0:T(8,128)(2,1)S(1)}, u32[]{:S(2)}, u32[]{:S(2)}) async-start(bf16[32,8,256]{2,1,0:T(8,128)(2,1)} %broadcast_in_dim.42), calls=%async_computation.3 | async-start | bytes 262144 | tf_op jit(solution)/shard_map/all_to_all | solution.py:468
  72.0 8.5 %shard_map.144 = (bf16[2304,256]{1,0:T(8,128)(2,1)}, f32[256,256]{1,0:T(8,128)}) custom-call(s32[1]{0:T(128)} %bitcast.refs_0_.base_ref, s32[20]{0:T(128)} %get-tuple-element.17.order_ref.refs_0_, s32[18,768]{1,0:T(8,128)} %src_ref.3, s32[18,768]{1,0:T(8,128)} %dst_ref.3, s32[18,768]{1,0:T(8,128)} %rel_ref.3, ...), custom_call_target="tpu_custom_call", output_to_operand_aliasing={{0}: (15, {})} | custom-call | flops 3623878656 | bytes 3538944 | tf_op jit(solution)/shard_map/pallas_call | solution.py:327
  80.5 0.0 all-to-all-done.3
  80.5 0.0 copy-start
  80.5 1.3 %copy-done = bf16[2304,256]{1,0:T(8,128)(2,1)S(1)} copy-done((bf16[2304,256]{1,0:T(8,128)(2,1)S(1)}, bf16[2304,256]{1,0:T(8,128)(2,1)}, u32[]{:S(2)}) %copy-start) | copy-done | bytes 1179672
  81.8 0.0 copy-start.1
  81.8 0.9 copy-done.1
  82.7 2.5 %shard_map.145 = (f32[256,2304]{1,0:T(8,128)S(1)}, bf16[32,24,128]{2,1,0:T(8,128)(2,1)}) custom-call(bf16[256,256]{1,0:T(8,128)(2,1)S(1)} %bitcast.22, f32[256,256]{1,0:T(8,128)S(1)} %copy-done.1, bf16[2304,256]{1,0:T(8,128)(2,1)S(1)} %copy-done), custom_call_target="tpu_custom_call" | custom-call | tf_op jit(solution)/shard_map/pallas_call | solution.py:494
  85.2 5.8 %all-to-all-start.4 = ((bf16[32,24,128]{2,1,0:T(8,128)(2,1)}), bf16[32,24,128]{2,1,0:T(8,128)(2,1)S(1)}, u32[]{:S(2)}, u32[]{:S(2)}) async-start(bf16[32,24,128]{2,1,0:T(8,128)(2,1)} %get-tuple-element.29), calls=%async_computation.4 | async-start | bytes 393216 | tf_op jit(solution)/shard_map/all_to_all | solution.py:500
  91.1 8.9 %all-to-all-done.4 = bf16[32,24,128]{2,1,0:T(8,128)(2,1)S(1)} async-done(((bf16[32,24,128]{2,1,0:T(8,128)(2,1)}), bf16[32,24,128]{2,1,0:T(8,128)(2,1)S(1)}, u32[]{:S(2)}, u32[]{:S(2)}) %all-to-all-start.4) | async-done | bytes 196640 | tf_op jit(solution)/shard_map/all_to_all | solution.py:500
  100.0 0.1 fusion.2
  100.1 0.1 dynamic-slice
  100.2 0.1 dynamic-slice_divide_fusion
  100.3 0.1 fusion
  100.4 0.6 broadcast_in_dim.44
  101.1 3.4 %all-to-all-start.5 = ((f32[8,8,256]{2,1,0:T(8,128)}), f32[8,8,256]{2,1,0:T(8,128)S(1)}, u32[]{:S(2)}, u32[]{:S(2)}) async-start(f32[8,8,256]{2,1,0:T(8,128)} %broadcast_in_dim.44), calls=%async_computation.5 | async-start | bytes 131072 | tf_op jit(solution)/shard_map/all_to_all | solution.py:527
  104.4 1.6 %broadcast_subtract_fusion = f32[256,2304]{1,0:T(8,128)} fusion(f32[256,2304]{1,0:T(8,128)S(1)} %get-tuple-element.28, f32[256]{0:T(256)S(1)} %log_add_fusion), kind=kLoop, calls=%fused_computation | loop fusion | flops 589824 | bytes 4719616 | tf_op jit(solution)/shard_map/sub | solution.py:530
  106.0 5.4 %all-to-all-done.5 = f32[8,8,256]{2,1,0:T(8,128)S(1)} async-done(((f32[8,8,256]{2,1,0:T(8,128)}), f32[8,8,256]{2,1,0:T(8,128)S(1)}, u32[]{:S(2)}, u32[]{:S(2)}) %all-to-all-start.5) | async-done | bytes 65568 | tf_op jit(solution)/shard_map/all_to_all | solution.py:527
  111.4 0.6 copy.40
  (7 shorter events, 0.2 us)
Async XLA Ops:
  0.6 8.5 %copy-start.2 = (bf16[2304,256]{1,0:T(8,128)(2,1)S(1)}, bf16[2304,256]{1,0:T(8,128)(2,1)}, u32[]{:S(2)}) copy-start(bf16[2304,256]{1,0:T(8,128)(2,1)} %emb_ref.5) | copy-start | bytes 3538948
  3.0 8.3 %all-to-all-start = ((bf16[4,32,256]{2,1,0:T(8,128)(2,1)}), bf16[4,32,256]{2,1,0:T(8,128)(2,1)S(1)}, u32[]{:S(2)}, u32[]{:S(2)}) async-start(bf16[4,32,256]{2,1,0:T(8,128)(2,1)} %bitcast.27), calls=%async_computation | async-start | bytes 131072 | tf_op jit(solution)/shard_map/all_to_all | solution.py:431
  12.2 24.4 %all-to-all-start.1 = ((bf16[32,32,256]{2,1,0:T(8,128)(2,1)}), bf16[32,32,256]{2,1,0:T(8,128)(2,1)S(1)}, u32[]{:S(2)}, u32[]{:S(2)}) async-start(bf16[32,32,256]{2,1,0:T(8,128)(2,1)} %broadcast_in_dim.18), calls=%async_computation.1 | async-start | bytes 1048576 | tf_op jit(solution)/shard_map/all_to_all | solution.py:437
  36.7 0.9 copy-start.3
  50.0 15.5 %all-to-all-start.2 = ((bf16[32,8,256]{2,1,0:T(8,128)(2,1)}), bf16[32,8,256]{2,1,0:T(8,128)(2,1)S(1)}, u32[]{:S(2)}, u32[]{:S(2)}) async-start(bf16[32,8,256]{2,1,0:T(8,128)(2,1)} %bitcast.29), calls=%async_computation.2 | async-start | bytes 262144 | tf_op jit(solution)/shard_map/all_to_all | solution.py:464
  66.2 14.3 %all-to-all-start.3 = ((bf16[32,8,256]{2,1,0:T(8,128)(2,1)}), bf16[32,8,256]{2,1,0:T(8,128)(2,1)S(1)}, u32[]{:S(2)}, u32[]{:S(2)}) async-start(bf16[32,8,256]{2,1,0:T(8,128)(2,1)} %broadcast_in_dim.42), calls=%async_computation.3 | async-start | bytes 262144 | tf_op jit(solution)/shard_map/all_to_all | solution.py:468
  80.5 1.3 %copy-start = (bf16[2304,256]{1,0:T(8,128)(2,1)S(1)}, bf16[2304,256]{1,0:T(8,128)(2,1)}, u32[]{:S(2)}) copy-start(bf16[2304,256]{1,0:T(8,128)(2,1)} %get-tuple-element.27.hidden_ref) | copy-start | bytes 3538948
  81.8 0.9 copy-start.1
  85.2 14.7 %all-to-all-start.4 = ((bf16[32,24,128]{2,1,0:T(8,128)(2,1)}), bf16[32,24,128]{2,1,0:T(8,128)(2,1)S(1)}, u32[]{:S(2)}, u32[]{:S(2)}) async-start(bf16[32,24,128]{2,1,0:T(8,128)(2,1)} %get-tuple-element.29), calls=%async_computation.4 | async-start | bytes 393216 | tf_op jit(solution)/shard_map/all_to_all | solution.py:500
  101.1 10.4 %all-to-all-start.5 = ((f32[8,8,256]{2,1,0:T(8,128)}), f32[8,8,256]{2,1,0:T(8,128)S(1)}, u32[]{:S(2)}, u32[]{:S(2)}) async-start(f32[8,8,256]{2,1,0:T(8,128)} %broadcast_in_dim.44), calls=%async_computation.5 | async-start | bytes 131072 | tf_op jit(solution)/shard_map/all_to_all | solution.py:527

commit v6 on v5

--- a/solution.py
+++ b/solution.py
@@ -56,21 +56,23 @@
     return jnp.maximum((order_ref[blocks] + STEP - 1) // STEP, ahead)
 
 
-def near_kernel(rest, ahead, *refs):
-    if rest:
-        order_ref, src_ref, rel_ref, near_ref, relation_ref, _ = refs[:6]
-        mixed_ref, held_ref, sems = refs[6:]
-    else:
-        base_ref, head_ref, src_ref, rel_ref, near_ref, relation_ref = refs[:6]
-        mixed_ref, order_ref, held_ref, sems = refs[6:]
+def near_kernel(
+    ahead,
+    base_ref,
+    head_ref,
+    src_ref,
+    rel_ref,
+    near_ref,
+    relation_ref,
+    mixed_ref,
+    order_ref,
+    held_ref,
+    sems,
+):
     blocks = src_ref.shape[0]
     rows_dev = near_ref.shape[1]
-    steps = blocks // STEP
-    if not rest:
-        order_blocks(head_ref, base_ref[0], blocks, order_ref)
-    middle = middle_step(order_ref, blocks, ahead)
-    start, stop = (middle, steps) if rest else (0, middle)
-    count = stop - start
+    order_blocks(head_ref, base_ref[0], blocks, order_ref)
+    count = middle_step(order_ref, blocks, ahead)
 
     def save(step, slot):
         return pltpu.make_async_copy(held_ref.at[slot], mixed_ref.at[step], sems.at[slot])
@@ -80,10 +82,10 @@
 
         @pl.when(i >= 2)
         def _():
-            save(start + i - 2, slot).wait()
+            save(i - 2, slot).wait()
 
         for u in range(STEP):
-            block = order_ref[(start + i) * STEP + u]
+            block = order_ref[i * STEP + u]
             src = src_ref[pl.ds(block, 1), :]
             rel = rel_ref[pl.ds(block, 1), :]
             gathered = jnp.dot(near_ref[...], one_hot(src, rows_dev), preferred_element_type=F32)
@@ -94,7 +96,7 @@
             )
             is_far = is_outside(src, rows_dev)
             held_ref[slot, u] = (gathered.astype(BF16) + is_far) * relation.astype(BF16)
-        save(start + i, slot).start()
+        save(i, slot).start()
         return carry
 
     lax.fori_loop(0, count, one_step, 0)
@@ -102,13 +104,29 @@
 
         @pl.when(count >= back)
         def _():
-            save(start + count - back, lax.rem(count - back, 2)).wait()
+            save(count - back, lax.rem(count - back, 2)).wait()
+
+
+def owners(head_row, devices, rows_dev):
+    limits = lax.broadcasted_iota(jnp.int32, (devices, head_row.shape[1]), 0) * rows_dev
+    return jnp.sum((limits <= head_row).astype(F32), axis=0, keepdims=True) - 1.0
+
+
+def ranks(owner_row):
+    queries = owner_row.shape[1]
+    across = jnp.broadcast_to(owner_row, (queries, queries))
+    earlier = lax.broadcasted_iota(jnp.int32, (queries, queries), 0) < lax.broadcasted_iota(
+        jnp.int32, (queries, queries), 1
+    )
+    same = (jnp.transpose(across) == across) & earlier
+    return jnp.sum(same.astype(F32), axis=0, keepdims=True)
 
 
 def far_kernel(
     half_rel,
     last,
     ahead,
+    devices,
     base_ref,
     order_ref,
     src_ref,
@@ -124,10 +142,10 @@
 ):
     far_t_ref, gathered_ref, agg_ref, held_ref, own_ref, made_ref, sems, own_sems, out_sems = rest[-9:]
     if last:
-        query_rel_ref, relation_ref, rel_weight_ref, mixed_ref, _ = rest[:5]
+        near_ref, query_rel_ref, relation_ref, rel_weight_ref, _ = rest[:5]
         hidden_ref, factor_ref = rest[5:7]
     else:
-        head_ref, mixed_ref, hidden_ref, heads_ref = rest[:4]
+        head_ref, mixed_ref, hidden_ref, heads_ref, rank_ref, most_ref = rest[:6]
     blocks = src_ref.shape[0]
     rows_dev = blocks * BLK
     far_chunks = far_ref.shape[0]
@@ -152,9 +170,11 @@
             made_ref.at[rows], hidden_ref.at[rows], out_sems.at[step * STEP + u]
         )
 
-    @pl.when(start < stop)
-    def _():
-        load(start, 0).start()
+    if not last:
+
+        @pl.when(start < stop)
+        def _():
+            load(start, 0).start()
 
     def turn(j, carry):
         far_t_ref[j] = jnp.transpose(far_ref[j])
@@ -205,19 +225,32 @@
         for u in range(STEP):
             load_own(step, u).start()
 
-        @pl.when(start + i + 1 < stop)
-        def _():
-            load(start + i + 1, 1 - slot).start()
-
-        load(start + i, slot).wait()
+        if not last:
+
+            @pl.when(step + 1 < stop)
+            def _():
+                load(step + 1, 1 - slot).start()
+
+            load(step, slot).wait()
         finish(before, lax.rem(step + 1, 2))
         rows = [pl.ds(order_ref[(start + i) * STEP + u], 1) for u in range(STEP)]
         srcs = [src_ref[row, :] for row in rows]
         found = [look_up(src, u) for u, src in enumerate(srcs)]
-        composed = [
-            (found[u].astype(BF16) + (1 - is_outside(srcs[u], rows_dev))) * held_ref[slot, u]
-            for u in range(STEP)
-        ]
+        composed = []
+        for u, row in enumerate(rows):
+            if last:
+                near = jnp.dot(
+                    near_ref[...], one_hot(srcs[u], rows_dev), preferred_element_type=F32
+                )
+                relation = jnp.dot(
+                    relation_ref[...],
+                    one_hot(rel_ref[row, :], relation_ref.shape[1]),
+                    preferred_element_type=F32,
+                )
+                composed.append((found[u] + near).astype(BF16) * relation.astype(BF16))
+            else:
+                is_near = 1 - is_outside(srcs[u], rows_dev)
+                composed.append((found[u].astype(BF16) + is_near) * held_ref[slot, u])
         for u, row in enumerate(rows):
             key = dst_ref[row, :] + jnp.where(rel_ref[row, :] >= half_rel, BLK, 0)
             selector = one_hot(key, 2 * BLK)
@@ -258,9 +291,12 @@
         )
     else:
         picks = one_hot_wide(head_ref[...] - base_ref[0] * BLK, rows_dev)
-        heads_ref[...] = lax.dot_general(
-            picks, made_ref[...], TN, preferred_element_type=F32
-        ).astype(BF16)
+        rows = lax.dot_general(picks, made_ref[...], TN, preferred_element_type=F32)
+        rank = ranks(owners(head_ref[...], devices, rows_dev))
+        slots = one_hot(rank.astype(jnp.int32), heads_ref.shape[0])
+        heads_ref[...] = jnp.dot(slots, rows.astype(BF16), preferred_element_type=F32).astype(BF16)
+        rank_ref[...] = rank.astype(jnp.int32)
+        most_ref[0] = jnp.max(rank).astype(jnp.int32)
 
     def gave(step, carry):
         for u in range(STEP):
@@ -282,59 +318,44 @@
 HBM = pl.BlockSpec(memory_space=pltpu.HBM)
 
 
-def near_call(rest, ahead, src, rel, near, relation, more):
+def near_call(ahead, base, query_head, src, rel, near, relation):
     columns, edges = near.shape[0], src.shape[1]
     blocks = src.shape[0]
-    steps = blocks // STEP
-    count = STEP * (steps - ahead if rest else ahead)
+    count = STEP * ahead
     flops = 2 * count * edges * columns * (near.shape[1] + relation.shape[1])
-    mixed_type = jax.ShapeDtypeStruct((steps, STEP, columns, edges), BF16)
-    order_type = jax.ShapeDtypeStruct((blocks + 2,), jnp.int32)
-    scratch = [
-        pltpu.VMEM((2, STEP, columns, edges), BF16),
-        pltpu.SemaphoreType.DMA((2,)),
-    ]
-    settings = dict(
+    return pl.pallas_call(
+        functools.partial(near_kernel, ahead),
+        out_shape=(
+            jax.ShapeDtypeStruct((blocks // STEP, STEP, columns, edges), BF16),
+            jax.ShapeDtypeStruct((blocks + 2,), jnp.int32),
+        ),
+        in_specs=[SMEM] * 2 + [WHOLE] * 4,
+        out_specs=(HBM, SMEM),
+        scratch_shapes=[
+            pltpu.VMEM((2, STEP, columns, edges), BF16),
+            pltpu.SemaphoreType.DMA((2,)),
+        ],
         compiler_params=pltpu.CompilerParams(vmem_limit_bytes=VMEM_LIMIT),
         cost_estimate=pl.CostEstimate(
             flops=flops, bytes_accessed=2 * count * edges * columns, transcendentals=0
         ),
-    )
-    if not rest:
-        return pl.pallas_call(
-            functools.partial(near_kernel, rest, ahead),
-            out_shape=(mixed_type, order_type),
-            in_specs=[SMEM] * 2 + [WHOLE] * 4,
-            out_specs=(HBM, SMEM),
-            scratch_shapes=scratch,
-            **settings,
-        )(*more, src, rel, near, relation)
-    mixed, order = more
-    return pl.pallas_call(
-        functools.partial(near_kernel, rest, ahead),
-        out_shape=mixed_type,
-        in_specs=[SMEM] + [WHOLE] * 4 + [HBM],
-        out_specs=HBM,
-        input_output_aliases={5: 0},
-        scratch_shapes=scratch,
-        **settings,
-    )(order, src, rel, near, relation, mixed)
-
-
-def far_call(half_rel, last, ahead, scalars, edges, emb, far, weights, more, kept, second):
+    )(base, query_head, src, rel, near, relation)
+
+
+def far_call(half_rel, last, ahead, devices, scalars, edges, emb, far, weights, more, kept, outs):
     rows_dev, columns = emb.shape
     blocks, width = edges[0].shape
     return pl.pallas_call(
-        functools.partial(far_kernel, half_rel, last, ahead),
-        out_shape=(jax.ShapeDtypeStruct((rows_dev, columns), BF16), second),
-        in_specs=[SMEM] * 2 + [WHOLE] * 3 + [HBM] + [WHOLE] * (5 + len(more)) + [HBM] * (2 if last else 1),
-        out_specs=(HBM, WHOLE),
-        input_output_aliases={12 + len(more): 0} if last else {},
+        functools.partial(far_kernel, half_rel, last, ahead, devices),
+        out_shape=(jax.ShapeDtypeStruct((rows_dev, columns), BF16),) + outs,
+        in_specs=[SMEM] * 2 + [WHOLE] * 3 + [HBM] + [WHOLE] * (5 + len(more)) + [HBM],
+        out_specs=(HBM, WHOLE) if last else (HBM, WHOLE, WHOLE, SMEM),
+        input_output_aliases={11 + len(more): 0} if last else {},
         scratch_shapes=[
             pltpu.VMEM((far.shape[0], columns, CHUNK), BF16),
             pltpu.VMEM((STEP, columns, width if far.shape[0] > 1 else 128), F32),
             pltpu.VMEM((2, 2, STEP * BLK, columns), BF16),
-            pltpu.VMEM((2, STEP, columns, width), BF16),
+            pltpu.VMEM((2, STEP, columns, 128 if last else width), BF16),
             pltpu.VMEM((2, STEP, BLK, columns), BF16),
             pltpu.VMEM((rows_dev, columns), BF16),
             pltpu.SemaphoreType.DMA((2,)),
@@ -347,11 +368,29 @@
             bytes_accessed=blocks * width * columns,
             transcendentals=0,
         ),
-    )(*scalars, *edges, emb, far, *weights, *more, *kept)
-
-
-def score_kernel(packed, groups, heads_ref, rel_ref, hidden_ref, scores_ref, *outs):
-    query = (heads_ref[...].astype(F32) * rel_ref[...]).astype(BF16)
+    )(*scalars, *edges, emb, far, *weights, *more, kept)
+
+
+def score_kernel(
+    packed,
+    groups,
+    devices,
+    sent_ref,
+    more_ref,
+    rank_ref,
+    head_ref,
+    rel_ref,
+    hidden_ref,
+    scores_ref,
+    *outs,
+):
+    slots = sent_ref.shape[0] // devices
+    owner = owners(head_ref[...], devices, hidden_ref.shape[0]).astype(jnp.int32)
+    place = jnp.where(rank_ref[...] < slots, owner * slots + rank_ref[...], -1)
+    picks = one_hot(place, sent_ref.shape[0])
+    heads = lax.dot_general(picks, sent_ref[...], TN, preferred_element_type=F32)
+    heads = heads + more_ref[...].astype(F32)
+    query = (heads * rel_ref[...]).astype(BF16)
     scores = lax.dot_general(query, hidden_ref[...], NT, preferred_element_type=F32)
     scores_ref[...] = scores
     top = jnp.max(scores, axis=1, keepdims=True)
@@ -375,7 +414,6 @@
     (payload_ref,) = outs
     upper = lax.broadcasted_iota(jnp.int32, (8, 128), 0) < 4
     figures = jnp.where(upper, stats[:8, :128], stats[:8, 128:])
-    devices = payload_ref.shape[0]
     copies = devices // groups
     share = query.shape[0] // devices
     for device in range(devices):
@@ -437,49 +475,67 @@
     table = lax.all_to_all(spread, BOTH, 0, 0).reshape(groups * slots, columns)
     base = (device * blocks)[None]
     mixed, order = near_call(
-        False, ahead, edge_src, edge_rel, near_t, relation_t, (base, query_head)
+        ahead, base, query_head, edge_src, edge_rel, near_t, relation_t
     )
     far_count = -(-(groups * slots) // CHUNK) * CHUNK
     far = jnp.pad(table, ((0, far_count - groups * slots), (0, 0)))
     far = far.reshape(far_count // CHUNK, CHUNK, columns)
 
-    heads_row = jnp.pad(query_head, (0, padded - queries), constant_values=-1)[None]
+    head_row = query_head[None]
     weights = (in_weight, out_weight, loop_weight, loop_rel[None])
     edges = (edge_src, edge_dst, edge_rel)
-    half_rel = relations // 2
-    hidden, heads = far_call(
-        half_rel,
+    cap = min(queries, -(-3 * queries // (8 * devices)) * 8)
+    hidden, heads, rank, most = far_call(
+        relations // 2,
         False,
         ahead,
+        devices,
         (base, order),
         edges,
         entity_emb,
         far,
         weights,
-        (heads_row,),
-        (mixed,),
-        jax.ShapeDtypeStruct((padded, columns), BF16),
-    )
-    heads, mixed = lax.optimization_barrier((heads, mixed))
-    parts = lax.all_to_all(heads, BOTH, 0, 0, tiled=True).reshape(devices, share, columns)
-    mixed = near_call(True, ahead, edge_src, edge_rel, near_t, relation_t, (mixed, order))
-    own_heads = jnp.sum(parts.astype(F32), axis=0).astype(BF16)
-    own_heads, mixed = lax.optimization_barrier((own_heads, mixed))
-    head_rows = lax.all_to_all(
-        jnp.broadcast_to(own_heads[None], (devices, share, columns)), BOTH, 0, 0
-    ).reshape(padded, columns)[:queries]
+        (head_row,),
+        mixed,
+        (
+            jax.ShapeDtypeStruct((-(-queries // cap) * cap, columns), BF16),
+            jax.ShapeDtypeStruct((1, queries), jnp.int32),
+            jax.ShapeDtypeStruct((1,), jnp.int32),
+        ),
+    )
+
+    def send_round(turn):
+        some = lax.dynamic_slice_in_dim(heads, turn * cap, cap, 0)
+        spread = jnp.broadcast_to(some[None], (devices,) + some.shape)
+        return lax.all_to_all(spread, BOTH, 0, 0).reshape(devices * cap, columns)
+
+    def another_round(state):
+        turn, more = state
+        slot = rank[0] - turn * cap
+        place = query_head // rows_dev * cap + slot
+        rows = jnp.take(send_round(turn), jnp.clip(place, 0, devices * cap - 1), axis=0)
+        inside = (slot >= 0) & (slot < cap)
+        return turn + 1, jnp.where(inside[:, None], rows, more)
+
+    sent = send_round(0)
     hidden, query_factor = far_call(
-        half_rel,
+        relations // 2,
         True,
         ahead,
+        devices,
         (base, order),
         edges,
         entity_emb,
         far,
         weights,
-        (query_rel[None], relation_t, rel_weight),
-        (mixed, hidden),
-        jax.ShapeDtypeStruct((queries, columns), F32),
+        (near_t, query_rel[None], relation_t, rel_weight),
+        hidden,
+        (jax.ShapeDtypeStruct((queries, columns), F32),),
+    )
+    _, more_heads = lax.while_loop(
+        lambda state: state[0] * cap <= most[0],
+        another_round,
+        (jnp.int32(1), jnp.zeros((queries, columns), BF16)),
     )
 
     packed = share == 8 and share * devices == queries and (queries, columns) == (256, 256)
@@ -492,10 +548,10 @@
             jax.ShapeDtypeStruct((16, queries), BF16),
         )
     scores, *parts = pl.pallas_call(
-        functools.partial(score_kernel, packed, groups),
+        functools.partial(score_kernel, packed, groups, devices),
         out_shape=(score_type,) + more,
         compiler_params=pltpu.CompilerParams(vmem_limit_bytes=SCORE_LIMIT),
-    )(head_rows, query_factor, hidden)
+    )(sent, more_heads, rank, head_row, query_factor, hidden)
     if packed:
         received = lax.all_to_all(parts[0], BOTH, 0, 0).astype(F32)
         sums = jnp.concatenate([received[:, :8], received[:, 8:16]], axis=2)

time: 113 us -> 105 us (0.929)
  starting transfers between devices: 31.2 us -> 24.6 us
  Pallas kernels: 53.7 us -> 50.6 us
    all_to_all x2 -> x1, starting transfers between devices: 11.7 us -> 5.83 us  [send_round(): return lax.all_to_all(spread, BOTH, 0, 0).reshape(devices * cap, columns)]
    pallas_call x5 -> x4, Pallas kernels: 51.3 us -> 48.3 us  [the longest x2 27.4 us: far_call(): pl.pallas_call(functools.partial(far_kernel, half_rel, last, ahead, devic...]
    unnamed x11 -> x13, local copies, waits for them, and re-layouts: 6.3 us -> 6.38 us
  transfers between devices with their start and end apart: 6 -> 5, of which waited for: 3 -> 3; matrix products, arithmetic and copies ran while one was open for 4% -> 4% of each run, Pallas kernels for 32% -> 31%
where the time goes in v6:
time: 105 us; the launch traced here: 104 us
  Pallas kernels  50.6 us (48%)
  starting transfers between devices  24.6 us (23%)
  waiting for transfers between devices  16.1 us (15%)
  local copies, waits for them, and re-layouts  9.52 us (9%)
  other arithmetic  1.98 us (2%)
    pallas_call x2, Pallas kernels, far_call(): pl.pallas_call(functools.partial(far_kernel, half_rel, last, ahead, devic...  27.4 us
    pallas_call x1, Pallas kernels, near_call(): pl.pallas_call(functools.partial(near_kernel, ahead), out_shape=(jax.Shap...  18.3 us
    all_to_all x1, waiting for transfers between devices, body(): received = lax.all_to_all(parts[0], BOTH, 0, 0).astype(F32)  8.88 us
    unnamed x13, local copies, waits for them, and re-layouts  6.38 us
    all_to_all x1, starting transfers between devices, send_round(): return lax.all_to_all(spread, BOTH, 0, 0).reshape(devices * cap, columns)  5.83 us
    all_to_all x1, starting transfers between devices, body(): received = lax.all_to_all(parts[0], BOTH, 0, 0).astype(F32)  5.83 us
    all_to_all x1, starting transfers between devices, body(): table = lax.all_to_all(spread, BOTH, 0, 0).reshape(groups * slots, columns)  5.42 us
    all_to_all x1, waiting for transfers between devices, body(): lax.all_to_all(jnp.broadcast_to(own_expected[None], (groups, share, colum...  5.36 us
  transfers between devices with their start and end apart: 5, of which 3 were waited for; matrix products, arithmetic and copies ran while one was open for 4% of the time, Pallas kernels for 31%

profile of v6, /device:TPU:0, one launch (start us, length us, event | category | flops | bytes accessed | tf_op | source)
XLA Modules:
  0.0 104.3 jit_solution(11486542755946879965)
XLA Ops:
  0.6 0.0 copy-start.2
  0.6 0.0 copy-start.4
  0.7 1.2 %copy.17 = bf16[474,256]{0,1:T(8,128)(2,1)S(1)} copy(bf16[474,256]{1,0:T(8,128)(2,1)} %param.16) | data formatting | bytes 485376 | tf_op args[1]
  1.8 2.3 %shard_map.140 = bf16[128,256]{1,0:T(8,128)(2,1)} custom-call(s32[1]{0:T(128)} %bitcast.7.base_ref, s32[1,128]{1,0:T(1,128)} %index_ref.1, bf16[2304,256]{1,0:T(8,128)(2,1)} %emb_ref.5), custom_call_target="tpu_custom_call" | custom-call | tf_op jit(solution)/shard_map/pallas_call | solution.py:462
  4.1 4.2 %all-to-all-start.1 = ((bf16[4,32,256]{2,1,0:T(8,128)(2,1)}), bf16[4,32,256]{2,1,0:T(8,128)(2,1)S(1)}, u32[]{:S(2)}, u32[]{:S(2)}) async-start(bf16[4,32,256]{2,1,0:T(8,128)(2,1)} %bitcast.50), calls=%async_computation.1 | async-start | bytes 131072 | tf_op jit(solution)/shard_map/all_to_all | solution.py:469
  8.3 0.7 pad_bitcast_fusion.relation_ref.rest_2_
  9.1 0.0 copy-done.2
  9.1 1.5 %copy.16 = bf16[2304,256]{0,1:T(8,128)(2,1)} copy(bf16[2304,256]{1,0:T(8,128)(2,1)S(1)} %copy-done.2) | data formatting | bytes 2359296 | tf_op args[0]
  10.6 0.0 copy-done.4
  10.6 1.8 %all-to-all-done.1 = bf16[4,32,256]{2,1,0:T(8,128)(2,1)S(1)} async-done(((bf16[4,32,256]{2,1,0:T(8,128)(2,1)}), bf16[4,32,256]{2,1,0:T(8,128)(2,1)S(1)}, u32[]{:S(2)}, u32[]{:S(2)}) %all-to-all-start.1) | async-done | bytes 65568 | tf_op jit(solution)/shard_map/all_to_all | solution.py:469
  12.5 0.8 broadcast_in_dim.80
  13.3 5.4 %all-to-all-start.2 = ((bf16[32,32,256]{2,1,0:T(8,128)(2,1)}), bf16[32,32,256]{2,1,0:T(8,128)(2,1)S(1)}, u32[]{:S(2)}, u32[]{:S(2)}) async-start(bf16[32,32,256]{2,1,0:T(8,128)(2,1)} %broadcast_in_dim.80), calls=%async_computation.2 | async-start | bytes 1048576 | tf_op jit(solution)/shard_map/all_to_all | solution.py:475
  18.8 18.3 %shard_map.141 = (bf16[9,2,256,768]{3,2,1,0:T(8,128)(2,1)}, s32[20]{0:T(128)}) custom-call(s32[1]{0:T(128)} %bitcast.6.base_ref, s32[256]{0:T(256)S(1)} %copy-done.4, s32[18,768]{1,0:T(8,128)} %src_ref.5, s32[18,768]{1,0:T(8,128)} %rel_ref.5, bf16[256,2304]{1,0:T(8,128)(2,1)} %bitcast.46, bf16[256,512]{1,0:T(8,128)(2,1)} %pad_bitcast_fusion.relation_ref.rest_2_), custom_call_target="tpu_custom_call" | custom-call | flops 13287555072 | bytes 4718592 | tf_op jit(solution)/shard_map/pallas_call | solution.py:326
  37.1 0.0 all-to-all-done.2
  37.1 0.0 copy-start.3
  37.1 0.8 copy-done.3
  37.9 12.9 %shard_map.142 = (bf16[2304,256]{1,0:T(8,128)(2,1)}, bf16[264,256]{1,0:T(8,128)(2,1)S(1)}, s32[1,256]{1,0:T(1,128)S(1)}, s32[1]{0:T(128)}) custom-call(s32[1]{0:T(128)} %bitcast.6.base_ref, s32[20]{0:T(128)} %get-tuple-element.107.order_ref, s32[18,768]{1,0:T(8,128)} %src_ref.5, s32[18,768]{1,0:T(8,128)} %dst_ref.3, s32[18,768]{1,0:T(8,128)} %rel_ref.5, ...), custom_call_target="tpu_custom_call" | custom-call | flops 3623878656 | bytes 3538944 | tf_op jit(solution)/shard_map/pallas_call | solution.py:348
  50.8 0.6 while.12
  51.5 0.8 broadcast_in_dim.83
  52.2 5.8 %all-to-all-start.3 = ((bf16[32,24,256]{2,1,0:T(8,128)(2,1)}), bf16[32,24,256]{2,1,0:T(8,128)(2,1)S(1)}, u32[]{:S(2)}, u32[]{:S(2)}) async-start(bf16[32,24,256]{2,1,0:T(8,128)(2,1)} %broadcast_in_dim.83), calls=%async_computation.3 | async-start | bytes 786432 | tf_op jit(solution)/shard_map/all_to_all | solution.py:510
  58.1 14.6 %shard_map.143 = (bf16[2304,256]{1,0:T(8,128)(2,1)}, f32[256,256]{1,0:T(8,128)}) custom-call(s32[1]{0:T(128)} %bitcast.6.base_ref, s32[20]{0:T(128)} %get-tuple-element.107.order_ref, s32[18,768]{1,0:T(8,128)} %src_ref.5, s32[18,768]{1,0:T(8,128)} %dst_ref.3, s32[18,768]{1,0:T(8,128)} %rel_ref.5, ...), custom_call_target="tpu_custom_call", output_to_operand_aliasing={{0}: (15, {})} | custom-call | flops 3623878656 | bytes 3538944 | tf_op jit(solution)/shard_map/pallas_call | solution.py:348
  72.6 0.0 all-to-all-done.3
  72.7 0.0 copy-start
  72.7 1.3 %copy-done = bf16[2304,256]{1,0:T(8,128)(2,1)S(1)} copy-done((bf16[2304,256]{1,0:T(8,128)(2,1)S(1)}, bf16[2304,256]{1,0:T(8,128)(2,1)}, u32[]{:S(2)}) %copy-start) | copy-done | bytes 1179672
  73.9 0.0 copy-start.1
  73.9 0.9 copy-done.1
  74.9 2.6 %shard_map.144 = (f32[256,2304]{1,0:T(8,128)S(1)}, bf16[32,24,128]{2,1,0:T(8,128)(2,1)}) custom-call(bf16[768,256]{1,0:T(8,128)(2,1)S(1)} %bitcast.44, bf16[256,256]{1,0:T(8,128)(2,1)S(1)} %get-tuple-element.113.more_ref, s32[1,256]{1,0:T(1,128)S(1)} %get-tuple-element.254, s32[1,256]{1,0:T(1,128)S(1)} %bitcast.59, f32[256,256]{1,0:T(8,128)S(1)} %copy-done.1, ...), custom_call_target="tpu_custom_call" | custom-call | tf_op jit(solution)/shard_map/pallas_call | solution.py:550
  77.5 5.8 %all-to-all-start.4 = ((bf16[32,24,128]{2,1,0:T(8,128)(2,1)}), bf16[32,24,128]{2,1,0:T(8,128)(2,1)S(1)}, u32[]{:S(2)}, u32[]{:S(2)}) async-start(bf16[32,24,128]{2,1,0:T(8,128)(2,1)} %get-tuple-element.118), calls=%async_computation.4 | async-start | bytes 393216 | tf_op jit(solution)/shard_map/all_to_all | solution.py:556
  83.3 8.9 %all-to-all-done.4 = bf16[32,24,128]{2,1,0:T(8,128)(2,1)S(1)} async-done(((bf16[32,24,128]{2,1,0:T(8,128)(2,1)}), bf16[32,24,128]{2,1,0:T(8,128)(2,1)S(1)}, u32[]{:S(2)}, u32[]{:S(2)}) %all-to-all-start.4) | async-done | bytes 196640 | tf_op jit(solution)/shard_map/all_to_all | solution.py:556
  92.2 0.1 fusion.5
  92.4 0.1 dynamic-slice
  92.5 0.1 dynamic-slice_divide_fusion
  92.6 0.1 fusion.3
  92.7 0.6 broadcast_in_dim.86
  93.3 3.4 %all-to-all-start.5 = ((f32[8,8,256]{2,1,0:T(8,128)}), f32[8,8,256]{2,1,0:T(8,128)S(1)}, u32[]{:S(2)}, u32[]{:S(2)}) async-start(f32[8,8,256]{2,1,0:T(8,128)} %broadcast_in_dim.86), calls=%async_computation.5 | async-start | bytes 131072 | tf_op jit(solution)/shard_map/all_to_all | solution.py:583
  96.7 1.6 %broadcast_subtract_fusion.1 = f32[256,2304]{1,0:T(8,128)} fusion(f32[256,2304]{1,0:T(8,128)S(1)} %get-tuple-element.117, f32[256]{0:T(256)S(1)} %log_add_fusion), kind=kLoop, calls=%fused_computation.17 | loop fusion | flops 589824 | bytes 4719616 | tf_op jit(solution)/shard_map/sub | solution.py:586
  98.3 5.4 %all-to-all-done.5 = f32[8,8,256]{2,1,0:T(8,128)S(1)} async-done(((f32[8,8,256]{2,1,0:T(8,128)}), f32[8,8,256]{2,1,0:T(8,128)S(1)}, u32[]{:S(2)}, u32[]{:S(2)}) %all-to-all-start.5) | async-done | bytes 65568 | tf_op jit(solution)/shard_map/all_to_all | solution.py:583
  103.7 0.6 copy.44
  (9 shorter events, 0.1 us)
Async XLA Ops:
  0.6 8.5 %copy-start.2 = (bf16[2304,256]{1,0:T(8,128)(2,1)S(1)}, bf16[2304,256]{1,0:T(8,128)(2,1)}, u32[]{:S(2)}) copy-start(bf16[2304,256]{1,0:T(8,128)(2,1)} %emb_ref.5) | copy-start | bytes 3538948
  0.6 10.0 %copy-start.4 = (s32[256]{0:T(256)S(1)}, s32[256]{0:T(256)}, u32[]{:S(2)}) copy-start(s32[256]{0:T(256)} %head_ref.1) | copy-start | bytes 3076
  4.1 8.3 %all-to-all-start.1 = ((bf16[4,32,256]{2,1,0:T(8,128)(2,1)}), bf16[4,32,256]{2,1,0:T(8,128)(2,1)S(1)}, u32[]{:S(2)}, u32[]{:S(2)}) async-start(bf16[4,32,256]{2,1,0:T(8,128)(2,1)} %bitcast.50), calls=%async_computation.1 | async-start | bytes 131072 | tf_op jit(solution)/shard_map/all_to_all | solution.py:469
  13.3 23.7 %all-to-all-start.2 = ((bf16[32,32,256]{2,1,0:T(8,128)(2,1)}), bf16[32,32,256]{2,1,0:T(8,128)(2,1)S(1)}, u32[]{:S(2)}, u32[]{:S(2)}) async-start(bf16[32,32,256]{2,1,0:T(8,128)(2,1)} %broadcast_in_dim.80), calls=%async_computation.2 | async-start | bytes 1048576 | tf_op jit(solution)/shard_map/all_to_all | solution.py:475
  37.1 0.8 copy-start.3
  52.2 20.4 %all-to-all-start.3 = ((bf16[32,24,256]{2,1,0:T(8,128)(2,1)}), bf16[32,24,256]{2,1,0:T(8,128)(2,1)S(1)}, u32[]{:S(2)}, u32[]{:S(2)}) async-start(bf16[32,24,256]{2,1,0:T(8,128)(2,1)} %broadcast_in_dim.83), calls=%async_computation.3 | async-start | bytes 786432 | tf_op jit(solution)/shard_map/all_to_all | solution.py:510
  72.7 1.3 %copy-start = (bf16[2304,256]{1,0:T(8,128)(2,1)S(1)}, bf16[2304,256]{1,0:T(8,128)(2,1)}, u32[]{:S(2)}) copy-start(bf16[2304,256]{1,0:T(8,128)(2,1)} %get-tuple-element.116.hidden_ref) | copy-start | bytes 3538948
  73.9 0.9 copy-start.1
  77.5 14.7 %all-to-all-start.4 = ((bf16[32,24,128]{2,1,0:T(8,128)(2,1)}), bf16[32,24,128]{2,1,0:T(8,128)(2,1)S(1)}, u32[]{:S(2)}, u32[]{:S(2)}) async-start(bf16[32,24,128]{2,1,0:T(8,128)(2,1)} %get-tuple-element.118), calls=%async_computation.4 | async-start | bytes 393216 | tf_op jit(solution)/shard_map/all_to_all | solution.py:556
  93.3 10.4 %all-to-all-start.5 = ((f32[8,8,256]{2,1,0:T(8,128)}), f32[8,8,256]{2,1,0:T(8,128)S(1)}, u32[]{:S(2)}, u32[]{:S(2)}) async-start(f32[8,8,256]{2,1,0:T(8,128)} %broadcast_in_dim.86), calls=%async_computation.5 | async-start | bytes 131072 | tf_op jit(solution)/shard_map/all_to_all | solution.py:583

commit v7 on v6

--- a/solution.py
+++ b/solution.py
@@ -9,6 +9,7 @@
 
 BLK = 128
 CHUNK = 1024
+LANES = 128
 BF16 = jnp.bfloat16
 F32 = jnp.float32
 BOTH = ("ent", "rep")
@@ -372,25 +373,34 @@
 
 
 def score_kernel(
-    packed,
-    groups,
     devices,
     sent_ref,
     more_ref,
     rank_ref,
     head_ref,
-    rel_ref,
+    factor_hbm,
+    hidden_hbm,
+    scores_ref,
+    payload_ref,
+    factor_ref,
     hidden_ref,
-    scores_ref,
-    *outs,
+    sems,
 ):
+    copies = (
+        pltpu.make_async_copy(factor_hbm, factor_ref, sems.at[0]),
+        pltpu.make_async_copy(hidden_hbm, hidden_ref, sems.at[1]),
+    )
+    for copy in copies:
+        copy.start()
     slots = sent_ref.shape[0] // devices
     owner = owners(head_ref[...], devices, hidden_ref.shape[0]).astype(jnp.int32)
     place = jnp.where(rank_ref[...] < slots, owner * slots + rank_ref[...], -1)
     picks = one_hot(place, sent_ref.shape[0])
     heads = lax.dot_general(picks, sent_ref[...], TN, preferred_element_type=F32)
     heads = heads + more_ref[...].astype(F32)
-    query = (heads * rel_ref[...]).astype(BF16)
+    for copy in copies:
+        copy.wait()
+    query = (heads * factor_ref[...]).astype(BF16)
     scores = lax.dot_general(query, hidden_ref[...], NT, preferred_element_type=F32)
     scores_ref[...] = scores
     top = jnp.max(scores, axis=1, keepdims=True)
@@ -401,27 +411,75 @@
     total = jnp.sum(weights, axis=1, keepdims=True)
     weighted = jnp.dot(weights.astype(BF16), hidden_ref[...], preferred_element_type=F32)
     total_high = total.astype(BF16).astype(F32)
-    lanes = lax.broadcasted_iota(jnp.int32, (query.shape[0], 128), 1) % 4
+    lanes = lax.broadcasted_iota(jnp.int32, (query.shape[0], LANES), 1) % 4
     wide = jnp.where(lanes == 0, high, total - total_high)
     wide = jnp.where(lanes == 1, low, wide)
     wide = jnp.where(lanes == 2, total_high, wide)
     stats = jnp.transpose(wide)
-    if not packed:
-        weighted_ref, stats_ref = outs
-        weighted_ref[...] = weighted.astype(BF16)
-        stats_ref[...] = stats[: stats_ref.shape[0]].astype(BF16)
-        return
-    (payload_ref,) = outs
-    upper = lax.broadcasted_iota(jnp.int32, (8, 128), 0) < 4
-    figures = jnp.where(upper, stats[:8, :128], stats[:8, 128:])
-    copies = devices // groups
-    share = query.shape[0] // devices
-    for device in range(devices):
-        first = (device % copies * groups + device // copies) * share
-        rows = weighted[first : first + share]
-        payload_ref[device] = jnp.concatenate(
-            [rows[:, :128], rows[:, 128:], figures], axis=0
-        ).astype(BF16)
+    upper = lax.broadcasted_iota(jnp.int32, (8, LANES), 0) < 4
+    figures = jnp.where(upper, stats[:8, :LANES], stats[:8, LANES:])
+    share = query.shape[0] // payload_ref.shape[0]
+    for peer in range(payload_ref.shape[0]):
+        rows = weighted[peer * share : (peer + 1) * share]
+        payload_ref[peer] = pack(rows[:, :LANES], rows[:, LANES:], figures)
+
+
+def pack(left, right, figures):
+    return jnp.concatenate([left, right, figures, figures], axis=0).astype(BF16)
+
+
+def merge(data, first):
+    share = (data.shape[1] - 16) // 2
+    figures = data[:, 2 * share : 2 * share + 8]
+    tops, totals, scales = [], [], []
+    for half in (0, 4):
+        each = figures[:, half : half + 1] + figures[:, half + 1 : half + 2]
+        top = jnp.max(each, axis=0)
+        scale = jnp.exp(each - top[None])
+        total = figures[:, half + 2 : half + 3] + figures[:, half + 3 : half + 4]
+        tops.append(top)
+        totals.append(jnp.sum(total * scale, axis=0))
+        scales.append(scale)
+    left = right = 0.0
+    for i in range(data.shape[0]):
+        scale = jnp.where(first >= LANES, scales[1][i], scales[0][i])
+        factor = column(scale, lax.rem(first, LANES), share)
+        left += factor * data[i, :share]
+        right += factor * data[i, share : 2 * share]
+    return left, right, tops, totals
+
+
+def column(row, first, rows):
+    lanes = lax.broadcasted_iota(jnp.int32, (rows, LANES), 1)
+    wanted = lax.broadcasted_iota(jnp.int32, (rows, LANES), 0) + first
+    return jnp.sum(jnp.where(lanes == wanted, row, 0.0), axis=1, keepdims=True)
+
+
+def merge_kernel(first_ref, received_ref, payload_ref):
+    left, right, tops, totals = merge(received_ref[...].astype(F32), first_ref[0])
+    row = lax.broadcasted_iota(jnp.int32, (8, LANES), 0)
+    figures = jnp.zeros((8, LANES), F32)
+    for half in range(2):
+        for at, value in ((0, tops[half]), (2, totals[half])):
+            high = value.astype(BF16).astype(F32)
+            figures = jnp.where(row == 4 * half + at, high, figures)
+            figures = jnp.where(row == 4 * half + at + 1, value - high, figures)
+    block = pack(left, right, figures)
+    for peer in range(payload_ref.shape[0]):
+        payload_ref[peer] = block
+
+
+def last_kernel(first_ref, received_ref, scores_ref, log_probs_ref, expected_ref):
+    first = first_ref[0]
+    left, right, tops, totals = merge(received_ref[...].astype(F32), first)
+    for half in range(2):
+        norm = column(tops[half] + jnp.log(totals[half]), 0, LANES)
+        rows = pl.ds(half * LANES, LANES)
+        log_probs_ref[rows, :] = scores_ref[rows, :] - norm
+    total = jnp.where(first >= LANES, totals[1], totals[0])
+    total = column(total, lax.rem(first, LANES), left.shape[0])
+    expected_ref[:, :LANES] = left / total
+    expected_ref[:, LANES:] = right / total
 
 
 def body(
@@ -447,15 +505,9 @@
     device = group * copies + member
     rows_dev, columns = entity_emb.shape
     queries = query_head.shape[0]
-    batch_rows = queries // copies
-    share = -(-batch_rows // groups)
-    padded = share * devices
 
     blocks = edge_src.shape[0]
     relations = relation_emb.shape[0]
-    rel_count = -(-relations // 256) * 256
-    relation_t = jnp.pad(relation_emb, ((0, rel_count - relations), (0, 0))).T
-    near_t = entity_emb.T
     ahead = min(AHEAD, blocks // STEP)
 
     slots = export_rows.shape[1]
@@ -466,6 +518,10 @@
         out_specs=WHOLE,
         compiler_params=pltpu.CompilerParams(vmem_limit_bytes=VMEM_LIMIT),
     )((member * rows_dev)[None], export_rows, entity_emb)
+    offered, later_relation = lax.optimization_barrier((offered, relation_emb))
+    rel_count = -(-relations // 256) * 256
+    relation_t = jnp.pad(later_relation, ((0, rel_count - relations), (0, 0))).T
+    near_t = entity_emb.T
     pieces = lax.all_to_all(offered, "rep", 0, 0, tiled=True)
     mine = jnp.sum(
         pieces.reshape(copies, slots // copies, columns).astype(F32), axis=0
@@ -538,52 +594,42 @@
         (jnp.int32(1), jnp.zeros((queries, columns), BF16)),
     )
 
-    packed = share == 8 and share * devices == queries and (queries, columns) == (256, 256)
-    score_type = jax.ShapeDtypeStruct((queries, rows_dev), F32)
-    if packed:
-        more = (jax.ShapeDtypeStruct((devices, 24, 128), BF16),)
-    else:
-        more = (
-            jax.ShapeDtypeStruct((queries, columns), BF16),
-            jax.ShapeDtypeStruct((16, queries), BF16),
-        )
-    scores, *parts = pl.pallas_call(
-        functools.partial(score_kernel, packed, groups, devices),
-        out_shape=(score_type,) + more,
-        compiler_params=pltpu.CompilerParams(vmem_limit_bytes=SCORE_LIMIT),
+    batch_rows = queries // copies
+    first = (member * batch_rows)[None]
+    part = (2 * batch_rows + 16, LANES)
+    few = pltpu.CompilerParams(vmem_limit_bytes=SCORE_LIMIT)
+    scores, payload = pl.pallas_call(
+        functools.partial(score_kernel, devices),
+        out_shape=(
+            jax.ShapeDtypeStruct((queries, rows_dev), F32),
+            jax.ShapeDtypeStruct((copies,) + part, BF16),
+        ),
+        in_specs=[WHOLE] * 4 + [HBM] * 2,
+        out_specs=(WHOLE, WHOLE),
+        scratch_shapes=[
+            pltpu.VMEM((queries, columns), F32),
+            pltpu.VMEM((rows_dev, columns), BF16),
+            pltpu.SemaphoreType.DMA((2,)),
+        ],
+        compiler_params=few,
     )(sent, more_heads, rank, head_row, query_factor, hidden)
-    if packed:
-        received = lax.all_to_all(parts[0], BOTH, 0, 0).astype(F32)
-        sums = jnp.concatenate([received[:, :8], received[:, 8:16]], axis=2)
-        figures = jnp.concatenate([received[:, 16:20], received[:, 20:24]], axis=2)
-    else:
-        split = parts[0].reshape(copies, batch_rows, columns)
-        split = jnp.pad(split, ((0, 0), (0, share * groups - batch_rows), (0, 0)))
-        split = split.reshape(copies, groups, share, columns).transpose(1, 0, 2, 3)
-        split = split.reshape(devices, share * columns)
-        figures = parts[1][:4].reshape(1, 4 * queries)
-        figures = jnp.broadcast_to(figures, (devices, 4 * queries))
-        payload = jnp.concatenate([split, figures], axis=1).reshape(devices, -1, 128)
-        received = lax.all_to_all(payload, BOTH, 0, 0).reshape(devices, -1).astype(F32)
-        sums = received[:, : share * columns].reshape(devices, share, columns)
-        figures = received[:, share * columns :].reshape(devices, 4, queries)
-    tops = figures[:, 0] + figures[:, 1]
-    totals = figures[:, 2] + figures[:, 3]
-    row_top = jnp.max(tops, axis=0)
-    scale = jnp.exp(tops - row_top)
-    row_total = jnp.sum(totals * scale, axis=0)
-    factor = jnp.pad(
-        (scale / row_total).reshape(devices, copies, batch_rows),
-        ((0, 0), (0, 0), (0, share * groups - batch_rows)),
-    ).reshape(devices, -1)
-    own_factor = lax.dynamic_slice_in_dim(
-        factor, (member * groups + group) * share, share, 1
-    )
-    own_expected = jnp.sum(sums * own_factor[:, :, None], axis=0)
-    expected_tail = lax.all_to_all(
-        jnp.broadcast_to(own_expected[None], (groups, share, columns)), "ent", 0, 0
-    ).reshape(groups * share, columns)[:batch_rows]
-    log_probs = scores - (row_top + jnp.log(row_total))[:, None]
+    payload = pl.pallas_call(
+        merge_kernel,
+        out_shape=jax.ShapeDtypeStruct((groups,) + part, BF16),
+        in_specs=[SMEM, WHOLE],
+        out_specs=WHOLE,
+        compiler_params=few,
+    )(first, lax.all_to_all(payload, "rep", 0, 0))
+    log_probs, expected_tail = pl.pallas_call(
+        last_kernel,
+        out_shape=(
+            jax.ShapeDtypeStruct((queries, rows_dev), F32),
+            jax.ShapeDtypeStruct((batch_rows, columns), F32),
+        ),
+        in_specs=[SMEM, WHOLE, WHOLE],
+        out_specs=(WHOLE, WHOLE),
+        compiler_params=few,
+    )(first, lax.all_to_all(payload, "ent", 0, 0), scores)
     return (log_probs, expected_tail)
 
 

time: 105 us -> 103 us (0.981)
  blocking collectives: 0 us -> 15.6 us
  waiting for transfers between devices: 16.1 us -> 6.61 us
  starting transfers between devices: 24.6 us -> 18.8 us
  local copies, waits for them, and re-layouts: 9.52 us -> 7.08 us
  Pallas kernels: 50.6 us -> 53 us
  other arithmetic: 1.98 us -> 0.02 us
    all_to_all x0 -> x1, blocking collectives: none -> 15.6 us  [body(): lax.all_to_all(payload, 'ent', 0, 0)]
    all_to_all x2 -> x1, waiting for transfers between devices: 14.2 us -> 4.77 us  [body(): lax.all_to_all(payload, 'rep', 0, 0)]
    all_to_all x2 -> x1, starting transfers between devices: 9.18 us -> 3.35 us  [body(): lax.all_to_all(payload, 'rep', 0, 0)]
    pallas_call x1 -> x3, Pallas kernels: 2.59 us -> 4.83 us  [the longest x1 2.96 us: body(): pl.pallas_call(functools.partial(score_kernel, devices), out_shape=(jax.S...]
    unnamed x13, local copies, waits for them, and re-layouts: 6.38 us -> 4.57 us
    sub x1 -> x0, other arithmetic: 1.63 us -> none  [body(): log_probs = scores - (row_top + jnp.log(row_total))[:, None]]
  transfers between devices with their start and end apart: 5 -> 4, of which waited for: 3 -> 2; matrix products, arithmetic and copies ran while one was open for 4% -> 2% of each run, Pallas kernels for 31% -> 32%
where the time goes in v7:
time: 103 us
  Pallas kernels  53 us (51%)
  starting transfers between devices  18.8 us (18%)
  blocking collectives  15.6 us (15%)
  local copies, waits for them, and re-layouts  7.08 us (7%)
  waiting for transfers between devices  6.61 us (6%)
    pallas_call x2, Pallas kernels, far_call(): pl.pallas_call(functools.partial(far_kernel, half_rel, last, ahead, devic...  27.5 us
    pallas_call x1, Pallas kernels, near_call(): pl.pallas_call(functools.partial(near_kernel, ahead), out_shape=(jax.Shap...  18.3 us
    all_to_all x1, blocking collectives, body(): lax.all_to_all(payload, 'ent', 0, 0)  15.6 us
    all_to_all x1, starting transfers between devices, send_round(): return lax.all_to_all(spread, BOTH, 0, 0).reshape(devices * cap, columns)  5.83 us
    all_to_all x1, starting transfers between devices, body(): table = lax.all_to_all(spread, BOTH, 0, 0).reshape(groups * slots, columns)  5.42 us
    all_to_all x1, waiting for transfers between devices, body(): lax.all_to_all(payload, 'rep', 0, 0)  4.77 us
    unnamed x13, local copies, waits for them, and re-layouts  4.57 us
    all_to_all x1, starting transfers between devices, body(): pieces = lax.all_to_all(offered, 'rep', 0, 0, tiled=True)  4.22 us
  transfers between devices with their start and end apart: 4, of which 2 were waited for; matrix products, arithmetic and copies ran while one was open for 2% of the time, Pallas kernels for 32%

profile of v7, /device:TPU:0, one launch (start us, length us, event | category | flops | bytes accessed | tf_op | source)
XLA Modules:
  0.0 102.6 jit_solution(8437556545036757222)
XLA Ops:
  0.6 0.0 copy-start.4
  0.6 0.0 copy-start.2
  0.7 2.4 %shard_map.140 = bf16[128,256]{1,0:T(8,128)(2,1)} custom-call(s32[1]{0:T(128)} %bitcast.8.base_ref, s32[1,128]{1,0:T(1,128)} %index_ref.1, bf16[2304,256]{1,0:T(8,128)(2,1)} %emb_ref.5), custom_call_target="tpu_custom_call" | custom-call | tf_op jit(solution)/shard_map/pallas_call | solution.py:514
  3.1 0.0 copy-done.4
  3.1 0.1 copy.17
  3.2 4.2 %all-to-all-start.1 = ((bf16[4,32,256]{2,1,0:T(8,128)(2,1)}), bf16[4,32,256]{2,1,0:T(8,128)(2,1)S(1)}, u32[]{:S(2)}, u32[]{:S(2)}) async-start(bf16[4,32,256]{2,1,0:T(8,128)(2,1)} %bitcast.41), calls=%async_computation.1 | async-start | bytes 131072 | tf_op jit(solution)/shard_map/all_to_all | solution.py:525
  7.4 0.7 pad_bitcast_fusion.relation_ref.rest_2_
  8.2 0.0 copy-done.2
  8.2 0.0 copy-start.5
  8.2 1.5 %copy.16 = bf16[2304,256]{0,1:T(8,128)(2,1)} copy(bf16[2304,256]{1,0:T(8,128)(2,1)S(1)} %copy-done.2) | data formatting | bytes 2359296 | tf_op args[0]
  9.7 0.0 copy-done.5
  9.7 1.8 %all-to-all-done.1 = bf16[4,32,256]{2,1,0:T(8,128)(2,1)S(1)} async-done(((bf16[4,32,256]{2,1,0:T(8,128)(2,1)}), bf16[4,32,256]{2,1,0:T(8,128)(2,1)S(1)}, u32[]{:S(2)}, u32[]{:S(2)}) %all-to-all-start.1) | async-done | bytes 65568 | tf_op jit(solution)/shard_map/all_to_all | solution.py:525
  11.6 0.8 broadcast_in_dim.74
  12.4 5.4 %all-to-all-start.2 = ((bf16[32,32,256]{2,1,0:T(8,128)(2,1)}), bf16[32,32,256]{2,1,0:T(8,128)(2,1)S(1)}, u32[]{:S(2)}, u32[]{:S(2)}) async-start(bf16[32,32,256]{2,1,0:T(8,128)(2,1)} %broadcast_in_dim.74), calls=%async_computation.2 | async-start | bytes 1048576 | tf_op jit(solution)/shard_map/all_to_all | solution.py:531
  17.8 18.3 %shard_map.141 = (bf16[9,2,256,768]{3,2,1,0:T(8,128)(2,1)}, s32[20]{0:T(128)}) custom-call(s32[1]{0:T(128)} %bitcast.7.base_ref, s32[256]{0:T(256)S(1)} %copy-done.5, s32[18,768]{1,0:T(8,128)} %src_ref.5, s32[18,768]{1,0:T(8,128)} %rel_ref.5, bf16[256,2304]{1,0:T(8,128)(2,1)} %bitcast.37, bf16[256,512]{1,0:T(8,128)(2,1)} %pad_bitcast_fusion.relation_ref.rest_2_), custom_call_target="tpu_custom_call" | custom-call | flops 13287555072 | bytes 4718592 | tf_op jit(solution)/shard_map/pallas_call | solution.py:327
  36.1 0.0 all-to-all-done.2
  36.1 0.0 copy-start.3
  36.2 0.8 copy-done.3
  37.0 12.9 %shard_map.142 = (bf16[2304,256]{1,0:T(8,128)(2,1)}, bf16[264,256]{1,0:T(8,128)(2,1)S(1)}, s32[1,256]{1,0:T(1,128)S(1)}, s32[1]{0:T(128)}) custom-call(s32[1]{0:T(128)} %bitcast.7.base_ref, s32[20]{0:T(128)} %get-tuple-element.111.order_ref, s32[18,768]{1,0:T(8,128)} %src_ref.5, s32[18,768]{1,0:T(8,128)} %dst_ref.3, s32[18,768]{1,0:T(8,128)} %rel_ref.5, ...), custom_call_target="tpu_custom_call" | custom-call | flops 3623878656 | bytes 3538944 | tf_op jit(solution)/shard_map/pallas_call | solution.py:349
  49.9 0.7 while.12
  50.6 0.8 broadcast_in_dim.77
  51.4 5.8 %all-to-all-start.3 = ((bf16[32,24,256]{2,1,0:T(8,128)(2,1)}), bf16[32,24,256]{2,1,0:T(8,128)(2,1)S(1)}, u32[]{:S(2)}, u32[]{:S(2)}) async-start(bf16[32,24,256]{2,1,0:T(8,128)(2,1)} %broadcast_in_dim.77), calls=%async_computation.3 | async-start | bytes 786432 | tf_op jit(solution)/shard_map/all_to_all | solution.py:566
  57.2 14.6 %shard_map.143 = (bf16[2304,256]{1,0:T(8,128)(2,1)}, f32[256,256]{1,0:T(8,128)}) custom-call(s32[1]{0:T(128)} %bitcast.7.base_ref, s32[20]{0:T(128)} %get-tuple-element.111.order_ref, s32[18,768]{1,0:T(8,128)} %src_ref.5, s32[18,768]{1,0:T(8,128)} %dst_ref.3, s32[18,768]{1,0:T(8,128)} %rel_ref.5, ...), custom_call_target="tpu_custom_call", output_to_operand_aliasing={{0}: (15, {})} | custom-call | flops 3623878656 | bytes 3538944 | tf_op jit(solution)/shard_map/pallas_call | solution.py:349
  71.8 0.0 all-to-all-done.3
  71.8 0.0 copy-start
  71.8 1.3 %copy-done = bf16[2304,256]{1,0:T(8,128)(2,1)S(1)} copy-done((bf16[2304,256]{1,0:T(8,128)(2,1)S(1)}, bf16[2304,256]{1,0:T(8,128)(2,1)}, u32[]{:S(2)}) %copy-start) | copy-done | bytes 1179672
  73.1 0.0 copy-start.1
  73.1 0.9 copy-done.1
  74.0 3.0 %shard_map.144 = (f32[256,2304]{1,0:T(8,128)S(1)}, bf16[4,144,128]{2,1,0:T(8,128)(2,1)}) custom-call(bf16[768,256]{1,0:T(8,128)(2,1)S(1)} %bitcast.35, bf16[256,256]{1,0:T(8,128)(2,1)S(1)} %get-tuple-element.117.more_ref, s32[1,256]{1,0:T(1,128)S(1)} %get-tuple-element.244, s32[1,256]{1,0:T(1,128)S(1)} %bitcast.49, f32[256,256]{1,0:T(8,128)S(1)} %copy-done.1, ...), custom_call_target="tpu_custom_call" | custom-call | tf_op jit(solution)/shard_map/pallas_call | solution.py:601
  77.0 3.3 %all-to-all-start.4 = ((bf16[4,144,128]{2,1,0:T(8,128)(2,1)}), bf16[4,144,128]{2,1,0:T(8,128)(2,1)S(1)}, u32[]{:S(2)}, u32[]{:S(2)}) async-start(bf16[4,144,128]{2,1,0:T(8,128)(2,1)} %get-tuple-element.121), calls=%async_computation.4 | async-start | bytes 294912 | tf_op jit(solution)/shard_map/all_to_all | solution.py:622
  80.3 4.8 %all-to-all-done.4.received_ref = bf16[4,144,128]{2,1,0:T(8,128)(2,1)S(1)} async-done(((bf16[4,144,128]{2,1,0:T(8,128)(2,1)}), bf16[4,144,128]{2,1,0:T(8,128)(2,1)S(1)}, u32[]{:S(2)}, u32[]{:S(2)}) %all-to-all-start.4) | async-done | bytes 147488 | tf_op jit(solution)/shard_map/all_to_all | solution.py:622
  85.1 0.1 shard_map.145
  85.2 15.6 %all_to_all.38.received_ref = bf16[8,144,128]{2,1,0:T(8,128)(2,1)S(1)} all-to-all(bf16[8,144,128]{2,1,0:T(8,128)(2,1)S(1)} %shard_map.145), channel_id=1, replica_groups=mesh['ent'=8,'rep'=4] {'ent'}, dimensions={0} | all-to-all | bytes 589824 | tf_op jit(solution)/shard_map/all_to_all | solution.py:632
  100.8 1.7 %shard_map.146 = (f32[256,2304]{1,0:T(8,128)}, f32[64,256]{1,0:T(8,128)}) custom-call(s32[1]{0:T(128)} %bitcast.6.first_ref, bf16[8,144,128]{2,1,0:T(8,128)(2,1)S(1)} %all_to_all.38.received_ref, f32[256,2304]{1,0:T(8,128)S(1)} %get-tuple-element.122.scores_ref), custom_call_target="tpu_custom_call" | custom-call | tf_op jit(solution)/shard_map/pallas_call | solution.py:623
  (4 shorter events, 0.0 us)
Async XLA Ops:
  0.6 2.4 %copy-start.4 = (bf16[474,256]{1,0:T(8,128)(2,1)S(1)}, bf16[474,256]{1,0:T(8,128)(2,1)}, u32[]{:S(2)}) copy-start(bf16[474,256]{1,0:T(8,128)(2,1)} %param.16) | copy-start | bytes 728068
  0.6 7.5 %copy-start.2 = (bf16[2304,256]{1,0:T(8,128)(2,1)S(1)}, bf16[2304,256]{1,0:T(8,128)(2,1)}, u32[]{:S(2)}) copy-start(bf16[2304,256]{1,0:T(8,128)(2,1)} %emb_ref.5) | copy-start | bytes 3538948
  3.2 8.3 %all-to-all-start.1 = ((bf16[4,32,256]{2,1,0:T(8,128)(2,1)}), bf16[4,32,256]{2,1,0:T(8,128)(2,1)S(1)}, u32[]{:S(2)}, u32[]{:S(2)}) async-start(bf16[4,32,256]{2,1,0:T(8,128)(2,1)} %bitcast.41), calls=%async_computation.1 | async-start | bytes 131072 | tf_op jit(solution)/shard_map/all_to_all | solution.py:525
  8.2 1.5 %copy-start.5 = (s32[256]{0:T(256)S(1)}, s32[256]{0:T(256)}, u32[]{:S(2)}) copy-start(s32[256]{0:T(256)} %head_ref.1) | copy-start | bytes 3076
  12.4 23.7 %all-to-all-start.2 = ((bf16[32,32,256]{2,1,0:T(8,128)(2,1)}), bf16[32,32,256]{2,1,0:T(8,128)(2,1)S(1)}, u32[]{:S(2)}, u32[]{:S(2)}) async-start(bf16[32,32,256]{2,1,0:T(8,128)(2,1)} %broadcast_in_dim.74), calls=%async_computation.2 | async-start | bytes 1048576 | tf_op jit(solution)/shard_map/all_to_all | solution.py:531
  36.1 0.8 copy-start.3
  51.4 20.4 %all-to-all-start.3 = ((bf16[32,24,256]{2,1,0:T(8,128)(2,1)}), bf16[32,24,256]{2,1,0:T(8,128)(2,1)S(1)}, u32[]{:S(2)}, u32[]{:S(2)}) async-start(bf16[32,24,256]{2,1,0:T(8,128)(2,1)} %broadcast_in_dim.77), calls=%async_computation.3 | async-start | bytes 786432 | tf_op jit(solution)/shard_map/all_to_all | solution.py:566
  71.8 1.3 %copy-start = (bf16[2304,256]{1,0:T(8,128)(2,1)S(1)}, bf16[2304,256]{1,0:T(8,128)(2,1)}, u32[]{:S(2)}) copy-start(bf16[2304,256]{1,0:T(8,128)(2,1)} %get-tuple-element.120.hidden_hbm) | copy-start | bytes 3538948
  73.1 0.9 copy-start.1
  77.0 8.1 %all-to-all-start.4 = ((bf16[4,144,128]{2,1,0:T(8,128)(2,1)}), bf16[4,144,128]{2,1,0:T(8,128)(2,1)S(1)}, u32[]{:S(2)}, u32[]{:S(2)}) async-start(bf16[4,144,128]{2,1,0:T(8,128)(2,1)} %get-tuple-element.121), calls=%async_computation.4 | async-start | bytes 294912 | tf_op jit(solution)/shard_map/all_to_all | solution.py:622

commit v8 on v7

--- a/solution.py
+++ b/solution.py
@@ -19,6 +19,8 @@
 STEP = 2
 AHEAD = 6
 SCORE_LIMIT = 24 * 2**20
+FAR_LIMIT = 56 * 2**20
+FIRST_LIMIT = 56 * 2**20
 
 
 def one_hot(index, rows):
@@ -146,7 +148,7 @@
         near_ref, query_rel_ref, relation_ref, rel_weight_ref, _ = rest[:5]
         hidden_ref, factor_ref = rest[5:7]
     else:
-        head_ref, mixed_ref, hidden_ref, heads_ref, rank_ref, most_ref = rest[:6]
+        head_ref, mixed_ref, hidden_ref, heads_ref, sent_ref, rank_ref, most_ref = rest[:7]
     blocks = src_ref.shape[0]
     rows_dev = blocks * BLK
     far_chunks = far_ref.shape[0]
@@ -295,7 +297,10 @@
         rows = lax.dot_general(picks, made_ref[...], TN, preferred_element_type=F32)
         rank = ranks(owners(head_ref[...], devices, rows_dev))
         slots = one_hot(rank.astype(jnp.int32), heads_ref.shape[0])
-        heads_ref[...] = jnp.dot(slots, rows.astype(BF16), preferred_element_type=F32).astype(BF16)
+        packed = jnp.dot(slots, rows.astype(BF16), preferred_element_type=F32)
+        heads_ref[...] = packed.astype(BF16)
+        for peer in range(devices):
+            sent_ref[peer] = packed[: sent_ref.shape[1]].astype(BF16)
         rank_ref[...] = rank.astype(jnp.int32)
         most_ref[0] = jnp.max(rank).astype(jnp.int32)
 
@@ -350,7 +355,7 @@
         functools.partial(far_kernel, half_rel, last, ahead, devices),
         out_shape=(jax.ShapeDtypeStruct((rows_dev, columns), BF16),) + outs,
         in_specs=[SMEM] * 2 + [WHOLE] * 3 + [HBM] + [WHOLE] * (5 + len(more)) + [HBM],
-        out_specs=(HBM, WHOLE) if last else (HBM, WHOLE, WHOLE, SMEM),
+        out_specs=(HBM, WHOLE) if last else (HBM, WHOLE, WHOLE, WHOLE, SMEM),
         input_output_aliases={11 + len(more): 0} if last else {},
         scratch_shapes=[
             pltpu.VMEM((far.shape[0], columns, CHUNK), BF16),
@@ -363,7 +368,7 @@
             pltpu.SemaphoreType.DMA((2, STEP)),
             pltpu.SemaphoreType.DMA((blocks,)),
         ],
-        compiler_params=pltpu.CompilerParams(vmem_limit_bytes=VMEM_LIMIT),
+        compiler_params=pltpu.CompilerParams(vmem_limit_bytes=FAR_LIMIT),
         cost_estimate=pl.CostEstimate(
             flops=blocks * width * columns * far.shape[0] * CHUNK,
             bytes_accessed=blocks * width * columns,
@@ -541,7 +546,7 @@
     weights = (in_weight, out_weight, loop_weight, loop_rel[None])
     edges = (edge_src, edge_dst, edge_rel)
     cap = min(queries, -(-3 * queries // (8 * devices)) * 8)
-    hidden, heads, rank, most = far_call(
+    hidden, heads, spread, rank, most = far_call(
         relations // 2,
         False,
         ahead,
@@ -555,6 +560,7 @@
         mixed,
         (
             jax.ShapeDtypeStruct((-(-queries // cap) * cap, columns), BF16),
+            jax.ShapeDtypeStruct((devices, cap, columns), BF16),
             jax.ShapeDtypeStruct((1, queries), jnp.int32),
             jax.ShapeDtypeStruct((1,), jnp.int32),
         ),
@@ -573,7 +579,7 @@
         inside = (slot >= 0) & (slot < cap)
         return turn + 1, jnp.where(inside[:, None], rows, more)
 
-    sent = send_round(0)
+    sent = lax.all_to_all(spread, BOTH, 0, 0).reshape(devices * cap, columns)
     hidden, query_factor = far_call(
         relations // 2,
         True,
@@ -611,7 +617,7 @@
             pltpu.VMEM((rows_dev, columns), BF16),
             pltpu.SemaphoreType.DMA((2,)),
         ],
-        compiler_params=few,
+        compiler_params=pltpu.CompilerParams(vmem_limit_bytes=FIRST_LIMIT),
     )(sent, more_heads, rank, head_row, query_factor, hidden)
     payload = pl.pallas_call(
         merge_kernel,

time: 103 us -> 105 us (1.019)
  Pallas kernels: 53 us -> 55 us
    pallas_call x1, Pallas kernels: 2.96 us -> 4.73 us  [body(): pl.pallas_call(functools.partial(score_kernel, devices), out_shape=(jax.S...]
  transfers between devices with their start and end apart: 4 -> 4, of which waited for: 2 -> 2; matrix products, arithmetic and copies ran while one was open for 2% -> 2% of each run, Pallas kernels for 32% -> 31%
where the time goes in v8:
time: 105 us
  Pallas kernels  55 us (52%)
  starting transfers between devices  19.8 us (19%)
  blocking collectives  15.6 us (15%)
  waiting for transfers between devices  6.65 us (6%)
  local copies, waits for them, and re-layouts  6.46 us (6%)
    pallas_call x2, Pallas kernels, far_call(): pl.pallas_call(functools.partial(far_kernel, half_rel, last, ahead, devic...  27.7 us
    pallas_call x1, Pallas kernels, near_call(): pl.pallas_call(functools.partial(near_kernel, ahead), out_shape=(jax.Shap...  18.3 us
    all_to_all x1, blocking collectives, body(): lax.all_to_all(payload, 'ent', 0, 0)  15.6 us
    all_to_all x1, starting transfers between devices, body(): sent = lax.all_to_all(spread, BOTH, 0, 0).reshape(devices * cap, columns)  6.86 us
    all_to_all x1, starting transfers between devices, body(): table = lax.all_to_all(spread, BOTH, 0, 0).reshape(groups * slots, columns)  5.42 us
    all_to_all x1, waiting for transfers between devices, body(): lax.all_to_all(payload, 'rep', 0, 0)  4.77 us
    unnamed x13, local copies, waits for them, and re-layouts  4.76 us
    pallas_call x1, Pallas kernels, body(): pl.pallas_call(functools.partial(score_kernel, devices), out_shape=(jax.S...  4.73 us
  transfers between devices with their start and end apart: 4, of which 2 were waited for; matrix products, arithmetic and copies ran while one was open for 2% of the time, Pallas kernels for 31%

profile of v8, /device:TPU:0, one launch (start us, length us, event | category | flops | bytes accessed | tf_op | source)
XLA Modules:
  0.0 104.9 jit_solution(4692924644465119010)
XLA Ops:
  0.6 0.0 copy-start.4
  0.6 0.0 copy-start.1
  0.7 2.4 %shard_map.140 = bf16[128,256]{1,0:T(8,128)(2,1)} custom-call(s32[1]{0:T(128)} %bitcast.8.base_ref, s32[1,128]{1,0:T(1,128)} %index_ref.1, bf16[2304,256]{1,0:T(8,128)(2,1)} %emb_ref.5), custom_call_target="tpu_custom_call" | custom-call | tf_op jit(solution)/shard_map/pallas_call | solution.py:519
  3.1 0.0 copy-done.4
  3.1 0.1 copy.17
  3.2 4.2 %all-to-all-start.1 = ((bf16[4,32,256]{2,1,0:T(8,128)(2,1)}), bf16[4,32,256]{2,1,0:T(8,128)(2,1)S(1)}, u32[]{:S(2)}, u32[]{:S(2)}) async-start(bf16[4,32,256]{2,1,0:T(8,128)(2,1)} %bitcast.41), calls=%async_computation.1 | async-start | bytes 131072 | tf_op jit(solution)/shard_map/all_to_all | solution.py:530
  7.4 0.7 pad_bitcast_fusion.relation_ref.rest_2_
  8.1 0.0 copy-done.1
  8.1 0.0 copy-start.5
  8.1 1.5 %copy.16 = bf16[2304,256]{0,1:T(8,128)(2,1)} copy(bf16[2304,256]{1,0:T(8,128)(2,1)S(1)} %copy-done.1) | data formatting | bytes 2359296 | tf_op args[0]
  9.7 0.0 copy-done.5
  9.7 1.9 %all-to-all-done.1 = bf16[4,32,256]{2,1,0:T(8,128)(2,1)S(1)} async-done(((bf16[4,32,256]{2,1,0:T(8,128)(2,1)}), bf16[4,32,256]{2,1,0:T(8,128)(2,1)S(1)}, u32[]{:S(2)}, u32[]{:S(2)}) %all-to-all-start.1) | async-done | bytes 65568 | tf_op jit(solution)/shard_map/all_to_all | solution.py:530
  11.6 0.8 broadcast_in_dim.68
  12.4 5.4 %all-to-all-start.2 = ((bf16[32,32,256]{2,1,0:T(8,128)(2,1)}), bf16[32,32,256]{2,1,0:T(8,128)(2,1)S(1)}, u32[]{:S(2)}, u32[]{:S(2)}) async-start(bf16[32,32,256]{2,1,0:T(8,128)(2,1)} %broadcast_in_dim.68), calls=%async_computation.2 | async-start | bytes 1048576 | tf_op jit(solution)/shard_map/all_to_all | solution.py:536
  17.8 18.3 %shard_map.141 = (bf16[9,2,256,768]{3,2,1,0:T(8,128)(2,1)}, s32[20]{0:T(128)}) custom-call(s32[1]{0:T(128)} %bitcast.7.base_ref, s32[256]{0:T(256)S(1)} %copy-done.5, s32[18,768]{1,0:T(8,128)} %src_ref.5, s32[18,768]{1,0:T(8,128)} %rel_ref.5, bf16[256,2304]{1,0:T(8,128)(2,1)} %bitcast.37, bf16[256,512]{1,0:T(8,128)(2,1)} %pad_bitcast_fusion.relation_ref.rest_2_), custom_call_target="tpu_custom_call" | custom-call | flops 13287555072 | bytes 4718592 | tf_op jit(solution)/shard_map/pallas_call | solution.py:332
  36.1 0.0 all-to-all-done.2
  36.1 0.0 copy-start.3
  36.2 0.8 copy-done.3
  37.0 13.2 %shard_map.142 = (bf16[2304,256]{1,0:T(8,128)(2,1)}, bf16[264,256]{1,0:T(8,128)(2,1)S(1)}, bf16[32,24,256]{2,1,0:T(8,128)(2,1)}, s32[1,256]{1,0:T(1,128)S(1)}, s32[1]{0:T(128)}) custom-call(s32[1]{0:T(128)} %bitcast.7.base_ref, s32[20]{0:T(128)} %get-tuple-element.112.order_ref, s32[18,768]{1,0:T(8,128)} %src_ref.5, s32[18,768]{1,0:T(8,128)} %dst_ref.3, ...), custom_call_target="tpu_custom_call" | custom-call | flops 3623878656 | bytes 3538944 | tf_op jit(solution)/shard_map/pallas_call | solution.py:354
  50.2 0.6 while.12
  50.7 6.9 %all-to-all-start.3 = ((bf16[32,24,256]{2,1,0:T(8,128)(2,1)}), bf16[32,24,256]{2,1,0:T(8,128)(2,1)S(1)}, u32[]{:S(2)}, u32[]{:S(2)}) async-start(bf16[32,24,256]{2,1,0:T(8,128)(2,1)} %get-tuple-element.115), calls=%async_computation.3 | async-start | bytes 786432 | tf_op jit(solution)/shard_map/all_to_all | solution.py:582
  57.6 14.5 %shard_map.143 = (bf16[2304,256]{1,0:T(8,128)(2,1)}, f32[256,256]{1,0:T(8,128)}) custom-call(s32[1]{0:T(128)} %bitcast.7.base_ref, s32[20]{0:T(128)} %get-tuple-element.112.order_ref, s32[18,768]{1,0:T(8,128)} %src_ref.5, s32[18,768]{1,0:T(8,128)} %dst_ref.3, s32[18,768]{1,0:T(8,128)} %rel_ref.5, ...), custom_call_target="tpu_custom_call", output_to_operand_aliasing={{0}: (15, {})} | custom-call | flops 3623878656 | bytes 3538944 | tf_op jit(solution)/shard_map/pallas_call | solution.py:354
  72.2 0.0 all-to-all-done.3
  72.2 0.0 copy-start.2
  72.2 0.7 copy-done.2
  72.9 4.7 %shard_map.144 = (f32[256,2304]{1,0:T(8,128)}, bf16[4,144,128]{2,1,0:T(8,128)(2,1)}) custom-call(bf16[768,256]{1,0:T(8,128)(2,1)} %bitcast.36, bf16[256,256]{1,0:T(8,128)(2,1)S(1)} %get-tuple-element.119.more_ref, s32[1,256]{1,0:T(1,128)S(1)} %get-tuple-element.248, s32[1,256]{1,0:T(1,128)S(1)} %bitcast.49, f32[256,256]{1,0:T(8,128)} %get-tuple-element.121.factor_hbm, ...), custom_call_target="tpu_custom_call" | custom-call | tf_op jit(solution)/shard_map/pallas_call | solution.py:607
  77.7 3.3 %all-to-all-start.4 = ((bf16[4,144,128]{2,1,0:T(8,128)(2,1)}), bf16[4,144,128]{2,1,0:T(8,128)(2,1)S(1)}, u32[]{:S(2)}, u32[]{:S(2)}) async-start(bf16[4,144,128]{2,1,0:T(8,128)(2,1)} %get-tuple-element.123), calls=%async_computation.4 | async-start | bytes 294912 | tf_op jit(solution)/shard_map/all_to_all | solution.py:628
  81.0 4.8 %all-to-all-done.4.received_ref = bf16[4,144,128]{2,1,0:T(8,128)(2,1)S(1)} async-done(((bf16[4,144,128]{2,1,0:T(8,128)(2,1)}), bf16[4,144,128]{2,1,0:T(8,128)(2,1)S(1)}, u32[]{:S(2)}, u32[]{:S(2)}) %all-to-all-start.4) | async-done | bytes 147488 | tf_op jit(solution)/shard_map/all_to_all | solution.py:628
  85.8 0.1 shard_map.145
  85.9 15.6 %all_to_all.38.received_ref = bf16[8,144,128]{2,1,0:T(8,128)(2,1)S(1)} all-to-all(bf16[8,144,128]{2,1,0:T(8,128)(2,1)S(1)} %shard_map.145), channel_id=1, replica_groups=mesh['ent'=8,'rep'=4] {'ent'}, dimensions={0} | all-to-all | bytes 589824 | tf_op jit(solution)/shard_map/all_to_all | solution.py:638
  101.5 0.0 copy-start
  101.5 1.7 %copy-done = f32[256,2304]{1,0:T(8,128)S(1)} copy-done((f32[256,2304]{1,0:T(8,128)S(1)}, f32[256,2304]{1,0:T(8,128)}, u32[]{:S(2)}) %copy-start) | copy-done | bytes 2359320
  103.2 1.7 %shard_map.146 = (f32[256,2304]{1,0:T(8,128)}, f32[64,256]{1,0:T(8,128)}) custom-call(s32[1]{0:T(128)} %bitcast.6.first_ref, bf16[8,144,128]{2,1,0:T(8,128)(2,1)S(1)} %all_to_all.38.received_ref, f32[256,2304]{1,0:T(8,128)S(1)} %copy-done), custom_call_target="tpu_custom_call" | custom-call | tf_op jit(solution)/shard_map/pallas_call | solution.py:629
  (3 shorter events, 0.0 us)
Async XLA Ops:
  0.6 2.4 %copy-start.4 = (bf16[474,256]{1,0:T(8,128)(2,1)S(1)}, bf16[474,256]{1,0:T(8,128)(2,1)}, u32[]{:S(2)}) copy-start(bf16[474,256]{1,0:T(8,128)(2,1)} %param.16) | copy-start | bytes 728068
  0.6 7.5 %copy-start.1 = (bf16[2304,256]{1,0:T(8,128)(2,1)S(1)}, bf16[2304,256]{1,0:T(8,128)(2,1)}, u32[]{:S(2)}) copy-start(bf16[2304,256]{1,0:T(8,128)(2,1)} %emb_ref.5) | copy-start | bytes 3538948
  3.2 8.3 %all-to-all-start.1 = ((bf16[4,32,256]{2,1,0:T(8,128)(2,1)}), bf16[4,32,256]{2,1,0:T(8,128)(2,1)S(1)}, u32[]{:S(2)}, u32[]{:S(2)}) async-start(bf16[4,32,256]{2,1,0:T(8,128)(2,1)} %bitcast.41), calls=%async_computation.1 | async-start | bytes 131072 | tf_op jit(solution)/shard_map/all_to_all | solution.py:530
  8.1 1.5 %copy-start.5 = (s32[256]{0:T(256)S(1)}, s32[256]{0:T(256)}, u32[]{:S(2)}) copy-start(s32[256]{0:T(256)} %head_ref.1) | copy-start | bytes 3076
  12.4 23.7 %all-to-all-start.2 = ((bf16[32,32,256]{2,1,0:T(8,128)(2,1)}), bf16[32,32,256]{2,1,0:T(8,128)(2,1)S(1)}, u32[]{:S(2)}, u32[]{:S(2)}) async-start(bf16[32,32,256]{2,1,0:T(8,128)(2,1)} %broadcast_in_dim.68), calls=%async_computation.2 | async-start | bytes 1048576 | tf_op jit(solution)/shard_map/all_to_all | solution.py:536
  36.1 0.8 copy-start.3
  50.7 21.4 %all-to-all-start.3 = ((bf16[32,24,256]{2,1,0:T(8,128)(2,1)}), bf16[32,24,256]{2,1,0:T(8,128)(2,1)S(1)}, u32[]{:S(2)}, u32[]{:S(2)}) async-start(bf16[32,24,256]{2,1,0:T(8,128)(2,1)} %get-tuple-element.115), calls=%async_computation.3 | async-start | bytes 786432 | tf_op jit(solution)/shard_map/all_to_all | solution.py:582
  72.2 0.7 copy-start.2
  77.7 8.1 %all-to-all-start.4 = ((bf16[4,144,128]{2,1,0:T(8,128)(2,1)}), bf16[4,144,128]{2,1,0:T(8,128)(2,1)S(1)}, u32[]{:S(2)}, u32[]{:S(2)}) async-start(bf16[4,144,128]{2,1,0:T(8,128)(2,1)} %get-tuple-element.123), calls=%async_computation.4 | async-start | bytes 294912 | tf_op jit(solution)/shard_map/all_to_all | solution.py:628
  101.5 1.7 %copy-start = (f32[256,2304]{1,0:T(8,128)S(1)}, f32[256,2304]{1,0:T(8,128)}, u32[]{:S(2)}) copy-start(f32[256,2304]{1,0:T(8,128)} %get-tuple-element.124.scores_ref) | copy-start | bytes 7077892

commit v9 on v8

--- a/solution.py
+++ b/solution.py
@@ -20,7 +20,7 @@
 AHEAD = 6
 SCORE_LIMIT = 24 * 2**20
 FAR_LIMIT = 56 * 2**20
-FIRST_LIMIT = 56 * 2**20
+FIRST_LIMIT = 24 * 2**20
 
 
 def one_hot(index, rows):
@@ -132,24 +132,21 @@
     devices,
     base_ref,
     order_ref,
-    src_ref,
-    dst_ref,
-    rel_ref,
-    emb_ref,
-    far_ref,
-    in_ref,
-    out_ref,
-    loop_ref,
-    loop_rel_ref,
-    *rest,
+    *refs,
 ):
+    if last:
+        counts_ref, code_ref = refs[:2]
+    else:
+        src_ref, dst_ref, rel_ref = refs[:3]
+    emb_ref, far_ref, in_ref, out_ref, loop_ref, loop_rel_ref, *rest = refs[2 if last else 3 :]
     far_t_ref, gathered_ref, agg_ref, held_ref, own_ref, made_ref, sems, own_sems, out_sems = rest[-9:]
     if last:
         near_ref, query_rel_ref, relation_ref, rel_weight_ref, _ = rest[:5]
         hidden_ref, factor_ref = rest[5:7]
     else:
         head_ref, mixed_ref, hidden_ref, heads_ref, sent_ref, rank_ref, most_ref = rest[:7]
-    blocks = src_ref.shape[0]
+    blocks, width = (code_ref if last else src_ref).shape
+    third = width // 3
     rows_dev = blocks * BLK
     far_chunks = far_ref.shape[0]
     middle = middle_step(order_ref, blocks, ahead)
@@ -186,6 +183,21 @@
     lax.fori_loop(0, far_chunks, turn, 0)
     if not last:
         made_ref[...] = jnp.zeros_like(made_ref)
+
+    def edges_of(row):
+        if last:
+            code = code_ref[row, :]
+            return code >> 16, (code >> 9) & (BLK - 1), code & 511
+        return src_ref[row, :], dst_ref[row, :], rel_ref[row, :]
+
+    def near_dot(src):
+        return jnp.dot(near_ref[...], one_hot(src, rows_dev), preferred_element_type=F32)
+
+    def look_up_sorted(src):
+        near = near_dot(src[:, : 2 * third])
+        far = look_up(src[:, third:], 0)
+        both = near[:, third:] + far[:, :third]
+        return jnp.concatenate([near[:, :third], both, far[:, third:]], axis=1)
 
     def look_up(src, u):
         if far_chunks == 1:
@@ -235,37 +247,49 @@
                 load(step + 1, 1 - slot).start()
 
             load(step, slot).wait()
-        finish(before, lax.rem(step + 1, 2))
-        rows = [pl.ds(order_ref[(start + i) * STEP + u], 1) for u in range(STEP)]
-        srcs = [src_ref[row, :] for row in rows]
-        found = [look_up(src, u) for u, src in enumerate(srcs)]
-        composed = []
-        for u, row in enumerate(rows):
-            if last:
-                near = jnp.dot(
-                    near_ref[...], one_hot(srcs[u], rows_dev), preferred_element_type=F32
-                )
-                relation = jnp.dot(
-                    relation_ref[...],
-                    one_hot(rel_ref[row, :], relation_ref.shape[1]),
-                    preferred_element_type=F32,
-                )
-                composed.append((found[u] + near).astype(BF16) * relation.astype(BF16))
+        def work(is_sorted):
+            finish(before, lax.rem(step + 1, 2))
+            rows = [pl.ds(order_ref[step * STEP + u], 1) for u in range(STEP)]
+            edges = [edges_of(row) for row in rows]
+            if is_sorted:
+                found = [look_up_sorted(src) for src, _, _ in edges]
             else:
-                is_near = 1 - is_outside(srcs[u], rows_dev)
-                composed.append((found[u].astype(BF16) + is_near) * held_ref[slot, u])
-        for u, row in enumerate(rows):
-            key = dst_ref[row, :] + jnp.where(rel_ref[row, :] >= half_rel, BLK, 0)
-            selector = one_hot(key, 2 * BLK)
-            counts = selector[:, :128]
-            for lane in range(128, selector.shape[1], 128):
-                counts = counts + selector[:, lane : lane + 128]
-            counts = jnp.sum(counts.astype(F32), axis=1, keepdims=True)
-            sums = lax.dot_general(selector, composed[u], NT, preferred_element_type=F32)
-            agg = (sums * (1.0 / jnp.maximum(counts, 1.0))).astype(BF16)
-            here = pl.ds(u * BLK, BLK)
-            agg_ref[0, lax.rem(step, 2), here, :] = agg[:BLK]
-            agg_ref[1, lax.rem(step, 2), here, :] = agg[BLK:]
+                found = [look_up(src, u) for u, (src, _, _) in enumerate(edges)]
+                if last:
+                    found = [some + near_dot(src) for some, (src, _, _) in zip(found, edges)]
+            composed = []
+            for u, (src, _, rel) in enumerate(edges):
+                if last:
+                    relation = jnp.dot(
+                        relation_ref[...],
+                        one_hot(rel, relation_ref.shape[1]),
+                        preferred_element_type=F32,
+                    )
+                    composed.append(found[u].astype(BF16) * relation.astype(BF16))
+                else:
+                    is_near = 1 - is_outside(src, rows_dev)
+                    composed.append((found[u].astype(BF16) + is_near) * held_ref[slot, u])
+            for u, (_, dst, rel) in enumerate(edges):
+                key = dst + jnp.where(rel >= half_rel, BLK, 0)
+                selector = one_hot(key, 2 * BLK)
+                counts = selector[:, :128]
+                for lane in range(128, selector.shape[1], 128):
+                    counts = counts + selector[:, lane : lane + 128]
+                counts = jnp.sum(counts.astype(F32), axis=1, keepdims=True)
+                sums = lax.dot_general(selector, composed[u], NT, preferred_element_type=F32)
+                agg = (sums * (1.0 / jnp.maximum(counts, 1.0))).astype(BF16)
+                here = pl.ds(u * BLK, BLK)
+                agg_ref[0, lax.rem(step, 2), here, :] = agg[:BLK]
+                agg_ref[1, lax.rem(step, 2), here, :] = agg[BLK:]
+
+        if last and far_chunks == 1 and width % 384 == 0:
+            near_counts = [counts_ref[order_ref[step * STEP + u]] for u in range(STEP)]
+            fits = [(count >= third) & (count <= 2 * third) for count in near_counts]
+            all_fit = functools.reduce(jnp.logical_and, fits)
+            pl.when(all_fit)(functools.partial(work, True))
+            pl.when(jnp.logical_not(all_fit))(functools.partial(work, False))
+        else:
+            work(False)
 
         @pl.when(i > 0)
         def _():
@@ -354,9 +378,9 @@
     return pl.pallas_call(
         functools.partial(far_kernel, half_rel, last, ahead, devices),
         out_shape=(jax.ShapeDtypeStruct((rows_dev, columns), BF16),) + outs,
-        in_specs=[SMEM] * 2 + [WHOLE] * 3 + [HBM] + [WHOLE] * (5 + len(more)) + [HBM],
+        in_specs=[SMEM] * len(scalars) + [WHOLE] * len(edges) + [HBM] + [WHOLE] * (5 + len(more)) + [HBM],
         out_specs=(HBM, WHOLE) if last else (HBM, WHOLE, WHOLE, WHOLE, SMEM),
-        input_output_aliases={11 + len(more): 0} if last else {},
+        input_output_aliases={len(scalars) + len(edges) + 6 + len(more): 0} if last else {},
         scratch_shapes=[
             pltpu.VMEM((far.shape[0], columns, CHUNK), BF16),
             pltpu.VMEM((STEP, columns, width if far.shape[0] > 1 else 128), F32),
@@ -523,7 +547,11 @@
         out_specs=WHOLE,
         compiler_params=pltpu.CompilerParams(vmem_limit_bytes=VMEM_LIMIT),
     )((member * rows_dev)[None], export_rows, entity_emb)
-    offered, later_relation = lax.optimization_barrier((offered, relation_emb))
+    offered, later_relation, later_src = lax.optimization_barrier(
+        (offered, relation_emb, edge_src)
+    )
+    code = (later_src << 16) | (edge_dst << 9) | edge_rel
+    near_counts = jnp.sum((later_src < rows_dev).astype(jnp.int32), axis=1)
     rel_count = -(-relations // 256) * 256
     relation_t = jnp.pad(later_relation, ((0, rel_count - relations), (0, 0))).T
     near_t = entity_emb.T
@@ -531,13 +559,15 @@
     mine = jnp.sum(
         pieces.reshape(copies, slots // copies, columns).astype(F32), axis=0
     ).astype(BF16)
-    mine, near_t = lax.optimization_barrier((mine, near_t))
+    mine, near_t, code, near_counts = lax.optimization_barrier((mine, near_t, code, near_counts))
+    code = lax.sort(code, dimension=1)
     spread = jnp.broadcast_to(mine[None], (devices,) + mine.shape)
     table = lax.all_to_all(spread, BOTH, 0, 0).reshape(groups * slots, columns)
     base = (device * blocks)[None]
     mixed, order = near_call(
         ahead, base, query_head, edge_src, edge_rel, near_t, relation_t
     )
+    mixed, code = lax.optimization_barrier((mixed, code))
     far_count = -(-(groups * slots) // CHUNK) * CHUNK
     far = jnp.pad(table, ((0, far_count - groups * slots), (0, 0)))
     far = far.reshape(far_count // CHUNK, CHUNK, columns)
@@ -585,8 +615,8 @@
         True,
         ahead,
         devices,
-        (base, order),
-        edges,
+        (base, order, near_counts),
+        (code,),
         entity_emb,
         far,
         weights,

time: 105 us -> 115 us (1.095)
  between operations: 0.78 us -> 14.2 us
  Pallas kernels: 55 us -> 50.8 us
  other arithmetic: 0.02 us -> 1.32 us
    pallas_call x2, Pallas kernels: 27.7 us -> 25.3 us  [far_call(): pl.pallas_call(functools.partial(far_kernel, half_rel, last, ahead, devic...]
    pallas_call x1, Pallas kernels: 4.73 us -> 2.96 us  [body(): pl.pallas_call(functools.partial(score_kernel, devices), out_shape=(jax.S...]
    reduce_sum x0 -> x1, other arithmetic: none -> 1.3 us  [body(): near_counts = jnp.sum((later_src < rows_dev).astype(jnp.int32), axis=1)]
    unnamed x13 -> x20, local copies, waits for them, and re-layouts: 4.76 us -> 4.61 us
  transfers between devices with their start and end apart: 4 -> 4, of which waited for: 2 -> 3; matrix products, arithmetic and copies ran while one was open for 2% -> 2% of each run, Pallas kernels for 31% -> 27%
where the time goes in v9:
time: 115 us; the launch traced here: 114 us
  Pallas kernels  50.8 us (44%)
  starting transfers between devices  18.8 us (16%)
  blocking collectives  14.5 us (13%)
  between operations  14.2 us (12%)
  waiting for transfers between devices  7.69 us (7%)
  local copies, waits for them, and re-layouts  6.34 us (6%)
  other arithmetic  1.32 us (1%)
    pallas_call x2, Pallas kernels, far_call(): pl.pallas_call(functools.partial(far_kernel, half_rel, last, ahead, devic...  25.3 us
    pallas_call x1, Pallas kernels, near_call(): pl.pallas_call(functools.partial(near_kernel, ahead), out_shape=(jax.Shap...  18.3 us
    all_to_all x1, blocking collectives, body(): lax.all_to_all(payload, 'ent', 0, 0)  14.5 us
    all_to_all x1, starting transfers between devices, body(): sent = lax.all_to_all(spread, BOTH, 0, 0).reshape(devices * cap, columns)  5.85 us
    all_to_all x1, starting transfers between devices, body(): table = lax.all_to_all(spread, BOTH, 0, 0).reshape(groups * slots, columns)  5.42 us
    all_to_all x1, waiting for transfers between devices, body(): lax.all_to_all(payload, 'rep', 0, 0)  4.77 us
    unnamed x20, local copies, waits for them, and re-layouts  4.61 us
    all_to_all x1, starting transfers between devices, body(): pieces = lax.all_to_all(offered, 'rep', 0, 0, tiled=True)  4.21 us
  transfers between devices with their start and end apart: 4, of which 3 were waited for; matrix products, arithmetic and copies ran while one was open for 2% of the time, Pallas kernels for 27%

profile of v9, /device:TPU:0, one launch (start us, length us, event | category | flops | bytes accessed | tf_op | source)
XLA Modules:
  0.0 114.3 jit_solution(17421641653800007253)
XLA Ops:
  7.2 0.0 copy-start.4
  7.2 0.0 copy-start.5
  7.2 0.0 copy-start.7
  7.2 0.0 copy-start.6
  7.2 0.0 copy-start.2
  7.2 2.4 %shard_map.140 = bf16[128,256]{1,0:T(8,128)(2,1)} custom-call(s32[1]{0:T(128)} %bitcast.8.base_ref, s32[1,128]{1,0:T(1,128)} %index_ref.1, bf16[2304,256]{1,0:T(8,128)(2,1)} %refs_2_.3), custom_call_target="tpu_custom_call" | custom-call | tf_op jit(solution)/shard_map/pallas_call | solution.py:543
  9.6 0.0 copy-done.4
  9.6 0.1 copy.17
  9.8 0.0 copy-done.5
  9.8 0.0 copy-done.7
  9.8 0.0 copy-done.6
  9.8 1.3 %convert_reduce_fusion = (s32[18]{0:T(128)}, s32[18,768]{1,0:T(8,128)}) fusion(s32[18,768]{1,0:T(8,128)S(1)} %copy-done.5, s32[18,768]{1,0:T(8,128)S(1)} %copy-done.6, s32[18,768]{1,0:T(8,128)S(1)} %copy-done.7), kind=kLoop, calls=%fused_computation.18 | loop fusion | flops 96750 | bytes 221256 | tf_op jit(solution)/shard_map/reduce_sum | solution.py:554
  11.1 4.2 %all-to-all-start.1 = ((bf16[4,32,256]{2,1,0:T(8,128)(2,1)}), bf16[4,32,256]{2,1,0:T(8,128)(2,1)S(1)}, u32[]{:S(2)}, u32[]{:S(2)}) async-start(bf16[4,32,256]{2,1,0:T(8,128)(2,1)} %bitcast.41), calls=%async_computation.1 | async-start | bytes 131072 | tf_op jit(solution)/shard_map/all_to_all | solution.py:558
  15.3 0.0 sort.9.cloned.1.call-start
  15.3 0.7 pad_bitcast_fusion.relation_ref.refs_10_
  16.0 0.0 copy-done.2
  16.1 0.0 copy-start.8
  16.1 1.5 %copy.16 = bf16[2304,256]{0,1:T(8,128)(2,1)} copy(bf16[2304,256]{1,0:T(8,128)(2,1)S(1)} %copy-done.2) | data formatting | bytes 2359296 | tf_op args[0]
  17.6 0.0 copy-done.8
  17.6 1.9 %all-to-all-done.1 = bf16[4,32,256]{2,1,0:T(8,128)(2,1)S(1)} async-done(((bf16[4,32,256]{2,1,0:T(8,128)(2,1)}), bf16[4,32,256]{2,1,0:T(8,128)(2,1)S(1)}, u32[]{:S(2)}, u32[]{:S(2)}) %all-to-all-start.1) | async-done | bytes 65568 | tf_op jit(solution)/shard_map/all_to_all | solution.py:558
  19.5 0.0 sort.9.cloned.1.call-update
  19.5 0.8 broadcast_in_dim.68
  20.3 5.4 %all-to-all-start.2 = ((bf16[32,32,256]{2,1,0:T(8,128)(2,1)}), bf16[32,32,256]{2,1,0:T(8,128)(2,1)S(1)}, u32[]{:S(2)}, u32[]{:S(2)}) async-start(bf16[32,32,256]{2,1,0:T(8,128)(2,1)} %broadcast_in_dim.68), calls=%async_computation.2 | async-start | bytes 1048576 | tf_op jit(solution)/shard_map/all_to_all | solution.py:565
  25.8 18.3 %shard_map.141 = (bf16[9,2,256,768]{3,2,1,0:T(8,128)(2,1)}, s32[20]{0:T(128)}) custom-call(s32[1]{0:T(128)} %bitcast.7.base_ref, s32[256]{0:T(256)S(1)} %copy-done.8, s32[18,768]{1,0:T(8,128)} %refs_0_.1, s32[18,768]{1,0:T(8,128)} %refs_2_.2, bf16[256,2304]{1,0:T(8,128)(2,1)} %bitcast.37, bf16[256,512]{1,0:T(8,128)(2,1)} %pad_bitcast_fusion.relation_ref.refs_10_), custom_call_target="tpu_custom_call" | custom-call | flops 13287555072 | bytes 4718592 | tf_op jit(solution)/shard_map/pallas_call | solution.py:356
  44.1 0.0 sort.9.cloned.1.call-done.refs_1_
  44.1 0.0 all-to-all-done.2
  44.1 0.0 copy-start.3
  44.1 0.8 copy-done.3
  44.9 13.2 %shard_map.142 = (bf16[2304,256]{1,0:T(8,128)(2,1)}, bf16[264,256]{1,0:T(8,128)(2,1)S(1)}, bf16[32,24,256]{2,1,0:T(8,128)(2,1)}, s32[1,256]{1,0:T(1,128)S(1)}, s32[1]{0:T(128)}) custom-call(s32[1]{0:T(128)} %bitcast.7.base_ref, s32[20]{0:T(128)} %get-tuple-element.118.order_ref, s32[18,768]{1,0:T(8,128)} %refs_0_.1, s32[18,768]{1,0:T(8,128)} %refs_1_.1, ...), custom_call_target="tpu_custom_call" | custom-call | flops 3623878656 | bytes 3538944 | tf_op jit(solution)/shard_map/pallas_call | solution.py:378
  58.1 0.6 while.12
  58.7 5.9 %all-to-all-start.3 = ((bf16[32,24,256]{2,1,0:T(8,128)(2,1)}), bf16[32,24,256]{2,1,0:T(8,128)(2,1)S(1)}, u32[]{:S(2)}, u32[]{:S(2)}) async-start(bf16[32,24,256]{2,1,0:T(8,128)(2,1)} %get-tuple-element.123), calls=%async_computation.3 | async-start | bytes 786432 | tf_op jit(solution)/shard_map/all_to_all | solution.py:612
  64.6 12.1 %shard_map.143 = (bf16[2304,256]{1,0:T(8,128)(2,1)}, f32[256,256]{1,0:T(8,128)}) custom-call(s32[1]{0:T(128)} %bitcast.7.base_ref, s32[20]{0:T(128)} %get-tuple-element.118.order_ref, s32[18]{0:T(128)} %get-tuple-element.128.refs_0_, s32[18,768]{1,0:T(8,128)} %sort.9.cloned.1.call-done.refs_1_, ...), custom_call_target="tpu_custom_call", output_to_operand_aliasing={{0}: (14, {})} | custom-call | flops 3623878656 | bytes 3538944 | tf_op jit(solution)/shard_map/pallas_call | solution.py:378
  76.7 1.1 all-to-all-done.3
  77.7 0.0 copy-start
  77.7 1.3 %copy-done = bf16[2304,256]{1,0:T(8,128)(2,1)S(1)} copy-done((bf16[2304,256]{1,0:T(8,128)(2,1)S(1)}, bf16[2304,256]{1,0:T(8,128)(2,1)}, u32[]{:S(2)}) %copy-start) | copy-done | bytes 1179672
  79.0 0.0 copy-start.1
  79.0 0.9 copy-done.1
  80.0 3.0 %shard_map.144 = (f32[256,2304]{1,0:T(8,128)S(1)}, bf16[4,144,128]{2,1,0:T(8,128)(2,1)}) custom-call(bf16[768,256]{1,0:T(8,128)(2,1)S(1)} %bitcast.35, bf16[256,256]{1,0:T(8,128)(2,1)S(1)} %get-tuple-element.127.more_ref, s32[1,256]{1,0:T(1,128)S(1)} %get-tuple-element.263, s32[1,256]{1,0:T(1,128)S(1)} %bitcast.49, f32[256,256]{1,0:T(8,128)S(1)} %copy-done.1, ...), custom_call_target="tpu_custom_call" | custom-call | tf_op jit(solution)/shard_map/pallas_call | solution.py:637
  82.9 3.3 %all-to-all-start.4 = ((bf16[4,144,128]{2,1,0:T(8,128)(2,1)}), bf16[4,144,128]{2,1,0:T(8,128)(2,1)S(1)}, u32[]{:S(2)}, u32[]{:S(2)}) async-start(bf16[4,144,128]{2,1,0:T(8,128)(2,1)} %get-tuple-element.133), calls=%async_computation.4 | async-start | bytes 294912 | tf_op jit(solution)/shard_map/all_to_all | solution.py:658
  86.3 4.8 %all-to-all-done.4.received_ref = bf16[4,144,128]{2,1,0:T(8,128)(2,1)S(1)} async-done(((bf16[4,144,128]{2,1,0:T(8,128)(2,1)}), bf16[4,144,128]{2,1,0:T(8,128)(2,1)S(1)}, u32[]{:S(2)}, u32[]{:S(2)}) %all-to-all-start.4) | async-done | bytes 147488 | tf_op jit(solution)/shard_map/all_to_all | solution.py:658
  91.1 0.1 shard_map.145
  91.2 14.5 %all_to_all.38.received_ref = bf16[8,144,128]{2,1,0:T(8,128)(2,1)S(1)} all-to-all(bf16[8,144,128]{2,1,0:T(8,128)(2,1)S(1)} %shard_map.145), channel_id=1, replica_groups=mesh['ent'=8,'rep'=4] {'ent'}, dimensions={0} | all-to-all | bytes 589824 | tf_op jit(solution)/shard_map/all_to_all | solution.py:668
  105.7 1.7 %shard_map.146 = (f32[256,2304]{1,0:T(8,128)}, f32[64,256]{1,0:T(8,128)}) custom-call(s32[1]{0:T(128)} %bitcast.6.first_ref, bf16[8,144,128]{2,1,0:T(8,128)(2,1)S(1)} %all_to_all.38.received_ref, f32[256,2304]{1,0:T(8,128)S(1)} %get-tuple-element.134.scores_ref), custom_call_target="tpu_custom_call" | custom-call | tf_op jit(solution)/shard_map/pallas_call | solution.py:659
  (3 shorter events, 0.0 us)
Async XLA Ops:
  7.2 2.5 %copy-start.4 = (bf16[474,256]{1,0:T(8,128)(2,1)S(1)}, bf16[474,256]{1,0:T(8,128)(2,1)}, u32[]{:S(2)}) copy-start(bf16[474,256]{1,0:T(8,128)(2,1)} %param.16) | copy-start | bytes 728068
  7.2 2.6 %copy-start.5 = (s32[18,768]{1,0:T(8,128)S(1)}, s32[18,768]{1,0:T(8,128)}, u32[]{:S(2)}) copy-start(s32[18,768]{1,0:T(8,128)} %refs_0_.1) | copy-start | bytes 165892
  7.2 2.6 %copy-start.7 = (s32[18,768]{1,0:T(8,128)S(1)}, s32[18,768]{1,0:T(8,128)}, u32[]{:S(2)}) copy-start(s32[18,768]{1,0:T(8,128)} %refs_1_.1) | copy-start | bytes 165892
  7.2 2.6 %copy-start.6 = (s32[18,768]{1,0:T(8,128)S(1)}, s32[18,768]{1,0:T(8,128)}, u32[]{:S(2)}) copy-start(s32[18,768]{1,0:T(8,128)} %refs_2_.2) | copy-start | bytes 165892
  7.2 8.8 %copy-start.2 = (bf16[2304,256]{1,0:T(8,128)(2,1)S(1)}, bf16[2304,256]{1,0:T(8,128)(2,1)}, u32[]{:S(2)}) copy-start(bf16[2304,256]{1,0:T(8,128)(2,1)} %refs_2_.3) | copy-start | bytes 3538948
  11.1 8.3 %all-to-all-start.1 = ((bf16[4,32,256]{2,1,0:T(8,128)(2,1)}), bf16[4,32,256]{2,1,0:T(8,128)(2,1)S(1)}, u32[]{:S(2)}, u32[]{:S(2)}) async-start(bf16[4,32,256]{2,1,0:T(8,128)(2,1)} %bitcast.41), calls=%async_computation.1 | async-start | bytes 131072 | tf_op jit(solution)/shard_map/all_to_all | solution.py:558
  15.3 28.8 %sort.9.cloned.1.call-start = ((), (), s32[]{:S(2)}) async-start(), calls=%async_computation.6 | async-start | bytes 221216 | tf_op jit(solution)/shard_map/sort | solution.py:563
  16.1 1.5 %copy-start.8 = (s32[256]{0:T(256)S(1)}, s32[256]{0:T(256)}, u32[]{:S(2)}) copy-start(s32[256]{0:T(256)} %head_ref.1) | copy-start | bytes 3076
  20.3 23.8 %all-to-all-start.2 = ((bf16[32,32,256]{2,1,0:T(8,128)(2,1)}), bf16[32,32,256]{2,1,0:T(8,128)(2,1)S(1)}, u32[]{:S(2)}, u32[]{:S(2)}) async-start(bf16[32,32,256]{2,1,0:T(8,128)(2,1)} %broadcast_in_dim.68), calls=%async_computation.2 | async-start | bytes 1048576 | tf_op jit(solution)/shard_map/all_to_all | solution.py:565
  44.1 0.8 copy-start.3
  58.7 19.0 %all-to-all-start.3 = ((bf16[32,24,256]{2,1,0:T(8,128)(2,1)}), bf16[32,24,256]{2,1,0:T(8,128)(2,1)S(1)}, u32[]{:S(2)}, u32[]{:S(2)}) async-start(bf16[32,24,256]{2,1,0:T(8,128)(2,1)} %get-tuple-element.123), calls=%async_computation.3 | async-start | bytes 786432 | tf_op jit(solution)/shard_map/all_to_all | solution.py:612
  77.7 1.3 %copy-start = (bf16[2304,256]{1,0:T(8,128)(2,1)S(1)}, bf16[2304,256]{1,0:T(8,128)(2,1)}, u32[]{:S(2)}) copy-start(bf16[2304,256]{1,0:T(8,128)(2,1)} %get-tuple-element.132.hidden_hbm) | copy-start | bytes 3538948
  79.0 0.9 copy-start.1
  82.9 8.1 %all-to-all-start.4 = ((bf16[4,144,128]{2,1,0:T(8,128)(2,1)}), bf16[4,144,128]{2,1,0:T(8,128)(2,1)S(1)}, u32[]{:S(2)}, u32[]{:S(2)}) async-start(bf16[4,144,128]{2,1,0:T(8,128)(2,1)} %get-tuple-element.133), calls=%async_computation.4 | async-start | bytes 294912 | tf_op jit(solution)/shard_map/all_to_all | solution.py:658
Sparse Core Ops, SparseCore 0:
  19.6 6.7 sort.11.cloned.1.call-done
  (1 shorter events, 0.0 us)

commit v10 on v8

--- a/solution.py
+++ b/solution.py
@@ -20,7 +20,7 @@
 AHEAD = 6
 SCORE_LIMIT = 24 * 2**20
 FAR_LIMIT = 56 * 2**20
-FIRST_LIMIT = 56 * 2**20
+FIRST_LIMIT = 24 * 2**20
 
 
 def one_hot(index, rows):
@@ -312,11 +312,14 @@
     lax.fori_loop(start, stop, gave, 0)
 
 
-def pick_kernel(base_ref, index_ref, emb_ref, offered_ref):
-    picks = one_hot(index_ref[...] - base_ref[0], emb_ref.shape[0])
-    offered_ref[...] = lax.dot_general(
-        picks, emb_ref[...], TN, preferred_element_type=F32
-    ).astype(BF16)
+def pick_kernel(bit, member_ref, index_ref, emb_ref, kept_ref, sent_ref):
+    rows_dev = emb_ref.shape[0]
+    picks = one_hot(index_ref[...] - member_ref[0] * rows_dev, rows_dev)
+    rows = lax.dot_general(picks, emb_ref[...], TN, preferred_element_type=F32)
+    half = kept_ref.shape[0]
+    upper = member_ref[0] & bit > 0
+    kept_ref[...] = jnp.where(upper, rows[half:], rows[:half]).astype(BF16)
+    sent_ref[...] = jnp.where(upper, rows[:half], rows[half:]).astype(BF16)
 
 
 SMEM = pl.BlockSpec(memory_space=pltpu.SMEM)
@@ -516,21 +519,30 @@
     ahead = min(AHEAD, blocks // STEP)
 
     slots = export_rows.shape[1]
-    offered = pl.pallas_call(
-        pick_kernel,
-        out_shape=jax.ShapeDtypeStruct((slots, columns), BF16),
+    bit = copies // 2
+    half = slots // 2
+    half_type = jax.ShapeDtypeStruct((half, columns), BF16)
+    kept, gone = pl.pallas_call(
+        functools.partial(pick_kernel, bit),
+        out_shape=(half_type, half_type),
         in_specs=[SMEM, WHOLE, WHOLE],
-        out_specs=WHOLE,
+        out_specs=(WHOLE, WHOLE),
         compiler_params=pltpu.CompilerParams(vmem_limit_bytes=VMEM_LIMIT),
-    )((member * rows_dev)[None], export_rows, entity_emb)
-    offered, later_relation = lax.optimization_barrier((offered, relation_emb))
+    )(member[None], export_rows, entity_emb)
+    gone, later_relation = lax.optimization_barrier((gone, relation_emb))
     rel_count = -(-relations // 256) * 256
     relation_t = jnp.pad(later_relation, ((0, rel_count - relations), (0, 0))).T
     near_t = entity_emb.T
-    pieces = lax.all_to_all(offered, "rep", 0, 0, tiled=True)
-    mine = jnp.sum(
-        pieces.reshape(copies, slots // copies, columns).astype(F32), axis=0
-    ).astype(BF16)
+    while True:
+        pairs = [(one, one ^ bit) for one in range(copies)]
+        mine = kept + lax.ppermute(gone, "rep", pairs)
+        bit //= 2
+        if bit == 0:
+            break
+        half //= 2
+        upper = (member & bit > 0).astype(jnp.int32)
+        kept = lax.dynamic_slice_in_dim(mine, upper * half, half, 0)
+        gone = lax.dynamic_slice_in_dim(mine, (1 - upper) * half, half, 0)
     mine, near_t = lax.optimization_barrier((mine, near_t))
     spread = jnp.broadcast_to(mine[None], (devices,) + mine.shape)
     table = lax.all_to_all(spread, BOTH, 0, 0).reshape(groups * slots, columns)

time: 105 us -> 103 us (0.981)
  Pallas kernels: 55 us -> 53.2 us
  starting transfers between devices: 19.8 us -> 18.7 us
    all_to_all x1 -> x0, starting transfers between devices: 4.22 us -> none  [body(): pieces = lax.all_to_all(offered, 'rep', 0, 0, tiled=True)]
    ppermute x0 -> x2, starting transfers between devices: none -> 3.01 us  [body(): mine = kept + lax.ppermute(gone, 'rep', pairs)]
    ppermute x0 -> x2, waiting for transfers between devices: none -> 1.96 us  [body(): mine = kept + lax.ppermute(gone, 'rep', pairs)]
    all_to_all x1 -> x0, waiting for transfers between devices: 1.87 us -> none  [body(): pieces = lax.all_to_all(offered, 'rep', 0, 0, tiled=True)]
    pallas_call x1, Pallas kernels: 4.73 us -> 2.96 us  [body(): pl.pallas_call(functools.partial(score_kernel, devices), out_shape=(jax.S...]
    all_to_all x1, starting transfers between devices: 5.42 us -> 6.48 us  [body(): table = lax.all_to_all(spread, BOTH, 0, 0).reshape(groups * slots, columns)]
  transfers between devices with their start and end apart: 4 -> 5, of which waited for: 2 -> 2; matrix products, arithmetic and copies ran while one was open for 2% -> 2% of each run, Pallas kernels for 31% -> 32%
where the time goes in v10:
time: 103 us
  Pallas kernels  53.2 us (52%)
  starting transfers between devices  18.7 us (18%)
  blocking collectives  15.6 us (15%)
  waiting for transfers between devices  6.73 us (7%)
  local copies, waits for them, and re-layouts  6.29 us (6%)
    pallas_call x2, Pallas kernels, far_call(): pl.pallas_call(functools.partial(far_kernel, half_rel, last, ahead, devic...  27.7 us
    pallas_call x1, Pallas kernels, near_call(): pl.pallas_call(functools.partial(near_kernel, ahead), out_shape=(jax.Shap...  18.3 us
    all_to_all x1, blocking collectives, body(): lax.all_to_all(payload, 'ent', 0, 0)  15.6 us
    all_to_all x1, starting transfers between devices, body(): table = lax.all_to_all(spread, BOTH, 0, 0).reshape(groups * slots, columns)  6.48 us
    all_to_all x1, starting transfers between devices, body(): sent = lax.all_to_all(spread, BOTH, 0, 0).reshape(devices * cap, columns)  5.85 us
    all_to_all x1, waiting for transfers between devices, body(): lax.all_to_all(payload, 'rep', 0, 0)  4.77 us
    unnamed x13, local copies, waits for them, and re-layouts  4.57 us
    all_to_all x1, starting transfers between devices, body(): lax.all_to_all(payload, 'rep', 0, 0)  3.35 us
  transfers between devices with their start and end apart: 5, of which 2 were waited for; matrix products, arithmetic and copies ran while one was open for 2% of the time, Pallas kernels for 32%

profile of v10, /device:TPU:0, one launch (start us, length us, event | category | flops | bytes accessed | tf_op | source)
XLA Modules:
  0.0 102.8 jit_solution(13399398504374493824)
XLA Ops:
  0.6 0.0 copy-start.4
  0.6 0.0 copy-start.2
  0.7 2.4 %shard_map.140 = (bf16[64,256]{1,0:T(8,128)(2,1)}, bf16[64,256]{1,0:T(8,128)(2,1)}) custom-call(s32[1]{0:T(128)} %bitcast.8.member_ref, s32[1,128]{1,0:T(1,128)} %index_ref.1, bf16[2304,256]{1,0:T(8,128)(2,1)} %emb_ref.5), custom_call_target="tpu_custom_call" | custom-call | tf_op jit(solution)/shard_map/pallas_call | solution.py:525
  3.1 2.9 %collective-permute-start = (bf16[64,256]{1,0:T(8,128)(2,1)}, bf16[64,256]{1,0:T(8,128)(2,1)S(1)}, u32[]{:S(2)}, u32[]{:S(2)}) collective-permute-start(bf16[64,256]{1,0:T(8,128)(2,1)} %get-tuple-element.113), channel_id=1, source_target_pairs={{0,2},{1,3},{2,0},{3,1},{4,6},{5,7},{6,4},{7,5},{8,10},{9,11},{10,... | collective-permute-start | bytes 98312 | tf_op jit(solution)/shard_map/ppermute | solution.py:538
  6.0 0.0 copy-done.4
  6.0 0.1 copy.17
  6.1 2.0 %collective-permute-done = bf16[64,256]{1,0:T(8,128)(2,1)S(1)} collective-permute-done((bf16[64,256]{1,0:T(8,128)(2,1)}, bf16[64,256]{1,0:T(8,128)(2,1)S(1)}, u32[]{:S(2)}, u32[]{:S(2)}) %collective-permute-start) | collective-permute-done | bytes 32800 | tf_op jit(solution)/shard_map/ppermute | solution.py:538
  8.1 0.8 add.91
  8.9 0.1 collective-permute-start.1
  9.0 0.7 pad_bitcast_fusion.relation_ref.rest_2_
  9.7 0.0 copy-done.2
  9.7 0.0 copy-start.5
  9.7 1.5 %copy.16 = bf16[2304,256]{0,1:T(8,128)(2,1)} copy(bf16[2304,256]{1,0:T(8,128)(2,1)S(1)} %copy-done.2) | data formatting | bytes 2359296 | tf_op args[0]
  11.2 0.0 copy-done.5
  11.2 0.0 collective-permute-done.1
  11.3 0.8 broadcast_in_dim.68
  12.1 6.5 %all-to-all-start.1 = ((bf16[32,32,256]{2,1,0:T(8,128)(2,1)}), bf16[32,32,256]{2,1,0:T(8,128)(2,1)S(1)}, u32[]{:S(2)}, u32[]{:S(2)}) async-start(bf16[32,32,256]{2,1,0:T(8,128)(2,1)} %broadcast_in_dim.68), calls=%async_computation.1 | async-start | bytes 1048576 | tf_op jit(solution)/shard_map/all_to_all | solution.py:548
  18.6 18.3 %shard_map.141 = (bf16[9,2,256,768]{3,2,1,0:T(8,128)(2,1)}, s32[20]{0:T(128)}) custom-call(s32[1]{0:T(128)} %bitcast.7.base_ref, s32[256]{0:T(256)S(1)} %copy-done.5, s32[18,768]{1,0:T(8,128)} %src_ref.5, s32[18,768]{1,0:T(8,128)} %rel_ref.5, bf16[256,2304]{1,0:T(8,128)(2,1)} %bitcast.36, bf16[256,512]{1,0:T(8,128)(2,1)} %pad_bitcast_fusion.relation_ref.rest_2_), custom_call_target="tpu_custom_call" | custom-call | flops 13287555072 | bytes 4718592 | tf_op jit(solution)/shard_map/pallas_call | solution.py:335
  36.9 0.0 all-to-all-done.1
  36.9 0.0 copy-start.3
  36.9 0.8 copy-done.3
  37.7 13.2 %shard_map.142 = (bf16[2304,256]{1,0:T(8,128)(2,1)}, bf16[264,256]{1,0:T(8,128)(2,1)S(1)}, bf16[32,24,256]{2,1,0:T(8,128)(2,1)}, s32[1,256]{1,0:T(1,128)S(1)}, s32[1]{0:T(128)}) custom-call(s32[1]{0:T(128)} %bitcast.7.base_ref, s32[20]{0:T(128)} %get-tuple-element.116.order_ref, s32[18,768]{1,0:T(8,128)} %src_ref.5, s32[18,768]{1,0:T(8,128)} %dst_ref.3, ...), custom_call_target="tpu_custom_call" | custom-call | flops 3623878656 | bytes 3538944 | tf_op jit(solution)/shard_map/pallas_call | solution.py:357
  50.9 0.6 while.12
  51.6 5.8 %all-to-all-start.2 = ((bf16[32,24,256]{2,1,0:T(8,128)(2,1)}), bf16[32,24,256]{2,1,0:T(8,128)(2,1)S(1)}, u32[]{:S(2)}, u32[]{:S(2)}) async-start(bf16[32,24,256]{2,1,0:T(8,128)(2,1)} %get-tuple-element.119), calls=%async_computation.2 | async-start | bytes 786432 | tf_op jit(solution)/shard_map/all_to_all | solution.py:594
  57.4 14.5 %shard_map.143 = (bf16[2304,256]{1,0:T(8,128)(2,1)}, f32[256,256]{1,0:T(8,128)}) custom-call(s32[1]{0:T(128)} %bitcast.7.base_ref, s32[20]{0:T(128)} %get-tuple-element.116.order_ref, s32[18,768]{1,0:T(8,128)} %src_ref.5, s32[18,768]{1,0:T(8,128)} %dst_ref.3, s32[18,768]{1,0:T(8,128)} %rel_ref.5, ...), custom_call_target="tpu_custom_call", output_to_operand_aliasing={{0}: (15, {})} | custom-call | flops 3623878656 | bytes 3538944 | tf_op jit(solution)/shard_map/pallas_call | solution.py:357
  72.0 0.0 all-to-all-done.2
  72.0 0.0 copy-start
  72.0 1.3 %copy-done = bf16[2304,256]{1,0:T(8,128)(2,1)S(1)} copy-done((bf16[2304,256]{1,0:T(8,128)(2,1)S(1)}, bf16[2304,256]{1,0:T(8,128)(2,1)}, u32[]{:S(2)}) %copy-start) | copy-done | bytes 1179672
  73.3 0.0 copy-start.1
  73.3 0.9 copy-done.1
  74.2 3.0 %shard_map.144 = (f32[256,2304]{1,0:T(8,128)S(1)}, bf16[4,144,128]{2,1,0:T(8,128)(2,1)}) custom-call(bf16[768,256]{1,0:T(8,128)(2,1)S(1)} %bitcast.34, bf16[256,256]{1,0:T(8,128)(2,1)S(1)} %get-tuple-element.123.more_ref, s32[1,256]{1,0:T(1,128)S(1)} %get-tuple-element.247, s32[1,256]{1,0:T(1,128)S(1)} %bitcast.47, f32[256,256]{1,0:T(8,128)S(1)} %copy-done.1, ...), custom_call_target="tpu_custom_call" | custom-call | tf_op jit(solution)/shard_map/pallas_call | solution.py:619
  77.2 3.3 %all-to-all-start.3 = ((bf16[4,144,128]{2,1,0:T(8,128)(2,1)}), bf16[4,144,128]{2,1,0:T(8,128)(2,1)S(1)}, u32[]{:S(2)}, u32[]{:S(2)}) async-start(bf16[4,144,128]{2,1,0:T(8,128)(2,1)} %get-tuple-element.127), calls=%async_computation.3 | async-start | bytes 294912 | tf_op jit(solution)/shard_map/all_to_all | solution.py:640
  80.5 4.8 %all-to-all-done.3.received_ref = bf16[4,144,128]{2,1,0:T(8,128)(2,1)S(1)} async-done(((bf16[4,144,128]{2,1,0:T(8,128)(2,1)}), bf16[4,144,128]{2,1,0:T(8,128)(2,1)S(1)}, u32[]{:S(2)}, u32[]{:S(2)}) %all-to-all-start.3) | async-done | bytes 147488 | tf_op jit(solution)/shard_map/all_to_all | solution.py:640
  85.3 0.1 shard_map.145
  85.5 15.6 %all_to_all.29.received_ref = bf16[8,144,128]{2,1,0:T(8,128)(2,1)S(1)} all-to-all(bf16[8,144,128]{2,1,0:T(8,128)(2,1)S(1)} %shard_map.145), channel_id=1, replica_groups=mesh['ent'=8,'rep'=4] {'ent'}, dimensions={0} | all-to-all | bytes 589824 | tf_op jit(solution)/shard_map/all_to_all | solution.py:650
  101.0 1.7 %shard_map.146 = (f32[256,2304]{1,0:T(8,128)}, f32[64,256]{1,0:T(8,128)}) custom-call(s32[1]{0:T(128)} %bitcast.6.first_ref, bf16[8,144,128]{2,1,0:T(8,128)(2,1)S(1)} %all_to_all.29.received_ref, f32[256,2304]{1,0:T(8,128)S(1)} %get-tuple-element.128.scores_ref), custom_call_target="tpu_custom_call" | custom-call | tf_op jit(solution)/shard_map/pallas_call | solution.py:641
  (4 shorter events, 0.0 us)
Async XLA Ops:
  0.6 5.4 %copy-start.4 = (bf16[474,256]{1,0:T(8,128)(2,1)S(1)}, bf16[474,256]{1,0:T(8,128)(2,1)}, u32[]{:S(2)}) copy-start(bf16[474,256]{1,0:T(8,128)(2,1)} %param.16) | copy-start | bytes 728068
  0.6 9.0 %copy-start.2 = (bf16[2304,256]{1,0:T(8,128)(2,1)S(1)}, bf16[2304,256]{1,0:T(8,128)(2,1)}, u32[]{:S(2)}) copy-start(bf16[2304,256]{1,0:T(8,128)(2,1)} %emb_ref.5) | copy-start | bytes 3538948
  3.1 5.0 %collective-permute-start = (bf16[64,256]{1,0:T(8,128)(2,1)}, bf16[64,256]{1,0:T(8,128)(2,1)S(1)}, u32[]{:S(2)}, u32[]{:S(2)}) collective-permute-start(bf16[64,256]{1,0:T(8,128)(2,1)} %get-tuple-element.113), channel_id=1, source_target_pairs={{0,2},{1,3},{2,0},{3,1},{4,6},{5,7},{6,4},{7,5},{8,10},{9,11},{10,... | collective-permute-start | bytes 98312 | tf_op jit(solution)/shard_map/ppermute | solution.py:538
  8.9 2.3 %collective-permute-start.1 = (bf16[32,256]{1,0:T(8,128)(2,1)S(1)}, bf16[32,256]{1,0:T(8,128)(2,1)S(1)}, u32[]{:S(2)}, u32[]{:S(2)}) collective-permute-start(bf16[32,256]{1,0:T(8,128)(2,1)S(1)} %constant_dynamic-slice_fusion.1), channel_id=1, source_target_pairs={{0,1},{1,0},{2,3},{3,2},{4,5},{5,4},{6,7},{7,6},{8,9},{9,8},{10,11... | collective-permute-start | bytes 49160 | tf_op jit(solution)/shard_map/ppermute | solution.py:538
  9.7 1.5 %copy-start.5 = (s32[256]{0:T(256)S(1)}, s32[256]{0:T(256)}, u32[]{:S(2)}) copy-start(s32[256]{0:T(256)} %head_ref.1) | copy-start | bytes 3076
  12.1 24.8 %all-to-all-start.1 = ((bf16[32,32,256]{2,1,0:T(8,128)(2,1)}), bf16[32,32,256]{2,1,0:T(8,128)(2,1)S(1)}, u32[]{:S(2)}, u32[]{:S(2)}) async-start(bf16[32,32,256]{2,1,0:T(8,128)(2,1)} %broadcast_in_dim.68), calls=%async_computation.1 | async-start | bytes 1048576 | tf_op jit(solution)/shard_map/all_to_all | solution.py:548
  36.9 0.8 copy-start.3
  51.6 20.4 %all-to-all-start.2 = ((bf16[32,24,256]{2,1,0:T(8,128)(2,1)}), bf16[32,24,256]{2,1,0:T(8,128)(2,1)S(1)}, u32[]{:S(2)}, u32[]{:S(2)}) async-start(bf16[32,24,256]{2,1,0:T(8,128)(2,1)} %get-tuple-element.119), calls=%async_computation.2 | async-start | bytes 786432 | tf_op jit(solution)/shard_map/all_to_all | solution.py:594
  72.0 1.3 %copy-start = (bf16[2304,256]{1,0:T(8,128)(2,1)S(1)}, bf16[2304,256]{1,0:T(8,128)(2,1)}, u32[]{:S(2)}) copy-start(bf16[2304,256]{1,0:T(8,128)(2,1)} %get-tuple-element.126.hidden_hbm) | copy-start | bytes 3538948
  73.3 0.9 copy-start.1
  77.2 8.1 %all-to-all-start.3 = ((bf16[4,144,128]{2,1,0:T(8,128)(2,1)}), bf16[4,144,128]{2,1,0:T(8,128)(2,1)S(1)}, u32[]{:S(2)}, u32[]{:S(2)}) async-start(bf16[4,144,128]{2,1,0:T(8,128)(2,1)} %get-tuple-element.127), calls=%async_computation.3 | async-start | bytes 294912 | tf_op jit(solution)/shard_map/all_to_all | solution.py:640

commit v11 on v7

--- a/solution.py
+++ b/solution.py
@@ -9,6 +9,7 @@
 
 BLK = 128
 CHUNK = 1024
+NARROW = 768
 LANES = 128
 BF16 = jnp.bfloat16
 F32 = jnp.float32
@@ -35,6 +36,19 @@
     return jnp.where(src < rows_dev, 0.0, 1.0).astype(BF16)
 
 
+def border_place(slot):
+    shard = (slot >> 7) & 7
+    low = slot & 63
+    place = jnp.where((slot & 64) == 0, shard * 64, 512 + (shard ^ 4) * 64) + low
+    return jnp.where(slot < 0, -1, (slot >> 10) * CHUNK + place)
+
+
+def reordered(rows):
+    first = [rows[shard * 128 : shard * 128 + 64] for shard in range(8)]
+    second = [rows[shard * 128 + 64 : shard * 128 + 128] for shard in (4, 5, 6, 7, 0, 1, 2, 3)]
+    return jnp.concatenate(first + second, axis=0)
+
+
 def order_blocks(head_ref, first_block, blocks, order_ref):
     def mark(q, marks):
         block = lax.shift_right_arithmetic(head_ref[q], BLK.bit_length() - 1) - first_block
@@ -67,12 +81,15 @@
     relation_ref,
     mixed_ref,
     order_ref,
+    wide_ref,
     held_ref,
     sems,
 ):
     blocks = src_ref.shape[0]
     rows_dev = near_ref.shape[1]
     order_blocks(head_ref, base_ref[0], blocks, order_ref)
+    places = border_place(src_ref[...] - rows_dev)
+    wide_ref[0] = jnp.max((places >= NARROW).astype(F32)).astype(jnp.int32)
     count = middle_step(order_ref, blocks, ahead)
 
     def save(step, slot):
@@ -130,6 +147,7 @@
     devices,
     base_ref,
     order_ref,
+    wide_ref,
     src_ref,
     dst_ref,
     rel_ref,
@@ -143,10 +161,10 @@
 ):
     far_t_ref, gathered_ref, agg_ref, held_ref, own_ref, made_ref, sems, own_sems, out_sems = rest[-9:]
     if last:
-        near_ref, query_rel_ref, relation_ref, rel_weight_ref, _ = rest[:5]
-        hidden_ref, factor_ref = rest[5:7]
+        near_ref, relation_ref, _, hidden_ref = rest[:4]
     else:
-        head_ref, mixed_ref, hidden_ref, heads_ref, rank_ref, most_ref = rest[:6]
+        head_ref, query_rel_ref, relation_ref, rel_weight_ref, mixed_ref = rest[:5]
+        hidden_ref, heads_ref, factor_ref, rank_ref, most_ref = rest[5:10]
     blocks = src_ref.shape[0]
     rows_dev = blocks * BLK
     far_chunks = far_ref.shape[0]
@@ -178,25 +196,24 @@
             load(start, 0).start()
 
     def turn(j, carry):
-        far_t_ref[j] = jnp.transpose(far_ref[j])
+        far_t_ref[j] = jnp.transpose(reordered(far_ref[j]))
         return carry
 
     lax.fori_loop(0, far_chunks, turn, 0)
     if not last:
         made_ref[...] = jnp.zeros_like(made_ref)
 
-    def look_up(src, u):
+    def look_up(src, u, depth):
+        place = border_place(src - rows_dev)
         if far_chunks == 1:
             return jnp.dot(
-                far_t_ref[0], one_hot(src - rows_dev, CHUNK), preferred_element_type=F32
+                far_t_ref[0, :, :depth], one_hot(place, depth), preferred_element_type=F32
             )
         gathered_ref[u] = jnp.zeros(gathered_ref.shape[1:], F32)
 
         def one_chunk(j, carry):
             gathered_ref[u] += jnp.dot(
-                far_t_ref[j],
-                one_hot(src - rows_dev - j * CHUNK, CHUNK),
-                preferred_element_type=F32,
+                far_t_ref[j], one_hot(place - j * CHUNK, CHUNK), preferred_element_type=F32
             )
             return carry
 
@@ -233,37 +250,44 @@
                 load(step + 1, 1 - slot).start()
 
             load(step, slot).wait()
-        finish(before, lax.rem(step + 1, 2))
-        rows = [pl.ds(order_ref[(start + i) * STEP + u], 1) for u in range(STEP)]
-        srcs = [src_ref[row, :] for row in rows]
-        found = [look_up(src, u) for u, src in enumerate(srcs)]
-        composed = []
-        for u, row in enumerate(rows):
-            if last:
-                near = jnp.dot(
-                    near_ref[...], one_hot(srcs[u], rows_dev), preferred_element_type=F32
-                )
-                relation = jnp.dot(
-                    relation_ref[...],
-                    one_hot(rel_ref[row, :], relation_ref.shape[1]),
-                    preferred_element_type=F32,
-                )
-                composed.append((found[u] + near).astype(BF16) * relation.astype(BF16))
-            else:
-                is_near = 1 - is_outside(srcs[u], rows_dev)
-                composed.append((found[u].astype(BF16) + is_near) * held_ref[slot, u])
-        for u, row in enumerate(rows):
-            key = dst_ref[row, :] + jnp.where(rel_ref[row, :] >= half_rel, BLK, 0)
-            selector = one_hot(key, 2 * BLK)
-            counts = selector[:, :128]
-            for lane in range(128, selector.shape[1], 128):
-                counts = counts + selector[:, lane : lane + 128]
-            counts = jnp.sum(counts.astype(F32), axis=1, keepdims=True)
-            sums = lax.dot_general(selector, composed[u], NT, preferred_element_type=F32)
-            agg = (sums * (1.0 / jnp.maximum(counts, 1.0))).astype(BF16)
-            here = pl.ds(u * BLK, BLK)
-            agg_ref[0, lax.rem(step, 2), here, :] = agg[:BLK]
-            agg_ref[1, lax.rem(step, 2), here, :] = agg[BLK:]
+        def work(depth):
+            finish(before, lax.rem(step + 1, 2))
+            rows = [pl.ds(order_ref[(start + i) * STEP + u], 1) for u in range(STEP)]
+            srcs = [src_ref[row, :] for row in rows]
+            found = [look_up(src, u, depth) for u, src in enumerate(srcs)]
+            composed = []
+            for u, row in enumerate(rows):
+                if last:
+                    near = jnp.dot(
+                        near_ref[...], one_hot(srcs[u], rows_dev), preferred_element_type=F32
+                    )
+                    relation = jnp.dot(
+                        relation_ref[...],
+                        one_hot(rel_ref[row, :], relation_ref.shape[1]),
+                        preferred_element_type=F32,
+                    )
+                    composed.append((found[u] + near).astype(BF16) * relation.astype(BF16))
+                else:
+                    is_near = 1 - is_outside(srcs[u], rows_dev)
+                    composed.append((found[u].astype(BF16) + is_near) * held_ref[slot, u])
+            for u, row in enumerate(rows):
+                key = dst_ref[row, :] + jnp.where(rel_ref[row, :] >= half_rel, BLK, 0)
+                selector = one_hot(key, 2 * BLK)
+                counts = selector[:, :128]
+                for lane in range(128, selector.shape[1], 128):
+                    counts = counts + selector[:, lane : lane + 128]
+                counts = jnp.sum(counts.astype(F32), axis=1, keepdims=True)
+                sums = lax.dot_general(selector, composed[u], NT, preferred_element_type=F32)
+                agg = (sums * (1.0 / jnp.maximum(counts, 1.0))).astype(BF16)
+                here = pl.ds(u * BLK, BLK)
+                agg_ref[0, lax.rem(step, 2), here, :] = agg[:BLK]
+                agg_ref[1, lax.rem(step, 2), here, :] = agg[BLK:]
+
+        if far_chunks == 1:
+            pl.when(wide_ref[0] == 0)(functools.partial(work, NARROW))
+            pl.when(wide_ref[0] != 0)(functools.partial(work, CHUNK))
+        else:
+            work(CHUNK)
 
         @pl.when(i > 0)
         def _():
@@ -282,7 +306,7 @@
         for u in range(STEP):
             give(stop - 1, u).start()
 
-    if last:
+    if not last:
         picks = one_hot(query_rel_ref[...], relation_ref.shape[1])
         rows = lax.dot_general(
             picks, relation_ref[...], (((0,), (1,)), ((), ())), preferred_element_type=F32
@@ -290,7 +314,6 @@
         factor_ref[...] = jnp.dot(
             rows.astype(BF16), rel_weight_ref[...], preferred_element_type=F32
         )
-    else:
         picks = one_hot_wide(head_ref[...] - base_ref[0] * BLK, rows_dev)
         rows = lax.dot_general(picks, made_ref[...], TN, preferred_element_type=F32)
         rank = ranks(owners(head_ref[...], devices, rows_dev))
@@ -329,9 +352,10 @@
         out_shape=(
             jax.ShapeDtypeStruct((blocks // STEP, STEP, columns, edges), BF16),
             jax.ShapeDtypeStruct((blocks + 2,), jnp.int32),
+            jax.ShapeDtypeStruct((1,), jnp.int32),
         ),
         in_specs=[SMEM] * 2 + [WHOLE] * 4,
-        out_specs=(HBM, SMEM),
+        out_specs=(HBM, SMEM, SMEM),
         scratch_shapes=[
             pltpu.VMEM((2, STEP, columns, edges), BF16),
             pltpu.SemaphoreType.DMA((2,)),
@@ -349,9 +373,9 @@
     return pl.pallas_call(
         functools.partial(far_kernel, half_rel, last, ahead, devices),
         out_shape=(jax.ShapeDtypeStruct((rows_dev, columns), BF16),) + outs,
-        in_specs=[SMEM] * 2 + [WHOLE] * 3 + [HBM] + [WHOLE] * (5 + len(more)) + [HBM],
-        out_specs=(HBM, WHOLE) if last else (HBM, WHOLE, WHOLE, SMEM),
-        input_output_aliases={11 + len(more): 0} if last else {},
+        in_specs=[SMEM] * 3 + [WHOLE] * 3 + [HBM] + [WHOLE] * (5 + len(more)) + [HBM],
+        out_specs=(HBM,) if last else (HBM, WHOLE, WHOLE, WHOLE, SMEM),
+        input_output_aliases={12 + len(more): 0} if last else {},
         scratch_shapes=[
             pltpu.VMEM((far.shape[0], columns, CHUNK), BF16),
             pltpu.VMEM((STEP, columns, width if far.shape[0] > 1 else 128), F32),
@@ -530,7 +554,7 @@
     spread = jnp.broadcast_to(mine[None], (devices,) + mine.shape)
     table = lax.all_to_all(spread, BOTH, 0, 0).reshape(groups * slots, columns)
     base = (device * blocks)[None]
-    mixed, order = near_call(
+    mixed, order, wide = near_call(
         ahead, base, query_head, edge_src, edge_rel, near_t, relation_t
     )
     far_count = -(-(groups * slots) // CHUNK) * CHUNK
@@ -541,20 +565,21 @@
     weights = (in_weight, out_weight, loop_weight, loop_rel[None])
     edges = (edge_src, edge_dst, edge_rel)
     cap = min(queries, -(-3 * queries // (8 * devices)) * 8)
-    hidden, heads, rank, most = far_call(
+    hidden, heads, query_factor, rank, most = far_call(
         relations // 2,
         False,
         ahead,
         devices,
-        (base, order),
+        (base, order, wide),
         edges,
         entity_emb,
         far,
         weights,
-        (head_row,),
+        (head_row, query_rel[None], relation_t, rel_weight),
         mixed,
         (
             jax.ShapeDtypeStruct((-(-queries // cap) * cap, columns), BF16),
+            jax.ShapeDtypeStruct((queries, columns), F32),
             jax.ShapeDtypeStruct((1, queries), jnp.int32),
             jax.ShapeDtypeStruct((1,), jnp.int32),
         ),
@@ -574,19 +599,19 @@
         return turn + 1, jnp.where(inside[:, None], rows, more)
 
     sent = send_round(0)
-    hidden, query_factor = far_call(
+    (hidden,) = far_call(
         relations // 2,
         True,
         ahead,
         devices,
-        (base, order),
+        (base, order, wide),
         edges,
         entity_emb,
         far,
         weights,
-        (near_t, query_rel[None], relation_t, rel_weight),
+        (near_t, relation_t),
         hidden,
-        (jax.ShapeDtypeStruct((queries, columns), F32),),
+        (),
     )
     _, more_heads = lax.while_loop(
         lambda state: state[0] * cap <= most[0],

time: 103 us -> 102 us (level)
  no operation moved by 1% of the time
where the time goes in v11:
time: 102 us; the launch traced here: 101 us
  Pallas kernels  52.8 us (52%)
  starting transfers between devices  18.8 us (18%)
  blocking collectives  15.6 us (15%)
  waiting for transfers between devices  6.61 us (6%)
  local copies, waits for them, and re-layouts  6.17 us (6%)
    pallas_call x2, Pallas kernels, far_call(): pl.pallas_call(functools.partial(far_kernel, half_rel, last, ahead, devic...  27.2 us
    pallas_call x1, Pallas kernels, near_call(): pl.pallas_call(functools.partial(near_kernel, ahead), out_shape=(jax.Shap...  18.4 us
    all_to_all x1, blocking collectives, body(): lax.all_to_all(payload, 'ent', 0, 0)  15.6 us
    all_to_all x1, starting transfers between devices, send_round(): return lax.all_to_all(spread, BOTH, 0, 0).reshape(devices * cap, columns)  5.83 us
    all_to_all x1, starting transfers between devices, body(): table = lax.all_to_all(spread, BOTH, 0, 0).reshape(groups * slots, columns)  5.42 us
    all_to_all x1, waiting for transfers between devices, body(): lax.all_to_all(payload, 'rep', 0, 0)  4.77 us
    all_to_all x1, starting transfers between devices, body(): pieces = lax.all_to_all(offered, 'rep', 0, 0, tiled=True)  4.22 us
    unnamed x13, local copies, waits for them, and re-layouts  3.64 us
  transfers between devices with their start and end apart: 4, of which 2 were waited for; matrix products, arithmetic and copies ran while one was open for 2% of the time, Pallas kernels for 32%

profile of v11, /device:TPU:0, one launch (start us, length us, event | category | flops | bytes accessed | tf_op | source)
XLA Modules:
  0.0 101.4 jit_solution(14013505726370276319)
XLA Ops:
  0.6 0.0 copy-start.4
  0.6 0.0 copy-start.2
  0.7 2.4 %shard_map.140 = bf16[128,256]{1,0:T(8,128)(2,1)} custom-call(s32[1]{0:T(128)} %bitcast.8.base_ref, s32[1,128]{1,0:T(1,128)} %index_ref.1, bf16[2304,256]{1,0:T(8,128)(2,1)} %emb_ref.5), custom_call_target="tpu_custom_call" | custom-call | tf_op jit(solution)/shard_map/pallas_call | solution.py:538
  3.1 0.0 copy-done.4
  3.1 0.1 copy.17
  3.2 4.2 %all-to-all-start.1 = ((bf16[4,32,256]{2,1,0:T(8,128)(2,1)}), bf16[4,32,256]{2,1,0:T(8,128)(2,1)S(1)}, u32[]{:S(2)}, u32[]{:S(2)}) async-start(bf16[4,32,256]{2,1,0:T(8,128)(2,1)} %bitcast.41), calls=%async_computation.1 | async-start | bytes 131072 | tf_op jit(solution)/shard_map/all_to_all | solution.py:549
  7.4 0.7 pad_bitcast_fusion.relation_ref.rest_2_.rest_1_
  8.2 0.0 copy-done.2
  8.2 0.0 copy-start.5
  8.2 1.5 %copy.16 = bf16[2304,256]{0,1:T(8,128)(2,1)} copy(bf16[2304,256]{1,0:T(8,128)(2,1)S(1)} %copy-done.2) | data formatting | bytes 2359296 | tf_op args[0]
  9.7 0.0 copy-done.5
  9.7 1.8 %all-to-all-done.1 = bf16[4,32,256]{2,1,0:T(8,128)(2,1)S(1)} async-done(((bf16[4,32,256]{2,1,0:T(8,128)(2,1)}), bf16[4,32,256]{2,1,0:T(8,128)(2,1)S(1)}, u32[]{:S(2)}, u32[]{:S(2)}) %all-to-all-start.1) | async-done | bytes 65568 | tf_op jit(solution)/shard_map/all_to_all | solution.py:549
  11.6 0.8 broadcast_in_dim.74
  12.4 5.4 %all-to-all-start.2 = ((bf16[32,32,256]{2,1,0:T(8,128)(2,1)}), bf16[32,32,256]{2,1,0:T(8,128)(2,1)S(1)}, u32[]{:S(2)}, u32[]{:S(2)}) async-start(bf16[32,32,256]{2,1,0:T(8,128)(2,1)} %broadcast_in_dim.74), calls=%async_computation.2 | async-start | bytes 1048576 | tf_op jit(solution)/shard_map/all_to_all | solution.py:555
  17.8 18.4 %shard_map.141 = (bf16[9,2,256,768]{3,2,1,0:T(8,128)(2,1)}, s32[20]{0:T(128)}, s32[1]{0:T(128)}) custom-call(s32[1]{0:T(128)} %bitcast.7.base_ref, s32[256]{0:T(256)S(1)} %copy-done.5, s32[18,768]{1,0:T(8,128)} %src_ref.5, s32[18,768]{1,0:T(8,128)} %rel_ref.5, bf16[256,2304]{1,0:T(8,128)(2,1)} %bitcast.37, ...), custom_call_target="tpu_custom_call" | custom-call | flops 13287555072 | bytes 4718592 | tf_op jit(solution)/shard_map/pallas_call | solution.py:350
  36.3 0.0 all-to-all-done.2
  36.3 0.0 copy-start.3
  36.3 0.8 copy-done.3
  37.1 13.0 %shard_map.142 = (bf16[2304,256]{1,0:T(8,128)(2,1)}, bf16[264,256]{1,0:T(8,128)(2,1)S(1)}, f32[256,256]{1,0:T(8,128)}, s32[1,256]{1,0:T(1,128)S(1)}, s32[1]{0:T(128)}) custom-call(s32[1]{0:T(128)} %bitcast.7.base_ref, s32[20]{0:T(128)} %get-tuple-element.111.order_ref, s32[1]{0:T(128)} %get-tuple-element.112.wide_ref, s32[18,768]{1,0:T(8,128)} %src_ref.5, ...), custom_call_target="tpu_custom_call" | custom-call | flops 3623878656 | bytes 3538944 | tf_op jit(solution)/shard_map/pallas_call | solution.py:373
  50.1 0.6 while.12
  50.8 0.8 broadcast_in_dim.78
  51.5 5.8 %all-to-all-start.3 = ((bf16[32,24,256]{2,1,0:T(8,128)(2,1)}), bf16[32,24,256]{2,1,0:T(8,128)(2,1)S(1)}, u32[]{:S(2)}, u32[]{:S(2)}) async-start(bf16[32,24,256]{2,1,0:T(8,128)(2,1)} %broadcast_in_dim.78), calls=%async_computation.3 | async-start | bytes 786432 | tf_op jit(solution)/shard_map/all_to_all | solution.py:591
  57.4 0.0 copy-start.1
  57.4 14.2 %shard_map.143.hidden_hbm = bf16[2304,256]{1,0:T(8,128)(2,1)} custom-call(s32[1]{0:T(128)} %bitcast.7.base_ref, s32[20]{0:T(128)} %get-tuple-element.111.order_ref, s32[1]{0:T(128)} %get-tuple-element.112.wide_ref, s32[18,768]{1,0:T(8,128)} %src_ref.5, s32[18,768]{1,0:T(8,128)} %dst_ref.3, s32[18,768]{1,0:T(8,128)} %rel_ref.5, ...), custom_call_target="tpu_custom_call", output_to_operand_aliasing={{}: (14, {})} | custom-call | flops 3623878656 | bytes 3538944 | tf_op jit(solution)/shard_map/pallas_call | solution.py:373
  71.6 0.0 all-to-all-done.3
  71.6 0.0 copy-done.1
  71.6 0.0 copy-start
  71.6 1.3 %copy-done = bf16[2304,256]{1,0:T(8,128)(2,1)S(1)} copy-done((bf16[2304,256]{1,0:T(8,128)(2,1)S(1)}, bf16[2304,256]{1,0:T(8,128)(2,1)}, u32[]{:S(2)}) %copy-start) | copy-done | bytes 1179672
  72.9 3.0 %shard_map.144 = (f32[256,2304]{1,0:T(8,128)S(1)}, bf16[4,144,128]{2,1,0:T(8,128)(2,1)}) custom-call(bf16[768,256]{1,0:T(8,128)(2,1)S(1)} %bitcast.35, bf16[256,256]{1,0:T(8,128)(2,1)S(1)} %get-tuple-element.118.more_ref, s32[1,256]{1,0:T(1,128)S(1)} %get-tuple-element.244, s32[1,256]{1,0:T(1,128)S(1)} %bitcast.49, f32[256,256]{1,0:T(8,128)S(1)} %copy-done.1, ...), custom_call_target="tpu_custom_call" | custom-call | tf_op jit(solution)/shard_map/pallas_call | solution.py:626
  75.9 3.3 %all-to-all-start.4 = ((bf16[4,144,128]{2,1,0:T(8,128)(2,1)}), bf16[4,144,128]{2,1,0:T(8,128)(2,1)S(1)}, u32[]{:S(2)}, u32[]{:S(2)}) async-start(bf16[4,144,128]{2,1,0:T(8,128)(2,1)} %get-tuple-element.121), calls=%async_computation.4 | async-start | bytes 294912 | tf_op jit(solution)/shard_map/all_to_all | solution.py:647
  79.2 4.8 %all-to-all-done.4.received_ref = bf16[4,144,128]{2,1,0:T(8,128)(2,1)S(1)} async-done(((bf16[4,144,128]{2,1,0:T(8,128)(2,1)}), bf16[4,144,128]{2,1,0:T(8,128)(2,1)S(1)}, u32[]{:S(2)}, u32[]{:S(2)}) %all-to-all-start.4) | async-done | bytes 147488 | tf_op jit(solution)/shard_map/all_to_all | solution.py:647
  84.0 0.1 shard_map.145
  84.1 15.6 %all_to_all.38.received_ref = bf16[8,144,128]{2,1,0:T(8,128)(2,1)S(1)} all-to-all(bf16[8,144,128]{2,1,0:T(8,128)(2,1)S(1)} %shard_map.145), channel_id=1, replica_groups=mesh['ent'=8,'rep'=4] {'ent'}, dimensions={0} | all-to-all | bytes 589824 | tf_op jit(solution)/shard_map/all_to_all | solution.py:657
  99.7 1.7 %shard_map.146 = (f32[256,2304]{1,0:T(8,128)}, f32[64,256]{1,0:T(8,128)}) custom-call(s32[1]{0:T(128)} %bitcast.6.first_ref, bf16[8,144,128]{2,1,0:T(8,128)(2,1)S(1)} %all_to_all.38.received_ref, f32[256,2304]{1,0:T(8,128)S(1)} %get-tuple-element.122.scores_ref), custom_call_target="tpu_custom_call" | custom-call | tf_op jit(solution)/shard_map/pallas_call | solution.py:648
  (4 shorter events, 0.0 us)
Async XLA Ops:
  0.6 2.4 %copy-start.4 = (bf16[474,256]{1,0:T(8,128)(2,1)S(1)}, bf16[474,256]{1,0:T(8,128)(2,1)}, u32[]{:S(2)}) copy-start(bf16[474,256]{1,0:T(8,128)(2,1)} %param.16) | copy-start | bytes 728068
  0.6 7.5 %copy-start.2 = (bf16[2304,256]{1,0:T(8,128)(2,1)S(1)}, bf16[2304,256]{1,0:T(8,128)(2,1)}, u32[]{:S(2)}) copy-start(bf16[2304,256]{1,0:T(8,128)(2,1)} %emb_ref.5) | copy-start | bytes 3538948
  3.2 8.3 %all-to-all-start.1 = ((bf16[4,32,256]{2,1,0:T(8,128)(2,1)}), bf16[4,32,256]{2,1,0:T(8,128)(2,1)S(1)}, u32[]{:S(2)}, u32[]{:S(2)}) async-start(bf16[4,32,256]{2,1,0:T(8,128)(2,1)} %bitcast.41), calls=%async_computation.1 | async-start | bytes 131072 | tf_op jit(solution)/shard_map/all_to_all | solution.py:549
  8.2 1.5 %copy-start.5 = (s32[256]{0:T(256)S(1)}, s32[256]{0:T(256)}, u32[]{:S(2)}) copy-start(s32[256]{0:T(256)} %head_ref.1) | copy-start | bytes 3076
  12.4 23.9 %all-to-all-start.2 = ((bf16[32,32,256]{2,1,0:T(8,128)(2,1)}), bf16[32,32,256]{2,1,0:T(8,128)(2,1)S(1)}, u32[]{:S(2)}, u32[]{:S(2)}) async-start(bf16[32,32,256]{2,1,0:T(8,128)(2,1)} %broadcast_in_dim.74), calls=%async_computation.2 | async-start | bytes 1048576 | tf_op jit(solution)/shard_map/all_to_all | solution.py:555
  36.3 0.8 copy-start.3
  51.5 20.1 %all-to-all-start.3 = ((bf16[32,24,256]{2,1,0:T(8,128)(2,1)}), bf16[32,24,256]{2,1,0:T(8,128)(2,1)S(1)}, u32[]{:S(2)}, u32[]{:S(2)}) async-start(bf16[32,24,256]{2,1,0:T(8,128)(2,1)} %broadcast_in_dim.78), calls=%async_computation.3 | async-start | bytes 786432 | tf_op jit(solution)/shard_map/all_to_all | solution.py:591
  57.4 14.2 %copy-start.1 = (f32[256,256]{1,0:T(8,128)S(1)}, f32[256,256]{1,0:T(8,128)}, u32[]{:S(2)}) copy-start(f32[256,256]{1,0:T(8,128)} %get-tuple-element.119.factor_hbm) | copy-start | bytes 786436
  71.6 1.3 %copy-start = (bf16[2304,256]{1,0:T(8,128)(2,1)S(1)}, bf16[2304,256]{1,0:T(8,128)(2,1)}, u32[]{:S(2)}) copy-start(bf16[2304,256]{1,0:T(8,128)(2,1)} %shard_map.143.hidden_hbm) | copy-start | bytes 3538948
  75.9 8.1 %all-to-all-start.4 = ((bf16[4,144,128]{2,1,0:T(8,128)(2,1)}), bf16[4,144,128]{2,1,0:T(8,128)(2,1)S(1)}, u32[]{:S(2)}, u32[]{:S(2)}) async-start(bf16[4,144,128]{2,1,0:T(8,128)(2,1)} %get-tuple-element.121), calls=%async_computation.4 | async-start | bytes 294912 | tf_op jit(solution)/shard_map/all_to_all | solution.py:647

commit v12 on v7

--- a/solution.py
+++ b/solution.py
@@ -143,10 +143,10 @@
 ):
     far_t_ref, gathered_ref, agg_ref, held_ref, own_ref, made_ref, sems, own_sems, out_sems = rest[-9:]
     if last:
-        near_ref, query_rel_ref, relation_ref, rel_weight_ref, _ = rest[:5]
-        hidden_ref, factor_ref = rest[5:7]
+        near_ref, relation_ref, _, hidden_ref = rest[:4]
     else:
-        head_ref, mixed_ref, hidden_ref, heads_ref, rank_ref, most_ref = rest[:6]
+        head_ref, query_rel_ref, relation_ref, rel_weight_ref, mixed_ref = rest[:5]
+        hidden_ref, heads_ref, factor_ref, rank_ref, most_ref = rest[5:10]
     blocks = src_ref.shape[0]
     rows_dev = blocks * BLK
     far_chunks = far_ref.shape[0]
@@ -282,7 +282,7 @@
         for u in range(STEP):
             give(stop - 1, u).start()
 
-    if last:
+    if not last:
         picks = one_hot(query_rel_ref[...], relation_ref.shape[1])
         rows = lax.dot_general(
             picks, relation_ref[...], (((0,), (1,)), ((), ())), preferred_element_type=F32
@@ -290,7 +290,6 @@
         factor_ref[...] = jnp.dot(
             rows.astype(BF16), rel_weight_ref[...], preferred_element_type=F32
         )
-    else:
         picks = one_hot_wide(head_ref[...] - base_ref[0] * BLK, rows_dev)
         rows = lax.dot_general(picks, made_ref[...], TN, preferred_element_type=F32)
         rank = ranks(owners(head_ref[...], devices, rows_dev))
@@ -350,7 +349,7 @@
         functools.partial(far_kernel, half_rel, last, ahead, devices),
         out_shape=(jax.ShapeDtypeStruct((rows_dev, columns), BF16),) + outs,
         in_specs=[SMEM] * 2 + [WHOLE] * 3 + [HBM] + [WHOLE] * (5 + len(more)) + [HBM],
-        out_specs=(HBM, WHOLE) if last else (HBM, WHOLE, WHOLE, SMEM),
+        out_specs=(HBM,) if last else (HBM, WHOLE, WHOLE, WHOLE, SMEM),
         input_output_aliases={11 + len(more): 0} if last else {},
         scratch_shapes=[
             pltpu.VMEM((far.shape[0], columns, CHUNK), BF16),
@@ -541,7 +540,7 @@
     weights = (in_weight, out_weight, loop_weight, loop_rel[None])
     edges = (edge_src, edge_dst, edge_rel)
     cap = min(queries, -(-3 * queries // (8 * devices)) * 8)
-    hidden, heads, rank, most = far_call(
+    hidden, heads, query_factor, rank, most = far_call(
         relations // 2,
         False,
         ahead,
@@ -551,10 +550,11 @@
         entity_emb,
         far,
         weights,
-        (head_row,),
+        (head_row, query_rel[None], relation_t, rel_weight),
         mixed,
         (
             jax.ShapeDtypeStruct((-(-queries // cap) * cap, columns), BF16),
+            jax.ShapeDtypeStruct((queries, columns), F32),
             jax.ShapeDtypeStruct((1, queries), jnp.int32),
             jax.ShapeDtypeStruct((1,), jnp.int32),
         ),
@@ -574,7 +574,7 @@
         return turn + 1, jnp.where(inside[:, None], rows, more)
 
     sent = send_round(0)
-    hidden, query_factor = far_call(
+    (hidden,) = far_call(
         relations // 2,
         True,
         ahead,
@@ -584,9 +584,9 @@
         entity_emb,
         far,
         weights,
-        (near_t, query_rel[None], relation_t, rel_weight),
+        (near_t, relation_t),
         hidden,
-        (jax.ShapeDtypeStruct((queries, columns), F32),),
+        (),
     )
     _, more_heads = lax.while_loop(
         lambda state: state[0] * cap <= most[0],

time: 103 us -> 102 us (level)
  no operation moved by 1% of the time
where the time goes in v12:
time: 102 us; the launch traced here: 101 us
  Pallas kernels  52.7 us (52%)
  starting transfers between devices  18.8 us (18%)
  blocking collectives  15.6 us (15%)
  waiting for transfers between devices  6.61 us (6%)
  local copies, waits for them, and re-layouts  6.17 us (6%)
    pallas_call x2, Pallas kernels, far_call(): pl.pallas_call(functools.partial(far_kernel, half_rel, last, ahead, devic...  27.2 us
    pallas_call x1, Pallas kernels, near_call(): pl.pallas_call(functools.partial(near_kernel, ahead), out_shape=(jax.Shap...  18.3 us
    all_to_all x1, blocking collectives, body(): lax.all_to_all(payload, 'ent', 0, 0)  15.6 us
    all_to_all x1, starting transfers between devices, send_round(): return lax.all_to_all(spread, BOTH, 0, 0).reshape(devices * cap, columns)  5.82 us
    all_to_all x1, starting transfers between devices, body(): table = lax.all_to_all(spread, BOTH, 0, 0).reshape(groups * slots, columns)  5.42 us
    all_to_all x1, waiting for transfers between devices, body(): lax.all_to_all(payload, 'rep', 0, 0)  4.77 us
    all_to_all x1, starting transfers between devices, body(): pieces = lax.all_to_all(offered, 'rep', 0, 0, tiled=True)  4.22 us
    unnamed x13, local copies, waits for them, and re-layouts  3.64 us
  transfers between devices with their start and end apart: 4, of which 2 were waited for; matrix products, arithmetic and copies ran while one was open for 2% of the time, Pallas kernels for 32%

profile of v12, /device:TPU:0, one launch (start us, length us, event | category | flops | bytes accessed | tf_op | source)
XLA Modules:
  0.0 101.4 jit_solution(4052329583147423674)
XLA Ops:
  0.6 0.0 copy-start.4
  0.6 0.0 copy-start.2
  0.7 2.4 %shard_map.140 = bf16[128,256]{1,0:T(8,128)(2,1)} custom-call(s32[1]{0:T(128)} %bitcast.8.base_ref, s32[1,128]{1,0:T(1,128)} %index_ref.1, bf16[2304,256]{1,0:T(8,128)(2,1)} %emb_ref.5), custom_call_target="tpu_custom_call" | custom-call | tf_op jit(solution)/shard_map/pallas_call | solution.py:513
  3.1 0.0 copy-done.4
  3.1 0.1 copy.17
  3.2 4.2 %all-to-all-start.1 = ((bf16[4,32,256]{2,1,0:T(8,128)(2,1)}), bf16[4,32,256]{2,1,0:T(8,128)(2,1)S(1)}, u32[]{:S(2)}, u32[]{:S(2)}) async-start(bf16[4,32,256]{2,1,0:T(8,128)(2,1)} %bitcast.41), calls=%async_computation.1 | async-start | bytes 131072 | tf_op jit(solution)/shard_map/all_to_all | solution.py:524
  7.4 0.7 pad_bitcast_fusion.relation_ref.rest_2_.rest_1_
  8.2 0.0 copy-done.2
  8.2 0.0 copy-start.5
  8.2 1.5 %copy.16 = bf16[2304,256]{0,1:T(8,128)(2,1)} copy(bf16[2304,256]{1,0:T(8,128)(2,1)S(1)} %copy-done.2) | data formatting | bytes 2359296 | tf_op args[0]
  9.7 0.0 copy-done.5
  9.7 1.8 %all-to-all-done.1 = bf16[4,32,256]{2,1,0:T(8,128)(2,1)S(1)} async-done(((bf16[4,32,256]{2,1,0:T(8,128)(2,1)}), bf16[4,32,256]{2,1,0:T(8,128)(2,1)S(1)}, u32[]{:S(2)}, u32[]{:S(2)}) %all-to-all-start.1) | async-done | bytes 65568 | tf_op jit(solution)/shard_map/all_to_all | solution.py:524
  11.6 0.8 broadcast_in_dim.74
  12.4 5.4 %all-to-all-start.2 = ((bf16[32,32,256]{2,1,0:T(8,128)(2,1)}), bf16[32,32,256]{2,1,0:T(8,128)(2,1)S(1)}, u32[]{:S(2)}, u32[]{:S(2)}) async-start(bf16[32,32,256]{2,1,0:T(8,128)(2,1)} %broadcast_in_dim.74), calls=%async_computation.2 | async-start | bytes 1048576 | tf_op jit(solution)/shard_map/all_to_all | solution.py:530
  17.8 18.3 %shard_map.141 = (bf16[9,2,256,768]{3,2,1,0:T(8,128)(2,1)}, s32[20]{0:T(128)}) custom-call(s32[1]{0:T(128)} %bitcast.7.base_ref, s32[256]{0:T(256)S(1)} %copy-done.5, s32[18,768]{1,0:T(8,128)} %src_ref.5, s32[18,768]{1,0:T(8,128)} %rel_ref.5, bf16[256,2304]{1,0:T(8,128)(2,1)} %bitcast.37, bf16[256,512]{1,0:T(8,128)(2,1)} %pad_bitcast_fusion.relation_ref.rest_2_.rest_1_), custom_call_target="tpu_custom_call" | custom-call | flops 13287555072 | bytes 4718592 | tf_op jit(solution)/shard_map/pallas_call | solution.py:326
  36.1 0.0 all-to-all-done.2
  36.2 0.0 copy-start.3
  36.2 0.8 copy-done.3
  37.0 13.3 %shard_map.142 = (bf16[2304,256]{1,0:T(8,128)(2,1)}, bf16[264,256]{1,0:T(8,128)(2,1)S(1)}, f32[256,256]{1,0:T(8,128)}, s32[1,256]{1,0:T(1,128)S(1)}, s32[1]{0:T(128)}) custom-call(s32[1]{0:T(128)} %bitcast.7.base_ref, s32[20]{0:T(128)} %get-tuple-element.110.order_ref, s32[18,768]{1,0:T(8,128)} %src_ref.5, s32[18,768]{1,0:T(8,128)} %dst_ref.3, ...), custom_call_target="tpu_custom_call" | custom-call | flops 3623878656 | bytes 3538944 | tf_op jit(solution)/shard_map/pallas_call | solution.py:348
  50.3 0.7 while.12
  51.0 0.8 broadcast_in_dim.78
  51.8 5.8 %all-to-all-start.3 = ((bf16[32,24,256]{2,1,0:T(8,128)(2,1)}), bf16[32,24,256]{2,1,0:T(8,128)(2,1)S(1)}, u32[]{:S(2)}, u32[]{:S(2)}) async-start(bf16[32,24,256]{2,1,0:T(8,128)(2,1)} %broadcast_in_dim.78), calls=%async_computation.3 | async-start | bytes 786432 | tf_op jit(solution)/shard_map/all_to_all | solution.py:566
  57.6 0.0 copy-start.1
  57.7 13.9 %shard_map.143.hidden_hbm = bf16[2304,256]{1,0:T(8,128)(2,1)} custom-call(s32[1]{0:T(128)} %bitcast.7.base_ref, s32[20]{0:T(128)} %get-tuple-element.110.order_ref, s32[18,768]{1,0:T(8,128)} %src_ref.5, s32[18,768]{1,0:T(8,128)} %dst_ref.3, s32[18,768]{1,0:T(8,128)} %rel_ref.5, bf16[2304,256]{1,0:T(8,128)(2,1)} %emb_ref.5, ...), custom_call_target="tpu_custom_call", output_to_operand_aliasing={{}: (13, {})} | custom-call | flops 3623878656 | bytes 3538944 | tf_op jit(solution)/shard_map/pallas_call | solution.py:348
  71.5 0.0 all-to-all-done.3
  71.5 0.0 copy-done.1
  71.5 0.0 copy-start
  71.5 1.3 %copy-done = bf16[2304,256]{1,0:T(8,128)(2,1)S(1)} copy-done((bf16[2304,256]{1,0:T(8,128)(2,1)S(1)}, bf16[2304,256]{1,0:T(8,128)(2,1)}, u32[]{:S(2)}) %copy-start) | copy-done | bytes 1179672
  72.8 3.0 %shard_map.144 = (f32[256,2304]{1,0:T(8,128)S(1)}, bf16[4,144,128]{2,1,0:T(8,128)(2,1)}) custom-call(bf16[768,256]{1,0:T(8,128)(2,1)S(1)} %bitcast.35, bf16[256,256]{1,0:T(8,128)(2,1)S(1)} %get-tuple-element.116.more_ref, s32[1,256]{1,0:T(1,128)S(1)} %get-tuple-element.242, s32[1,256]{1,0:T(1,128)S(1)} %bitcast.49, f32[256,256]{1,0:T(8,128)S(1)} %copy-done.1, ...), custom_call_target="tpu_custom_call" | custom-call | tf_op jit(solution)/shard_map/pallas_call | solution.py:601
  75.8 3.3 %all-to-all-start.4 = ((bf16[4,144,128]{2,1,0:T(8,128)(2,1)}), bf16[4,144,128]{2,1,0:T(8,128)(2,1)S(1)}, u32[]{:S(2)}, u32[]{:S(2)}) async-start(bf16[4,144,128]{2,1,0:T(8,128)(2,1)} %get-tuple-element.119), calls=%async_computation.4 | async-start | bytes 294912 | tf_op jit(solution)/shard_map/all_to_all | solution.py:622
  79.1 4.8 %all-to-all-done.4.received_ref = bf16[4,144,128]{2,1,0:T(8,128)(2,1)S(1)} async-done(((bf16[4,144,128]{2,1,0:T(8,128)(2,1)}), bf16[4,144,128]{2,1,0:T(8,128)(2,1)S(1)}, u32[]{:S(2)}, u32[]{:S(2)}) %all-to-all-start.4) | async-done | bytes 147488 | tf_op jit(solution)/shard_map/all_to_all | solution.py:622
  83.9 0.1 shard_map.145
  84.0 15.6 %all_to_all.38.received_ref = bf16[8,144,128]{2,1,0:T(8,128)(2,1)S(1)} all-to-all(bf16[8,144,128]{2,1,0:T(8,128)(2,1)S(1)} %shard_map.145), channel_id=1, replica_groups=mesh['ent'=8,'rep'=4] {'ent'}, dimensions={0} | all-to-all | bytes 589824 | tf_op jit(solution)/shard_map/all_to_all | solution.py:632
  99.6 1.7 %shard_map.146 = (f32[256,2304]{1,0:T(8,128)}, f32[64,256]{1,0:T(8,128)}) custom-call(s32[1]{0:T(128)} %bitcast.6.first_ref, bf16[8,144,128]{2,1,0:T(8,128)(2,1)S(1)} %all_to_all.38.received_ref, f32[256,2304]{1,0:T(8,128)S(1)} %get-tuple-element.120.scores_ref), custom_call_target="tpu_custom_call" | custom-call | tf_op jit(solution)/shard_map/pallas_call | solution.py:623
  (4 shorter events, 0.0 us)
Async XLA Ops:
  0.6 2.4 %copy-start.4 = (bf16[474,256]{1,0:T(8,128)(2,1)S(1)}, bf16[474,256]{1,0:T(8,128)(2,1)}, u32[]{:S(2)}) copy-start(bf16[474,256]{1,0:T(8,128)(2,1)} %param.16) | copy-start | bytes 728068
  0.6 7.5 %copy-start.2 = (bf16[2304,256]{1,0:T(8,128)(2,1)S(1)}, bf16[2304,256]{1,0:T(8,128)(2,1)}, u32[]{:S(2)}) copy-start(bf16[2304,256]{1,0:T(8,128)(2,1)} %emb_ref.5) | copy-start | bytes 3538948
  3.2 8.3 %all-to-all-start.1 = ((bf16[4,32,256]{2,1,0:T(8,128)(2,1)}), bf16[4,32,256]{2,1,0:T(8,128)(2,1)S(1)}, u32[]{:S(2)}, u32[]{:S(2)}) async-start(bf16[4,32,256]{2,1,0:T(8,128)(2,1)} %bitcast.41), calls=%async_computation.1 | async-start | bytes 131072 | tf_op jit(solution)/shard_map/all_to_all | solution.py:524
  8.2 1.5 %copy-start.5 = (s32[256]{0:T(256)S(1)}, s32[256]{0:T(256)}, u32[]{:S(2)}) copy-start(s32[256]{0:T(256)} %head_ref.1) | copy-start | bytes 3076
  12.4 23.7 %all-to-all-start.2 = ((bf16[32,32,256]{2,1,0:T(8,128)(2,1)}), bf16[32,32,256]{2,1,0:T(8,128)(2,1)S(1)}, u32[]{:S(2)}, u32[]{:S(2)}) async-start(bf16[32,32,256]{2,1,0:T(8,128)(2,1)} %broadcast_in_dim.74), calls=%async_computation.2 | async-start | bytes 1048576 | tf_op jit(solution)/shard_map/all_to_all | solution.py:530
  36.2 0.8 copy-start.3
  51.8 19.7 %all-to-all-start.3 = ((bf16[32,24,256]{2,1,0:T(8,128)(2,1)}), bf16[32,24,256]{2,1,0:T(8,128)(2,1)S(1)}, u32[]{:S(2)}, u32[]{:S(2)}) async-start(bf16[32,24,256]{2,1,0:T(8,128)(2,1)} %broadcast_in_dim.78), calls=%async_computation.3 | async-start | bytes 786432 | tf_op jit(solution)/shard_map/all_to_all | solution.py:566
  57.6 13.9 %copy-start.1 = (f32[256,256]{1,0:T(8,128)S(1)}, f32[256,256]{1,0:T(8,128)}, u32[]{:S(2)}) copy-start(f32[256,256]{1,0:T(8,128)} %get-tuple-element.117.factor_hbm) | copy-start | bytes 786436
  71.5 1.3 %copy-start = (bf16[2304,256]{1,0:T(8,128)(2,1)S(1)}, bf16[2304,256]{1,0:T(8,128)(2,1)}, u32[]{:S(2)}) copy-start(bf16[2304,256]{1,0:T(8,128)(2,1)} %shard_map.143.hidden_hbm) | copy-start | bytes 3538948
  75.8 8.1 %all-to-all-start.4 = ((bf16[4,144,128]{2,1,0:T(8,128)(2,1)}), bf16[4,144,128]{2,1,0:T(8,128)(2,1)S(1)}, u32[]{:S(2)}, u32[]{:S(2)}) async-start(bf16[4,144,128]{2,1,0:T(8,128)(2,1)} %get-tuple-element.119), calls=%async_computation.4 | async-start | bytes 294912 | tf_op jit(solution)/shard_map/all_to_all | solution.py:622

commit v13 on v12

--- a/solution.py
+++ b/solution.py
@@ -468,17 +468,26 @@
         payload_ref[peer] = block
 
 
-def last_kernel(first_ref, received_ref, scores_ref, log_probs_ref, expected_ref):
+def last_kernel(
+    first_ref, received_ref, scores_ref, log_probs_ref, expected_ref, made_ref, sems
+):
     first = first_ref[0]
     left, right, tops, totals = merge(received_ref[...].astype(F32), first)
+    copies = []
     for half in range(2):
         norm = column(tops[half] + jnp.log(totals[half]), 0, LANES)
         rows = pl.ds(half * LANES, LANES)
-        log_probs_ref[rows, :] = scores_ref[rows, :] - norm
+        made_ref[rows, :] = scores_ref[rows, :] - norm
+        copies.append(
+            pltpu.make_async_copy(made_ref.at[rows], log_probs_ref.at[rows], sems.at[half])
+        )
+        copies[half].start()
     total = jnp.where(first >= LANES, totals[1], totals[0])
     total = column(total, lax.rem(first, LANES), left.shape[0])
     expected_ref[:, :LANES] = left / total
     expected_ref[:, LANES:] = right / total
+    for copy in copies:
+        copy.wait()
 
 
 def body(
@@ -627,7 +636,11 @@
             jax.ShapeDtypeStruct((batch_rows, columns), F32),
         ),
         in_specs=[SMEM, WHOLE, WHOLE],
-        out_specs=(WHOLE, WHOLE),
+        out_specs=(HBM, WHOLE),
+        scratch_shapes=[
+            pltpu.VMEM((queries, rows_dev), F32),
+            pltpu.SemaphoreType.DMA((2,)),
+        ],
         compiler_params=few,
     )(first, lax.all_to_all(payload, "ent", 0, 0), scores)
     return (log_probs, expected_tail)

time: 102 us -> 104 us (1.020)
  starting transfers between devices: 18.8 us -> 20.8 us
    all_to_all x1, starting transfers between devices: 5.82 us -> 7.78 us  [send_round(): return lax.all_to_all(spread, BOTH, 0, 0).reshape(devices * cap, columns)]
  transfers between devices with their start and end apart: 4 -> 4, of which waited for: 2 -> 2; matrix products, arithmetic and copies ran while one was open for 2% -> 2% of each run, Pallas kernels for 32% -> 31%
where the time goes in v13:
time: 104 us
  Pallas kernels  53.2 us (51%)
  starting transfers between devices  20.8 us (20%)
  blocking collectives  15.6 us (15%)
  waiting for transfers between devices  6.61 us (6%)
  local copies, waits for them, and re-layouts  6.17 us (6%)
    pallas_call x2, Pallas kernels, far_call(): pl.pallas_call(functools.partial(far_kernel, half_rel, last, ahead, devic...  27.1 us
    pallas_call x1, Pallas kernels, near_call(): pl.pallas_call(functools.partial(near_kernel, ahead), out_shape=(jax.Shap...  18.3 us
    all_to_all x1, blocking collectives, body(): lax.all_to_all(payload, 'ent', 0, 0)  15.6 us
    all_to_all x1, starting transfers between devices, send_round(): return lax.all_to_all(spread, BOTH, 0, 0).reshape(devices * cap, columns)  7.78 us
    all_to_all x1, starting transfers between devices, body(): table = lax.all_to_all(spread, BOTH, 0, 0).reshape(groups * slots, columns)  5.42 us
    all_to_all x1, waiting for transfers between devices, body(): lax.all_to_all(payload, 'rep', 0, 0)  4.77 us
    all_to_all x1, starting transfers between devices, body(): pieces = lax.all_to_all(offered, 'rep', 0, 0, tiled=True)  4.22 us
    unnamed x13, local copies, waits for them, and re-layouts  3.64 us
  transfers between devices with their start and end apart: 4, of which 2 were waited for; matrix products, arithmetic and copies ran while one was open for 2% of the time, Pallas kernels for 31%

profile of v13, /device:TPU:0, one launch (start us, length us, event | category | flops | bytes accessed | tf_op | source)
XLA Modules:
  0.0 104.0 jit_solution(11223682954649265564)
XLA Ops:
  0.6 0.0 copy-start.4
  0.6 0.0 copy-start.2
  0.7 2.4 %shard_map.140 = bf16[128,256]{1,0:T(8,128)(2,1)} custom-call(s32[1]{0:T(128)} %bitcast.8.base_ref, s32[1,128]{1,0:T(1,128)} %index_ref.1, bf16[2304,256]{1,0:T(8,128)(2,1)} %emb_ref.5), custom_call_target="tpu_custom_call" | custom-call | tf_op jit(solution)/shard_map/pallas_call | solution.py:522
  3.1 0.0 copy-done.4
  3.1 0.1 copy.17
  3.2 4.2 %all-to-all-start.1 = ((bf16[4,32,256]{2,1,0:T(8,128)(2,1)}), bf16[4,32,256]{2,1,0:T(8,128)(2,1)S(1)}, u32[]{:S(2)}, u32[]{:S(2)}) async-start(bf16[4,32,256]{2,1,0:T(8,128)(2,1)} %bitcast.41), calls=%async_computation.1 | async-start | bytes 131072 | tf_op jit(solution)/shard_map/all_to_all | solution.py:533
  7.4 0.7 pad_bitcast_fusion.relation_ref.rest_2_.rest_1_
  8.2 0.0 copy-done.2
  8.2 0.0 copy-start.5
  8.2 1.5 %copy.16 = bf16[2304,256]{0,1:T(8,128)(2,1)} copy(bf16[2304,256]{1,0:T(8,128)(2,1)S(1)} %copy-done.2) | data formatting | bytes 2359296 | tf_op args[0]
  9.7 0.0 copy-done.5
  9.7 1.8 %all-to-all-done.1 = bf16[4,32,256]{2,1,0:T(8,128)(2,1)S(1)} async-done(((bf16[4,32,256]{2,1,0:T(8,128)(2,1)}), bf16[4,32,256]{2,1,0:T(8,128)(2,1)S(1)}, u32[]{:S(2)}, u32[]{:S(2)}) %all-to-all-start.1) | async-done | bytes 65568 | tf_op jit(solution)/shard_map/all_to_all | solution.py:533
  11.6 0.8 broadcast_in_dim.74
  12.4 5.4 %all-to-all-start.2 = ((bf16[32,32,256]{2,1,0:T(8,128)(2,1)}), bf16[32,32,256]{2,1,0:T(8,128)(2,1)S(1)}, u32[]{:S(2)}, u32[]{:S(2)}) async-start(bf16[32,32,256]{2,1,0:T(8,128)(2,1)} %broadcast_in_dim.74), calls=%async_computation.2 | async-start | bytes 1048576 | tf_op jit(solution)/shard_map/all_to_all | solution.py:539
  17.8 18.3 %shard_map.141 = (bf16[9,2,256,768]{3,2,1,0:T(8,128)(2,1)}, s32[20]{0:T(128)}) custom-call(s32[1]{0:T(128)} %bitcast.7.base_ref, s32[256]{0:T(256)S(1)} %copy-done.5, s32[18,768]{1,0:T(8,128)} %src_ref.5, s32[18,768]{1,0:T(8,128)} %rel_ref.5, bf16[256,2304]{1,0:T(8,128)(2,1)} %bitcast.37, bf16[256,512]{1,0:T(8,128)(2,1)} %pad_bitcast_fusion.relation_ref.rest_2_.rest_1_), custom_call_target="tpu_custom_call" | custom-call | flops 13287555072 | bytes 4718592 | tf_op jit(solution)/shard_map/pallas_call | solution.py:326
  36.1 0.0 all-to-all-done.2
  36.2 0.0 copy-start.3
  36.2 0.8 copy-done.3
  37.0 13.3 %shard_map.142 = (bf16[2304,256]{1,0:T(8,128)(2,1)}, bf16[264,256]{1,0:T(8,128)(2,1)S(1)}, f32[256,256]{1,0:T(8,128)}, s32[1,256]{1,0:T(1,128)S(1)}, s32[1]{0:T(128)}) custom-call(s32[1]{0:T(128)} %bitcast.7.base_ref, s32[20]{0:T(128)} %get-tuple-element.110.order_ref, s32[18,768]{1,0:T(8,128)} %src_ref.5, s32[18,768]{1,0:T(8,128)} %dst_ref.3, ...), custom_call_target="tpu_custom_call" | custom-call | flops 3623878656 | bytes 3538944 | tf_op jit(solution)/shard_map/pallas_call | solution.py:348
  50.3 0.7 while.12
  51.0 0.8 broadcast_in_dim.78
  51.8 7.8 %all-to-all-start.3 = ((bf16[32,24,256]{2,1,0:T(8,128)(2,1)}), bf16[32,24,256]{2,1,0:T(8,128)(2,1)S(1)}, u32[]{:S(2)}, u32[]{:S(2)}) async-start(bf16[32,24,256]{2,1,0:T(8,128)(2,1)} %broadcast_in_dim.78), calls=%async_computation.3 | async-start | bytes 786432 | tf_op jit(solution)/shard_map/all_to_all | solution.py:575
  59.6 0.0 copy-start.1
  59.6 13.9 %shard_map.143.hidden_hbm = bf16[2304,256]{1,0:T(8,128)(2,1)} custom-call(s32[1]{0:T(128)} %bitcast.7.base_ref, s32[20]{0:T(128)} %get-tuple-element.110.order_ref, s32[18,768]{1,0:T(8,128)} %src_ref.5, s32[18,768]{1,0:T(8,128)} %dst_ref.3, s32[18,768]{1,0:T(8,128)} %rel_ref.5, bf16[2304,256]{1,0:T(8,128)(2,1)} %emb_ref.5, ...), custom_call_target="tpu_custom_call", output_to_operand_aliasing={{}: (13, {})} | custom-call | flops 3623878656 | bytes 3538944 | tf_op jit(solution)/shard_map/pallas_call | solution.py:348
  73.5 0.0 all-to-all-done.3
  73.5 0.0 copy-done.1
  73.5 0.0 copy-start
  73.5 1.3 %copy-done = bf16[2304,256]{1,0:T(8,128)(2,1)S(1)} copy-done((bf16[2304,256]{1,0:T(8,128)(2,1)S(1)}, bf16[2304,256]{1,0:T(8,128)(2,1)}, u32[]{:S(2)}) %copy-start) | copy-done | bytes 1179672
  74.8 3.0 %shard_map.144 = (f32[256,2304]{1,0:T(8,128)S(1)}, bf16[4,144,128]{2,1,0:T(8,128)(2,1)}) custom-call(bf16[768,256]{1,0:T(8,128)(2,1)S(1)} %bitcast.35, bf16[256,256]{1,0:T(8,128)(2,1)S(1)} %get-tuple-element.116.more_ref, s32[1,256]{1,0:T(1,128)S(1)} %get-tuple-element.242, s32[1,256]{1,0:T(1,128)S(1)} %bitcast.49, f32[256,256]{1,0:T(8,128)S(1)} %copy-done.1, ...), custom_call_target="tpu_custom_call" | custom-call | tf_op jit(solution)/shard_map/pallas_call | solution.py:610
  77.7 3.3 %all-to-all-start.4 = ((bf16[4,144,128]{2,1,0:T(8,128)(2,1)}), bf16[4,144,128]{2,1,0:T(8,128)(2,1)S(1)}, u32[]{:S(2)}, u32[]{:S(2)}) async-start(bf16[4,144,128]{2,1,0:T(8,128)(2,1)} %get-tuple-element.119), calls=%async_computation.4 | async-start | bytes 294912 | tf_op jit(solution)/shard_map/all_to_all | solution.py:631
  81.1 4.8 %all-to-all-done.4.received_ref = bf16[4,144,128]{2,1,0:T(8,128)(2,1)S(1)} async-done(((bf16[4,144,128]{2,1,0:T(8,128)(2,1)}), bf16[4,144,128]{2,1,0:T(8,128)(2,1)S(1)}, u32[]{:S(2)}, u32[]{:S(2)}) %all-to-all-start.4) | async-done | bytes 147488 | tf_op jit(solution)/shard_map/all_to_all | solution.py:631
  85.9 0.1 shard_map.145
  86.0 15.6 %all_to_all.38.received_ref = bf16[8,144,128]{2,1,0:T(8,128)(2,1)S(1)} all-to-all(bf16[8,144,128]{2,1,0:T(8,128)(2,1)S(1)} %shard_map.145), channel_id=1, replica_groups=mesh['ent'=8,'rep'=4] {'ent'}, dimensions={0} | all-to-all | bytes 589824 | tf_op jit(solution)/shard_map/all_to_all | solution.py:645
  101.6 2.3 %shard_map.146 = (f32[256,2304]{1,0:T(8,128)}, f32[64,256]{1,0:T(8,128)}) custom-call(s32[1]{0:T(128)} %bitcast.6.first_ref, bf16[8,144,128]{2,1,0:T(8,128)(2,1)S(1)} %all_to_all.38.received_ref, f32[256,2304]{1,0:T(8,128)S(1)} %get-tuple-element.120.scores_ref), custom_call_target="tpu_custom_call" | custom-call | tf_op jit(solution)/shard_map/pallas_call | solution.py:632
  (4 shorter events, 0.0 us)
Async XLA Ops:
  0.6 2.4 %copy-start.4 = (bf16[474,256]{1,0:T(8,128)(2,1)S(1)}, bf16[474,256]{1,0:T(8,128)(2,1)}, u32[]{:S(2)}) copy-start(bf16[474,256]{1,0:T(8,128)(2,1)} %param.16) | copy-start | bytes 728068
  0.6 7.5 %copy-start.2 = (bf16[2304,256]{1,0:T(8,128)(2,1)S(1)}, bf16[2304,256]{1,0:T(8,128)(2,1)}, u32[]{:S(2)}) copy-start(bf16[2304,256]{1,0:T(8,128)(2,1)} %emb_ref.5) | copy-start | bytes 3538948
  3.2 8.3 %all-to-all-start.1 = ((bf16[4,32,256]{2,1,0:T(8,128)(2,1)}), bf16[4,32,256]{2,1,0:T(8,128)(2,1)S(1)}, u32[]{:S(2)}, u32[]{:S(2)}) async-start(bf16[4,32,256]{2,1,0:T(8,128)(2,1)} %bitcast.41), calls=%async_computation.1 | async-start | bytes 131072 | tf_op jit(solution)/shard_map/all_to_all | solution.py:533
  8.2 1.5 %copy-start.5 = (s32[256]{0:T(256)S(1)}, s32[256]{0:T(256)}, u32[]{:S(2)}) copy-start(s32[256]{0:T(256)} %head_ref.1) | copy-start | bytes 3076
  12.4 23.7 %all-to-all-start.2 = ((bf16[32,32,256]{2,1,0:T(8,128)(2,1)}), bf16[32,32,256]{2,1,0:T(8,128)(2,1)S(1)}, u32[]{:S(2)}, u32[]{:S(2)}) async-start(bf16[32,32,256]{2,1,0:T(8,128)(2,1)} %broadcast_in_dim.74), calls=%async_computation.2 | async-start | bytes 1048576 | tf_op jit(solution)/shard_map/all_to_all | solution.py:539
  36.2 0.8 copy-start.3
  51.8 21.7 %all-to-all-start.3 = ((bf16[32,24,256]{2,1,0:T(8,128)(2,1)}), bf16[32,24,256]{2,1,0:T(8,128)(2,1)S(1)}, u32[]{:S(2)}, u32[]{:S(2)}) async-start(bf16[32,24,256]{2,1,0:T(8,128)(2,1)} %broadcast_in_dim.78), calls=%async_computation.3 | async-start | bytes 786432 | tf_op jit(solution)/shard_map/all_to_all | solution.py:575
  59.6 13.9 %copy-start.1 = (f32[256,256]{1,0:T(8,128)S(1)}, f32[256,256]{1,0:T(8,128)}, u32[]{:S(2)}) copy-start(f32[256,256]{1,0:T(8,128)} %get-tuple-element.117.factor_hbm) | copy-start | bytes 786436
  73.5 1.3 %copy-start = (bf16[2304,256]{1,0:T(8,128)(2,1)S(1)}, bf16[2304,256]{1,0:T(8,128)(2,1)}, u32[]{:S(2)}) copy-start(bf16[2304,256]{1,0:T(8,128)(2,1)} %shard_map.143.hidden_hbm) | copy-start | bytes 3538948
  77.7 8.1 %all-to-all-start.4 = ((bf16[4,144,128]{2,1,0:T(8,128)(2,1)}), bf16[4,144,128]{2,1,0:T(8,128)(2,1)S(1)}, u32[]{:S(2)}, u32[]{:S(2)}) async-start(bf16[4,144,128]{2,1,0:T(8,128)(2,1)} %get-tuple-element.119), calls=%async_computation.4 | async-start | bytes 294912 | tf_op jit(solution)/shard_map/all_to_all | solution.py:631

commit v14 on v12

--- a/solution.py
+++ b/solution.py
@@ -17,7 +17,7 @@
 TN = (((0,), (0,)), ((), ()))
 VMEM_LIMIT = 56 * 2**20
 STEP = 2
-AHEAD = 6
+AHEAD = 5
 SCORE_LIMIT = 24 * 2**20
 
 

time: 102 us -> 102 us (level)
    pallas_call x1, Pallas kernels: 18.3 us -> 15.9 us  [near_call(): pl.pallas_call(functools.partial(near_kernel, ahead), out_shape=(jax.Shap...]
    pallas_call x2, Pallas kernels: 27.2 us -> 29.4 us  [far_call(): pl.pallas_call(functools.partial(far_kernel, half_rel, last, ahead, devic...]
  transfers between devices with their start and end apart: 4 -> 4, of which waited for: 2 -> 2; matrix products, arithmetic and copies ran while one was open for 2% -> 2% of each run, Pallas kernels for 32% -> 33%
where the time goes in v14:
time: 102 us; the launch traced here: 101 us
  Pallas kernels  52.5 us (51%)
  starting transfers between devices  18.8 us (18%)
  blocking collectives  15.6 us (15%)
  waiting for transfers between devices  6.61 us (6%)
  local copies, waits for them, and re-layouts  6.17 us (6%)
    pallas_call x2, Pallas kernels, far_call(): pl.pallas_call(functools.partial(far_kernel, half_rel, last, ahead, devic...  29.4 us
    pallas_call x1, Pallas kernels, near_call(): pl.pallas_call(functools.partial(near_kernel, ahead), out_shape=(jax.Shap...  15.9 us
    all_to_all x1, blocking collectives, body(): lax.all_to_all(payload, 'ent', 0, 0)  15.6 us
    all_to_all x1, starting transfers between devices, send_round(): return lax.all_to_all(spread, BOTH, 0, 0).reshape(devices * cap, columns)  5.83 us
    all_to_all x1, starting transfers between devices, body(): table = lax.all_to_all(spread, BOTH, 0, 0).reshape(groups * slots, columns)  5.42 us
    all_to_all x1, waiting for transfers between devices, body(): lax.all_to_all(payload, 'rep', 0, 0)  4.77 us
    all_to_all x1, starting transfers between devices, body(): pieces = lax.all_to_all(offered, 'rep', 0, 0, tiled=True)  4.22 us
    unnamed x13, local copies, waits for them, and re-layouts  3.64 us
  transfers between devices with their start and end apart: 4, of which 2 were waited for; matrix products, arithmetic and copies ran while one was open for 2% of the time, Pallas kernels for 33%

profile of v14, /device:TPU:0, one launch (start us, length us, event | category | flops | bytes accessed | tf_op | source)
XLA Modules:
  0.0 101.2 jit_solution(17916534013653536582)
XLA Ops:
  0.6 0.0 copy-start.4
  0.6 0.0 copy-start.2
  0.7 2.4 %shard_map.140 = bf16[128,256]{1,0:T(8,128)(2,1)} custom-call(s32[1]{0:T(128)} %bitcast.8.base_ref, s32[1,128]{1,0:T(1,128)} %index_ref.1, bf16[2304,256]{1,0:T(8,128)(2,1)} %emb_ref.5), custom_call_target="tpu_custom_call" | custom-call | tf_op jit(solution)/shard_map/pallas_call | solution.py:513
  3.1 0.0 copy-done.4
  3.1 0.1 copy.17
  3.2 4.2 %all-to-all-start.1 = ((bf16[4,32,256]{2,1,0:T(8,128)(2,1)}), bf16[4,32,256]{2,1,0:T(8,128)(2,1)S(1)}, u32[]{:S(2)}, u32[]{:S(2)}) async-start(bf16[4,32,256]{2,1,0:T(8,128)(2,1)} %bitcast.41), calls=%async_computation.1 | async-start | bytes 131072 | tf_op jit(solution)/shard_map/all_to_all | solution.py:524
  7.4 0.7 pad_bitcast_fusion.relation_ref.rest_2_.rest_1_
  8.2 0.0 copy-done.2
  8.2 0.0 copy-start.5
  8.2 1.5 %copy.16 = bf16[2304,256]{0,1:T(8,128)(2,1)} copy(bf16[2304,256]{1,0:T(8,128)(2,1)S(1)} %copy-done.2) | data formatting | bytes 2359296 | tf_op args[0]
  9.7 0.0 copy-done.5
  9.7 1.8 %all-to-all-done.1 = bf16[4,32,256]{2,1,0:T(8,128)(2,1)S(1)} async-done(((bf16[4,32,256]{2,1,0:T(8,128)(2,1)}), bf16[4,32,256]{2,1,0:T(8,128)(2,1)S(1)}, u32[]{:S(2)}, u32[]{:S(2)}) %all-to-all-start.1) | async-done | bytes 65568 | tf_op jit(solution)/shard_map/all_to_all | solution.py:524
  11.6 0.8 broadcast_in_dim.74
  12.4 5.4 %all-to-all-start.2 = ((bf16[32,32,256]{2,1,0:T(8,128)(2,1)}), bf16[32,32,256]{2,1,0:T(8,128)(2,1)S(1)}, u32[]{:S(2)}, u32[]{:S(2)}) async-start(bf16[32,32,256]{2,1,0:T(8,128)(2,1)} %broadcast_in_dim.74), calls=%async_computation.2 | async-start | bytes 1048576 | tf_op jit(solution)/shard_map/all_to_all | solution.py:530
  17.8 15.9 %shard_map.141 = (bf16[9,2,256,768]{3,2,1,0:T(8,128)(2,1)}, s32[20]{0:T(128)}) custom-call(s32[1]{0:T(128)} %bitcast.7.base_ref, s32[256]{0:T(256)S(1)} %copy-done.5, s32[18,768]{1,0:T(8,128)} %src_ref.5, s32[18,768]{1,0:T(8,128)} %rel_ref.5, bf16[256,2304]{1,0:T(8,128)(2,1)} %bitcast.37, bf16[256,512]{1,0:T(8,128)(2,1)} %pad_bitcast_fusion.relation_ref.rest_2_.rest_1_), custom_call_target="tpu_custom_call" | custom-call | flops 11072962560 | bytes 3932160 | tf_op jit(solution)/shard_map/pallas_call | solution.py:326
  33.7 0.0 all-to-all-done.2
  33.7 0.0 copy-start.3
  33.8 0.8 copy-done.3
  34.6 11.9 %shard_map.142 = (bf16[2304,256]{1,0:T(8,128)(2,1)}, bf16[264,256]{1,0:T(8,128)(2,1)S(1)}, f32[256,256]{1,0:T(8,128)}, s32[1,256]{1,0:T(1,128)S(1)}, s32[1]{0:T(128)}) custom-call(s32[1]{0:T(128)} %bitcast.7.base_ref, s32[20]{0:T(128)} %get-tuple-element.110.order_ref, s32[18,768]{1,0:T(8,128)} %src_ref.5, s32[18,768]{1,0:T(8,128)} %dst_ref.3, ...), custom_call_target="tpu_custom_call" | custom-call | flops 3623878656 | bytes 3538944 | tf_op jit(solution)/shard_map/pallas_call | solution.py:348
  46.6 0.7 while.12
  47.3 0.8 broadcast_in_dim.78
  48.0 5.8 %all-to-all-start.3 = ((bf16[32,24,256]{2,1,0:T(8,128)(2,1)}), bf16[32,24,256]{2,1,0:T(8,128)(2,1)S(1)}, u32[]{:S(2)}, u32[]{:S(2)}) async-start(bf16[32,24,256]{2,1,0:T(8,128)(2,1)} %broadcast_in_dim.78), calls=%async_computation.3 | async-start | bytes 786432 | tf_op jit(solution)/shard_map/all_to_all | solution.py:566
  53.9 0.0 copy-start.1
  53.9 17.5 %shard_map.143.hidden_hbm = bf16[2304,256]{1,0:T(8,128)(2,1)} custom-call(s32[1]{0:T(128)} %bitcast.7.base_ref, s32[20]{0:T(128)} %get-tuple-element.110.order_ref, s32[18,768]{1,0:T(8,128)} %src_ref.5, s32[18,768]{1,0:T(8,128)} %dst_ref.3, s32[18,768]{1,0:T(8,128)} %rel_ref.5, bf16[2304,256]{1,0:T(8,128)(2,1)} %emb_ref.5, ...), custom_call_target="tpu_custom_call", output_to_operand_aliasing={{}: (13, {})} | custom-call | flops 3623878656 | bytes 3538944 | tf_op jit(solution)/shard_map/pallas_call | solution.py:348
  71.3 0.0 all-to-all-done.3
  71.4 0.0 copy-done.1
  71.4 0.0 copy-start
  71.4 1.3 %copy-done = bf16[2304,256]{1,0:T(8,128)(2,1)S(1)} copy-done((bf16[2304,256]{1,0:T(8,128)(2,1)S(1)}, bf16[2304,256]{1,0:T(8,128)(2,1)}, u32[]{:S(2)}) %copy-start) | copy-done | bytes 1179672
  72.6 3.0 %shard_map.144 = (f32[256,2304]{1,0:T(8,128)S(1)}, bf16[4,144,128]{2,1,0:T(8,128)(2,1)}) custom-call(bf16[768,256]{1,0:T(8,128)(2,1)S(1)} %bitcast.35, bf16[256,256]{1,0:T(8,128)(2,1)S(1)} %get-tuple-element.116.more_ref, s32[1,256]{1,0:T(1,128)S(1)} %get-tuple-element.242, s32[1,256]{1,0:T(1,128)S(1)} %bitcast.49, f32[256,256]{1,0:T(8,128)S(1)} %copy-done.1, ...), custom_call_target="tpu_custom_call" | custom-call | tf_op jit(solution)/shard_map/pallas_call | solution.py:601
  75.6 3.3 %all-to-all-start.4 = ((bf16[4,144,128]{2,1,0:T(8,128)(2,1)}), bf16[4,144,128]{2,1,0:T(8,128)(2,1)S(1)}, u32[]{:S(2)}, u32[]{:S(2)}) async-start(bf16[4,144,128]{2,1,0:T(8,128)(2,1)} %get-tuple-element.119), calls=%async_computation.4 | async-start | bytes 294912 | tf_op jit(solution)/shard_map/all_to_all | solution.py:622
  79.0 4.8 %all-to-all-done.4.received_ref = bf16[4,144,128]{2,1,0:T(8,128)(2,1)S(1)} async-done(((bf16[4,144,128]{2,1,0:T(8,128)(2,1)}), bf16[4,144,128]{2,1,0:T(8,128)(2,1)S(1)}, u32[]{:S(2)}, u32[]{:S(2)}) %all-to-all-start.4) | async-done | bytes 147488 | tf_op jit(solution)/shard_map/all_to_all | solution.py:622
  83.7 0.1 shard_map.145
  83.9 15.6 %all_to_all.38.received_ref = bf16[8,144,128]{2,1,0:T(8,128)(2,1)S(1)} all-to-all(bf16[8,144,128]{2,1,0:T(8,128)(2,1)S(1)} %shard_map.145), channel_id=1, replica_groups=mesh['ent'=8,'rep'=4] {'ent'}, dimensions={0} | all-to-all | bytes 589824 | tf_op jit(solution)/shard_map/all_to_all | solution.py:632
  99.5 1.7 %shard_map.146 = (f32[256,2304]{1,0:T(8,128)}, f32[64,256]{1,0:T(8,128)}) custom-call(s32[1]{0:T(128)} %bitcast.6.first_ref, bf16[8,144,128]{2,1,0:T(8,128)(2,1)S(1)} %all_to_all.38.received_ref, f32[256,2304]{1,0:T(8,128)S(1)} %get-tuple-element.120.scores_ref), custom_call_target="tpu_custom_call" | custom-call | tf_op jit(solution)/shard_map/pallas_call | solution.py:623
  (4 shorter events, 0.0 us)
Async XLA Ops:
  0.6 2.4 %copy-start.4 = (bf16[474,256]{1,0:T(8,128)(2,1)S(1)}, bf16[474,256]{1,0:T(8,128)(2,1)}, u32[]{:S(2)}) copy-start(bf16[474,256]{1,0:T(8,128)(2,1)} %param.16) | copy-start | bytes 728068
  0.6 7.5 %copy-start.2 = (bf16[2304,256]{1,0:T(8,128)(2,1)S(1)}, bf16[2304,256]{1,0:T(8,128)(2,1)}, u32[]{:S(2)}) copy-start(bf16[2304,256]{1,0:T(8,128)(2,1)} %emb_ref.5) | copy-start | bytes 3538948
  3.2 8.3 %all-to-all-start.1 = ((bf16[4,32,256]{2,1,0:T(8,128)(2,1)}), bf16[4,32,256]{2,1,0:T(8,128)(2,1)S(1)}, u32[]{:S(2)}, u32[]{:S(2)}) async-start(bf16[4,32,256]{2,1,0:T(8,128)(2,1)} %bitcast.41), calls=%async_computation.1 | async-start | bytes 131072 | tf_op jit(solution)/shard_map/all_to_all | solution.py:524
  8.2 1.5 %copy-start.5 = (s32[256]{0:T(256)S(1)}, s32[256]{0:T(256)}, u32[]{:S(2)}) copy-start(s32[256]{0:T(256)} %head_ref.1) | copy-start | bytes 3076
  12.4 21.3 %all-to-all-start.2 = ((bf16[32,32,256]{2,1,0:T(8,128)(2,1)}), bf16[32,32,256]{2,1,0:T(8,128)(2,1)S(1)}, u32[]{:S(2)}, u32[]{:S(2)}) async-start(bf16[32,32,256]{2,1,0:T(8,128)(2,1)} %broadcast_in_dim.74), calls=%async_computation.2 | async-start | bytes 1048576 | tf_op jit(solution)/shard_map/all_to_all | solution.py:530
  33.7 0.8 copy-start.3
  48.0 23.3 %all-to-all-start.3 = ((bf16[32,24,256]{2,1,0:T(8,128)(2,1)}), bf16[32,24,256]{2,1,0:T(8,128)(2,1)S(1)}, u32[]{:S(2)}, u32[]{:S(2)}) async-start(bf16[32,24,256]{2,1,0:T(8,128)(2,1)} %broadcast_in_dim.78), calls=%async_computation.3 | async-start | bytes 786432 | tf_op jit(solution)/shard_map/all_to_all | solution.py:566
  53.9 17.5 %copy-start.1 = (f32[256,256]{1,0:T(8,128)S(1)}, f32[256,256]{1,0:T(8,128)}, u32[]{:S(2)}) copy-start(f32[256,256]{1,0:T(8,128)} %get-tuple-element.117.factor_hbm) | copy-start | bytes 786436
  71.4 1.3 %copy-start = (bf16[2304,256]{1,0:T(8,128)(2,1)S(1)}, bf16[2304,256]{1,0:T(8,128)(2,1)}, u32[]{:S(2)}) copy-start(bf16[2304,256]{1,0:T(8,128)(2,1)} %shard_map.143.hidden_hbm) | copy-start | bytes 3538948
  75.6 8.1 %all-to-all-start.4 = ((bf16[4,144,128]{2,1,0:T(8,128)(2,1)}), bf16[4,144,128]{2,1,0:T(8,128)(2,1)S(1)}, u32[]{:S(2)}, u32[]{:S(2)}) async-start(bf16[4,144,128]{2,1,0:T(8,128)(2,1)} %get-tuple-element.119), calls=%async_computation.4 | async-start | bytes 294912 | tf_op jit(solution)/shard_map/all_to_all | solution.py:622
